TPU v7x, 32 devices: a whole 2x2x4 slice. The times are simulated.
32 devices in a mesh: row: 4 (over y, core), col: 8 (over z, x).
Axes of the slice: x: 2, y: 2, z: 4, core: 2. Of those that a mesh axis runs over, the one named last changes fastest.
Arguments:
- points: float32 [3, 65536], P(None, ('row', 'col')), as said below
- values: float32 [16, 65536], P(None, ('row', 'col'))
- tile_lists: int32 [3, 1536], P(None, ('row', 'col')), may hold values from 0 to 63, as said below
Outputs:
- solution: float32 [16, 65536], P(None, ('row', 'col'))
- residual: float32 [16, 65536], P(None, ('row', 'col'))
Inputs may be any that keep to these rules, and one draw needn't show every extreme that they name: `tile_lists`: on every device the live slots come first and the rest hold 0, 0, 0; a device holds at most 48 live slots and some device holds exactly that many; no unordered pair of blocks is listed twice, in either order. Block pairs whose points can come within the support radius are listed. Coordinates of point blocks that lie in cells of a square lattice of unit cells, 256 points to a block.
All inputs are finite; a program needn't handle non-finite values.
Results may differ from a plain program's by a relative error of at most 0.0003.
Values sent between devices are 32-bit elements; how exact they have to be, the bound alone decides.
No kernel may reach another device: no remote copies, remote signals or barrier semaphores. Data moves between devices by JAX's collectives and lax.ppermute only.
A program may use at most 64 MiB of HBM per device.

v0:
```python
import functools
import itertools

import jax
import jax.numpy as jnp
from jax import lax
from jax.experimental import pallas as pl
from jax.experimental.pallas import tpu as pltpu
from jax.sharding import PartitionSpec as P

BLK = 256
LANES = 128
CHUNK = 256
GROUP = 8
UNROLL = 4

support = 0.5
ridge_shift = 1.0

SHIFT, VV, VW, QQ, QW, WW, QS, CROSS, WX = range(9)
HALF = 64


def pack_kernel(per_device, place_ref, values_ref, points_ref, lists_ref, blocks_ref, out_ref):
    row_base = place_ref[0]
    col_id = place_ref[1]
    col_count = place_ref[2]
    x_step = place_ref[3]
    for b in range(per_device):
        for half in range(2):
            blocks_ref[2 * b + half] = values_ref[8 * half : 8 * half + 8, b * BLK : (b + 1) * BLK]
    for axis in range(3):
        for b in range(per_device):
            out_ref[axis, b : b + 1, :] = points_ref[axis : axis + 1, b * BLK : (b + 1) * BLK] * (1.0 / support)
    shift = per_device.bit_length() - 1
    low = per_device - 1

    def code(row, col, b):
        device = row * col_count + (col & 1) * x_step + lax.shift_right_logical(col, 1)
        return device * per_device + b

    row_local = lists_ref[0:1, :]
    col_local = lists_ref[1:2, :]
    live = lists_ref[2:3, :] == 1
    row_code = code(row_base, lax.shift_right_logical(row_local, shift), row_local & low)
    col_code = code(lax.shift_right_logical(col_local, shift), jnp.full_like(col_local, col_id), col_local & low)
    row_code = jnp.where(live, row_code, -1).astype(jnp.float32)
    col_code = jnp.where(live, col_code, -1).astype(jnp.float32)
    tiles = row_local.shape[1]
    out_ref[3] = jnp.full((8, BLK), -1.0, jnp.float32)
    out_ref[3, 0:1, 0:tiles] = row_code
    out_ref[3, 0:1, HALF : HALF + tiles] = col_code
    out_ref[3, 1:2, 0:tiles] = col_code
    out_ref[3, 1:2, HALF : HALF + tiles] = row_code


def split(x):
    high = x.astype(jnp.bfloat16)
    low = (x - high.astype(jnp.float32)).astype(jnp.bfloat16)
    return high, low


def evaluate(across, down, high_ref, low_ref):
    down = jnp.transpose(jnp.concatenate(down + [jnp.zeros((5, BLK), jnp.float32)], axis=0))
    for s in range(0, BLK, 32):
        square = None
        for axis in range(3):
            gap = down[s : s + 32, axis : axis + 1] - across[axis]
            square = gap * gap if square is None else square + gap * gap
        scaled = square * lax.rsqrt(jnp.maximum(square, 1e-30))
        remain = jnp.maximum(1.0 - scaled, 0.0)
        remain = remain * remain
        high, low = split(remain * remain * (4.0 * scaled + 1.0))
        high_ref[s : s + 32, :] = high
        low_ref[s : s + 32, :] = low


def point_rows(cloud, b, per_device):
    device = lax.shift_right_logical(b, per_device.bit_length() - 1)
    line = b & (per_device - 1)
    return [cloud[device, axis, pl.ds(line, 1), :] for axis in range(3)]


def entry(lists, k):
    chunk = lax.shift_right_logical(k, CHUNK.bit_length() - 1)
    lane = k & (CHUNK - 1)
    return lists[chunk, 0, lane], lists[chunk, 1, lane]


def gather(refs, target, sems):
    run = target.shape[0] // len(refs)
    return [pltpu.make_async_copy(ref, target.at[pl.ds(p * run, run)], sems.at[p]) for p, ref in enumerate(refs)]


def tiles_kernel(pieces, per_device, cap, me_ref, *refs):
    list_ref, tile_ref = refs[pieces : pieces + 2]
    cloud, stage, plan, lists, ring, sems, list_sem, tile_sem = refs[pieces + 2 :]
    devices = cloud.shape[0]
    blocks = devices * per_device
    copies = gather(refs[:pieces], cloud, sems)
    for copy in copies:
        copy.start()
    for copy in copies:
        copy.wait()

    mine = me_ref[0] * per_device
    ids = lax.broadcasted_iota(jnp.int32, (blocks, 2 * LANES), 0)

    def one_hot(pair, line):
        codes = []
        for k in range(2):
            row = cloud[2 * pair + k, 3, line : line + 1, 0:LANES].astype(jnp.int32)
            codes.append(jnp.where(row >= 0, row ^ mine, -1))
        codes = jnp.concatenate(codes, axis=1)
        return jnp.where(ids == codes, 1.0, 0.0).astype(jnp.bfloat16)

    stage[...] = jnp.zeros_like(stage)

    def add_pairs(pair, carry):
        stage[...] += lax.dot_general(
            one_hot(pair, 0), one_hot(pair, 1), (((1,), (1,)), ((), ())), preferred_element_type=jnp.float32
        )
        return carry

    lax.fori_loop(0, devices // 2, add_pairs, 0)

    lane = lax.broadcasted_iota(jnp.int32, (blocks, LANES), 1)
    boxes = jnp.zeros((blocks, LANES), jnp.float32)
    for axis in range(3):
        coordinates = cloud[:, axis].reshape(blocks, BLK)
        boxes = jnp.where(lane == axis, jnp.min(coordinates, axis=1, keepdims=True), boxes)
        boxes = jnp.where(lane == 3 + axis, jnp.max(coordinates, axis=1, keepdims=True), boxes)
    flat = jnp.transpose(boxes)
    apart = None
    for axis in range(3):
        gap = jnp.maximum(
            boxes[:, axis : axis + 1] - flat[3 + axis : 4 + axis, :],
            flat[axis : axis + 1, :] - boxes[:, 3 + axis : 4 + axis],
        )
        gap = jnp.maximum(gap, 0.0)
        apart = gap * gap if apart is None else apart + gap * gap
    stage[...] = jnp.where(apart < 1.0001, stage[...], 0.0)

    listed = stage[...] > 0.0
    rows = lax.broadcasted_iota(jnp.int32, (blocks, blocks), 0)
    cols = lax.broadcasted_iota(jnp.int32, (blocks, blocks), 1)
    near_row = jnp.max(stage[0:per_device, :], axis=0, keepdims=True) > 0.0
    near_row = near_row | (lax.broadcasted_iota(jnp.int32, (1, blocks), 1) < per_device)
    near_col = jnp.max(stage[:, 0:per_device], axis=1, keepdims=True) > 0.0
    near_col = near_col | (lax.broadcasted_iota(jnp.int32, (blocks, 1), 0) < per_device)
    near = jnp.where(near_row, 1.0, 0.0) + jnp.where(near_col, 1.0, 0.0)
    used = jnp.where(listed & (rows >= cols) & (near > 0.0), 1.0, 0.0)
    exact = dict(precision=lax.Precision.HIGHEST, preferred_element_type=jnp.float32)
    rank = jnp.dot(jnp.where(rows >= cols, 1.0, 0.0), used, **exact)
    count = jnp.broadcast_to(rank[blocks - 1 : blocks, :], (8, blocks))
    start = jnp.dot(count, jnp.where(rows < cols, 1.0, 0.0), **exact)
    n = jnp.sum(count[0:1, :]).astype(jnp.int32)
    own = lax.broadcasted_iota(jnp.int32, (1, blocks), 1) < per_device
    n_own = jnp.sum(jnp.where(own, count[0:1, :], 0.0)).astype(jnp.int32)
    start_col = jnp.transpose(start)[:, 0:1]
    stop_col = start_col + jnp.transpose(count)[:, 0:1]
    stage[...] = rank * used
    index_col = lax.broadcasted_iota(jnp.int32, (blocks, CHUNK), 0).astype(jnp.float32)

    def write_list(chunk, carry):
        place = lax.broadcasted_iota(jnp.int32, (1, CHUNK), 1).astype(jnp.float32) + (chunk * CHUNK).astype(jnp.float32)
        pick = jnp.where((start_col <= place) & (place < stop_col), 1.0, 0.0)
        low_index = jnp.sum(pick * index_col, axis=0, keepdims=True)
        begin = jnp.sum(pick * start_col, axis=0, keepdims=True)
        ranks = jnp.dot(stage[...], pick, **exact)
        match = jnp.where(ranks == place - begin + 1.0, 1.0, 0.0)
        high_index = jnp.sum(match * index_col, axis=0, keepdims=True)
        both = jnp.concatenate([low_index, high_index], axis=0).astype(jnp.int32)
        sizes = jnp.concatenate(
            [jnp.full((1, CHUNK), n, jnp.int32), jnp.full((1, CHUNK), n_own, jnp.int32)], axis=0
        )
        plan[...] = jnp.concatenate([both, sizes, jnp.zeros((4, CHUNK), jnp.int32)], axis=0)
        list_ref[chunk] = plan[...]
        copy = pltpu.make_async_copy(plan, lists.at[chunk], list_sem)
        copy.start()
        copy.wait()
        return carry

    lax.fori_loop(0, jnp.maximum((n + CHUNK - 1) // CHUNK, 1), write_list, 0)

    def send(step):
        slot = step & 1
        return pltpu.make_async_copy(ring.at[slot], tile_ref.at[pl.ds(2 * step, 2)], tile_sem.at[slot])

    def write_tiles(step, carry):
        slot = step & 1

        @pl.when(step >= 2)
        def _():
            send(step - 2).wait()

        for part in range(2):
            i, j = entry(lists, 2 * step + part)
            evaluate(
                point_rows(cloud, i, per_device),
                point_rows(cloud, j, per_device),
                ring.at[slot, part, 0],
                ring.at[slot, part, 1],
            )
        send(step).start()
        return carry

    steps = (jnp.minimum(n, cap) + 1) // 2
    lax.fori_loop(0, steps, write_tiles, 0)
    for back in (2, 1):

        @pl.when(steps >= back)
        def _():
            send(steps - back).wait()


def apply_kernel(pieces, point_pieces, per_device, cap, lists, tile_ref, *refs):
    value_refs = refs[:pieces]
    point_refs = refs[pieces : pieces + point_pieces]
    w_ref, x_ref, moment_ref = refs[pieces + point_pieces : pieces + point_pieces + 3]
    field, total, second, cache, cloud, sems, total_sems, point_sems, tile_sems = refs[pieces + point_pieces + 3 :]
    devices = field.shape[0]
    blocks = devices * per_device
    block_shift = per_device.bit_length() - 1
    low_mask = per_device - 1
    n = lists[0, 2, 0]
    n_own = lists[0, 3, 0]
    held = jnp.minimum(n, cap)
    groups = (held + GROUP - 1) // GROUP

    def fetch(group):
        span = pl.ds(group * GROUP, GROUP)
        return pltpu.make_async_copy(tile_ref.at[span], cache.at[span], tile_sems.at[group])

    fills = gather(value_refs, field, sems) + gather(value_refs, total.at[pl.ds(0, devices)], total_sems)
    for copy in fills:
        copy.start()

    def start_fetch(group, carry):
        fetch(group).start()
        return carry

    lax.fori_loop(0, groups, start_fetch, 0)
    for copy in fills:
        copy.wait()

    def at(b):
        return lax.shift_right_logical(b, block_shift), pl.ds(2 * (b & low_mask), 2)

    def product(vector, slot, contract):
        high, low = split(vector)
        both = jnp.concatenate([high, low], axis=0)
        dims = (((1,), (contract,)), ((), ()))
        first = lax.dot_general(both, cache[slot, 0], dims, preferred_element_type=jnp.float32)
        later = lax.dot_general(high, cache[slot, 1], dims, preferred_element_type=jnp.float32)
        return (first[0:16] + first[16:32] + later).reshape(2, 8, BLK)

    def load(ref, b):
        device, span = at(b)
        return ref[device, span].reshape(16, BLK)

    def add(ref, b, value):
        device, span = at(b)
        ref[device, span] += value

    def evaluate_late(k):
        i, j = entry(lists, k)
        evaluate(
            point_rows(cloud, i, per_device), point_rows(cloud, j, per_device), cache.at[cap, 0], cache.at[cap, 1]
        )
        return i, j

    def first_group(group, carry):
        fetch(group).wait()
        for quad in range(0, GROUP, UNROLL):
            pending = []
            for u in range(UNROLL):
                k = group * GROUP + quad + u
                i, j = entry(lists, k)
                live = k < held
                pending.append((jnp.where(live, i, blocks), product(load(field, j), k, 0)))
                pending.append((jnp.where(live & (i != j), j, blocks), product(load(field, i), k, 1)))
            for b, value in pending:
                add(total, b, value)
        return carry

    lax.fori_loop(0, groups, first_group, 0)

    @pl.when(n > cap)
    def _():
        copies = gather(point_refs, cloud, point_sems)
        for copy in copies:
            copy.start()
        for copy in copies:
            copy.wait()

        def first_late(k, carry):
            i, j = evaluate_late(k)
            add(total, i, product(load(field, j), cap, 0))

            @pl.when(i != j)
            def _():
                add(total, j, product(load(field, i), cap, 1))

            return carry

        lax.fori_loop(cap, n, first_late, 0)

    second[0] = total[0]
    held_own = jnp.minimum(n_own, cap)

    def second_group(group, carry):
        pending = []
        for u in range(UNROLL):
            k = group * UNROLL + u
            i, j = entry(lists, k)
            live = k < held_own
            pending.append((jnp.where(live, i, per_device), product(load(total, j), k, 0)))
        for b, value in pending:
            add(second, b, value)
        for u in range(UNROLL):
            k = group * UNROLL + u
            i, j = entry(lists, k)

            @pl.when((k < held_own) & (i != j) & (j < per_device))
            def _():
                add(second, j, product(load(total, i), k, 1))

        return carry

    lax.fori_loop(0, (held_own + UNROLL - 1) // UNROLL, second_group, 0)

    def second_late(k, carry):
        i, j = evaluate_late(k)
        add(second, i, product(load(total, j), cap, 0))

        @pl.when((i != j) & (j < per_device))
        def _():
            add(second, j, product(load(total, i), cap, 1))

        return carry

    lax.fori_loop(cap, n_own, second_late, 0)

    v = field[0].reshape(per_device, 16, BLK)
    w = total[0].reshape(per_device, 16, BLK)
    x = second[0].reshape(per_device, 16, BLK)
    w_ref[...] = w
    x_ref[...] = x

    def over(values):
        return jnp.sum(jnp.sum(values, axis=0), axis=1, keepdims=True)

    vv = over(v * v)
    vw = over(v * w)
    shift = jnp.where(vw != 0.0, vv / jnp.where(vw != 0.0, vw, 1.0), 0.0)
    q = v - shift[None] * w
    s = w - shift[None] * x
    sums = [shift, vv, vw, over(q * q), over(q * w), over(w * w), over(q * s), over(w * s + q * x), over(w * x)]
    lane = lax.broadcasted_iota(jnp.int32, (8, LANES), 1)
    sent = jnp.zeros((8, LANES), jnp.float32)
    for m, value in enumerate(sums):
        for half in range(2):
            sent = jnp.where(lane == half * HALF + m, value[8 * half : 8 * half + 8], sent)
    for device in range(devices):
        moment_ref[device] = sent


def finish_kernel(per_device, moment_ref, values_ref, w_ref, x_ref, solution_ref, residual_ref):
    moments = moment_ref[...]

    for half in range(2):

        def take(m):
            return moments[:, :, half * HALF + m : half * HALF + m + 1]

        def whole(values):
            return jnp.sum(values, axis=0)

        rr = whole(take(VV))
        vw = whole(take(VW))
        alpha = rr / vw
        delta = alpha[None] - take(SHIFT)
        fresh = whole(take(QQ) - 2.0 * delta * take(QW) + delta * delta * take(WW))
        mixed = whole(take(QW) - delta * take(WW))
        curve = whole(take(QS) - delta * take(CROSS) + delta * delta * take(WX))
        beta = fresh / rr
        curve = curve + 2.0 * beta * mixed + beta * beta * vw
        again = fresh / curve
        for b in range(per_device):
            at = (slice(8 * half, 8 * half + 8), slice(b * BLK, (b + 1) * BLK))
            v = values_ref[at]
            w = w_ref[b, 8 * half : 8 * half + 8, :]
            x = x_ref[b, 8 * half : 8 * half + 8, :]
            r = v - alpha * w
            d = r + beta * v
            solution_ref[at] = alpha * v + again * d
            residual_ref[at] = r - again * (w - alpha * x + beta * w)


def local(points, values, tile_lists):
    fields, owned_points = values.shape
    per_device = owned_points // BLK
    rows = lax.axis_size("row")
    cols = lax.axis_size("col")
    devices = rows * cols
    row_id = lax.axis_index("row")
    col_id = lax.axis_index("col")
    depth = cols // 2
    vmem = pl.BlockSpec(memory_space=pltpu.VMEM)
    smem = pl.BlockSpec(memory_space=pltpu.SMEM)
    anywhere = pl.BlockSpec(memory_space=pl.ANY)
    height = 2 * per_device
    blocks = devices * per_device

    place = jnp.stack([row_id, col_id, jnp.int32(cols), jnp.int32(depth)]).astype(jnp.int32)
    own_values, own_points = pl.pallas_call(
        functools.partial(pack_kernel, per_device),
        out_shape=(
            jax.ShapeDtypeStruct((height, 8, BLK), jnp.float32),
            jax.ShapeDtypeStruct((4, per_device, BLK), jnp.float32),
        ),
        in_specs=[smem, vmem, vmem, vmem],
        out_specs=(vmem, vmem),
        name="pack",
    )(place, values, points, tile_lists)

    def swap(array, row_mask, col_mask):
        if row_mask == 0:
            return lax.ppermute(array, "col", [(i, i ^ col_mask) for i in range(cols)])
        if col_mask == 0:
            return lax.ppermute(array, "row", [(i, i ^ row_mask) for i in range(rows)])
        pairs = [
            (r * cols + c, (r ^ row_mask) * cols + (c ^ col_mask)) for r in range(rows) for c in range(cols)
        ]
        return lax.ppermute(array, ("row", "col"), pairs)

    def along(array):
        return jnp.stack([array] + [swap(array, 0, 2 * z) for z in range(1, depth)])

    def across(line):
        return {
            (row_mask, x): swap(line, row_mask, x) if (row_mask, x) != (0, 0) else line
            for row_mask, x in itertools.product(range(0, rows, 2), range(2))
        }

    def pairs(plane):
        plane = dict(plane)
        for (row_mask, x), part in list(plane.items()):
            plane[row_mask + 1, x] = swap(part, 1, 0)
        return [plane[row_mask, x] for row_mask in range(rows) for x in range(2)]

    point_parts = pairs(across(along(own_points)))
    value_line = along(own_values)
    value_line, point_parts = lax.optimization_barrier((value_line, point_parts))
    value_plane = across(value_line)

    me = row_id * cols + (col_id & 1) * depth + lax.shift_right_logical(col_id, 1)
    chunks = (devices * tile_lists.shape[1] + CHUNK - 1) // CHUNK
    used = 2 * blocks * fields * BLK * 4
    cap = max(GROUP, min(152, (54 * 2**20 - used) // (BLK * BLK * 4) // GROUP * GROUP))
    lists, tiles = pl.pallas_call(
        functools.partial(tiles_kernel, len(point_parts), per_device, cap),
        out_shape=(
            jax.ShapeDtypeStruct((chunks, 8, CHUNK), jnp.int32),
            jax.ShapeDtypeStruct((cap, 2, BLK, BLK), jnp.bfloat16),
        ),
        in_specs=[smem] + [anywhere] * len(point_parts),
        out_specs=(vmem, anywhere),
        scratch_shapes=[
            pltpu.VMEM((devices, 4, per_device, BLK), jnp.float32),
            pltpu.VMEM((blocks, blocks), jnp.float32),
            pltpu.VMEM((8, CHUNK), jnp.int32),
            pltpu.SMEM((chunks, 8, CHUNK), jnp.int32),
            pltpu.VMEM((2, 2, 2, BLK, BLK), jnp.bfloat16),
            pltpu.SemaphoreType.DMA((len(point_parts),)),
            pltpu.SemaphoreType.DMA,
            pltpu.SemaphoreType.DMA((2,)),
        ],
        compiler_params=pltpu.CompilerParams(vmem_limit_bytes=40 * 2**20),
        cost_estimate=pl.CostEstimate(flops=10**9, bytes_accessed=30 * 2**20, transcendentals=10**7),
        name="tiles",
    )(me.reshape(1).astype(jnp.int32), *point_parts)
    value_plane, lists, tiles = lax.optimization_barrier((value_plane, lists, tiles))
    value_parts = pairs(value_plane)
    block_shape = jax.ShapeDtypeStruct((per_device, fields, BLK), jnp.float32)
    w, x, moments = pl.pallas_call(
        functools.partial(apply_kernel, len(value_parts), len(point_parts), per_device, cap),
        out_shape=(block_shape, block_shape, jax.ShapeDtypeStruct((devices, 8, LANES), jnp.float32)),
        in_specs=[smem, anywhere] + [anywhere] * (len(value_parts) + len(point_parts)),
        out_specs=(vmem, vmem, vmem),
        scratch_shapes=[
            pltpu.VMEM((devices, height, 8, BLK), jnp.float32),
            pltpu.VMEM((devices + 1, height, 8, BLK), jnp.float32),
            pltpu.VMEM((2, height, 8, BLK), jnp.float32),
            pltpu.VMEM((cap + 1, 2, BLK, BLK), jnp.bfloat16),
            pltpu.VMEM((devices, 4, per_device, BLK), jnp.float32),
            pltpu.SemaphoreType.DMA((len(value_parts),)),
            pltpu.SemaphoreType.DMA((len(value_parts),)),
            pltpu.SemaphoreType.DMA((len(point_parts),)),
            pltpu.SemaphoreType.DMA((cap // GROUP,)),
        ],
        compiler_params=pltpu.CompilerParams(vmem_limit_bytes=60 * 2**20),
        name="apply",
    )(lists, tiles, *value_parts, *point_parts)
    moments = lax.all_to_all(moments, ("row", "col"), 0, 0, tiled=False)
    return pl.pallas_call(
        functools.partial(finish_kernel, per_device),
        out_shape=(jax.ShapeDtypeStruct(values.shape, jnp.float32),) * 2,
        in_specs=[vmem] * 4,
        out_specs=(vmem, vmem),
        name="finish",
    )(moments, values, w, x)


def solution(mesh):
    placed = (P(None, ("row", "col")), P(None, ("row", "col")), P(None, ("row", "col")))
    return jax.shard_map(
        local,
        mesh=mesh,
        in_specs=placed,
        out_specs=(P(None, ("row", "col")), P(None, ("row", "col"))),
        check_vma=False,
    )
```

profile of v0, /device:TPU:0, one launch (start us, length us, event | category | flops | bytes accessed | tf_op | source)
XLA Modules:
  0.0 117.3 jit_solution(1551558206599110764)
XLA Ops:
  0.6 0.6 pad_add_fusion.place_ref
  1.2 1.6 %pack.1 = (f32[16,8,256]{2,1,0:T(8,128)}, f32[4,8,256]{2,1,0:T(8,128)}) custom-call(s32[4]{0:T(128)} %pad_add_fusion.place_ref, f32[16,2048]{1,0:T(8,128)} %values_ref.3, f32[3,2048]{1,0:T(4,128)} %points_ref.1, s32[3,48]{1,0:T(4,128)} %lists_ref.1), custom_call_target="tpu_custom_call" | custom-call | tf_op jit(solution)/shard_map/pack/pallas_call | solution.py:417
  2.8 5.0 %collective-permute-start.5 = (f32[4,8,256]{2,1,0:T(8,128)}, f32[4,8,256]{2,1,0:T(8,128)S(1)}, u32[]{:S(2)}, u32[]{:S(2)}) collective-permute-start(f32[4,8,256]{2,1,0:T(8,128)} %get-tuple-element.25), channel_id=1, source_target_pairs={{0,6},{1,7},{2,4},{3,5},{4,2},{5,3},{6,0},{7,1},{8,14},{9,15},{10,... | collective-permute-start | bytes 98312 | tf_op jit(solution)/shard_map/ppermute | solution.py:430
  7.9 0.0 collective-permute-start.4
  7.9 0.6 collective-permute-start.3
  8.5 3.8 %collective-permute-start.2 = (f32[16,8,256]{2,1,0:T(8,128)}, f32[16,8,256]{2,1,0:T(8,128)S(1)}, u32[]{:S(2)}, u32[]{:S(2)}) collective-permute-start(f32[16,8,256]{2,1,0:T(8,128)} %get-tuple-element.24), channel_id=1, source_target_pairs={{0,6},{1,7},{2,4},{3,5},{4,2},{5,3},{6,0},{7,1},{8,14},{9,15},{10,... | collective-permute-start | bytes 393224 | tf_op jit(solution)/shard_map/ppermute | solution.py:430
  12.3 6.6 %collective-permute-done.4 = f32[4,8,256]{2,1,0:T(8,128)S(1)} collective-permute-done((f32[4,8,256]{2,1,0:T(8,128)}, f32[4,8,256]{2,1,0:T(8,128)S(1)}, u32[]{:S(2)}, u32[]{:S(2)}) %collective-permute-start.4) | collective-permute-done | bytes 32800 | tf_op jit(solution)/shard_map/ppermute | solution.py:430
  18.9 0.0 collective-permute-done.3
  18.9 0.8 pad_maximum_fusion.1.refs_0_.refs_8_
  19.7 0.0 copy-start
  19.7 2.5 %collective-permute-start.10 = (f32[4,4,8,256]{3,2,1,0:T(8,128)S(1)}, f32[4,4,8,256]{3,2,1,0:T(8,128)S(1)}, u32[]{:S(2)}, u32[]{:S(2)}) collective-permute-start(f32[4,4,8,256]{3,2,1,0:T(8,128)S(1)} %pad_maximum_fusion.1.refs_0_.refs_8_), channel_id=1, source_target_pairs={{0,17},{1,16},{2,19},{3,18},{4,21},{5,20},{6,23},{7,22},{8,25},{9,... | collective-permute-start | bytes 393224 | tf_op jit(solution)/shard_map/ppermute | solution.py:436
  22.2 0.5 collective-permute-start.9
  22.7 0.5 collective-permute-start.6
  23.3 0.0 collective-permute-done.2
  23.3 0.0 collective-permute-start
  23.3 0.3 collective-permute-done.1
  23.5 0.0 collective-permute-start.7
  23.6 2.1 %collective-permute-done.10.refs_5_.refs_13_ = f32[4,4,8,256]{3,2,1,0:T(8,128)S(1)} collective-permute-done((f32[4,4,8,256]{3,2,1,0:T(8,128)S(1)}, f32[4,4,8,256]{3,2,1,0:T(8,128)S(1)}, u32[]{:S(2)}, u32[]{:S(2)}) %collective-permute-start.10) | collective-permute-done | bytes 131104 | tf_op jit(solution)/shard_map/ppermute | solution.py:436
  25.7 0.0 collective-permute-start.12
  25.7 1.5 %collective-permute-done.9.refs_4_.refs_12_ = f32[4,4,8,256]{3,2,1,0:T(8,128)S(1)} collective-permute-done((f32[4,4,8,256]{3,2,1,0:T(8,128)S(1)}, f32[4,4,8,256]{3,2,1,0:T(8,128)S(1)}, u32[]{:S(2)}, u32[]{:S(2)}) %collective-permute-start.9) | collective-permute-done | bytes 131104 | tf_op jit(solution)/shard_map/ppermute | solution.py:432
  27.2 0.0 collective-permute-start.11
  27.2 0.5 collective-permute-done.6.refs_1_.refs_9_
  27.7 0.0 collective-permute-start.8
  27.7 0.7 collective-permute-done
  28.5 0.9 pad_maximum_fusion.refs_0_
  29.4 0.0 copy-start.4
  29.4 0.0 collective-permute-done.12.refs_7_.refs_15_
  29.5 0.0 collective-permute-done.8.refs_3_.refs_11_
  29.5 2.5 %collective-permute-start.15 = (f32[4,16,8,256]{3,2,1,0:T(8,128)S(1)}, f32[4,16,8,256]{3,2,1,0:T(8,128)S(1)}, u32[]{:S(2)}, u32[]{:S(2)}) collective-permute-start(f32[4,16,8,256]{3,2,1,0:T(8,128)S(1)} %pad_maximum_fusion.refs_0_), channel_id=1, source_target_pairs={{0,17},{1,16},{2,19},{3,18},{4,21},{5,20},{6,23},{7,22},{8,25},{9,... | collective-permute-start | bytes 1572872 | tf_op jit(solution)/shard_map/ppermute | solution.py:436
  32.0 0.5 collective-permute-start.14
  32.5 0.5 collective-permute-start.13
  33.1 22.7 %tiles.1 = (s32[6,8,256]{2,1,0:T(8,128)S(1)}, bf16[152,2,256,256]{3,2,1,0:T(8,128)(2,1)}) custom-call(s32[1]{0:T(128)} %bitcast.10.me_ref, f32[4,4,8,256]{3,2,1,0:T(8,128)S(1)} %pad_maximum_fusion.1.refs_0_.refs_8_, f32[4,4,8,256]{3,2,1,0:T(8,128)S(1)} %collective-permute-done.6.refs_1_.refs_9_, ...), custom_call_target="tpu_custom_call" | custom-call | flops 1000000000 | bytes 31457280 | tf_op jit(solution)/shard_map/tiles/pallas_call | solution.py:462
  55.7 0.6 copy-done.8
  56.3 0.0 collective-permute-done.15.refs_5_
  56.3 0.0 collective-permute-done.13.refs_1_
  56.4 3.9 %collective-permute-start.16 = (f32[4,16,8,256]{3,2,1,0:T(8,128)S(1)}, f32[4,16,8,256]{3,2,1,0:T(8,128)S(1)}, u32[]{:S(2)}, u32[]{:S(2)}) collective-permute-start(f32[4,16,8,256]{3,2,1,0:T(8,128)S(1)} %pad_maximum_fusion.refs_0_), channel_id=1, source_target_pairs={{0,8},{8,0},{16,24},{24,16},{1,9},{9,1},{17,25},{25,17},{2,10},{10... | collective-permute-start | bytes 1572872 | tf_op jit(solution)/shard_map/ppermute | solution.py:432
  60.3 0.1 collective-permute-start.17
  60.4 0.4 collective-permute-start.18
  60.8 0.1 collective-permute-start.19
  60.9 0.9 collective-permute-done.16.refs_2_
  61.8 1.5 %collective-permute-done.17.refs_3_ = f32[4,16,8,256]{3,2,1,0:T(8,128)S(1)} collective-permute-done((f32[4,16,8,256]{3,2,1,0:T(8,128)S(1)}, f32[4,16,8,256]{3,2,1,0:T(8,128)S(1)}, u32[]{:S(2)}, u32[]{:S(2)}) %collective-permute-start.17) | collective-permute-done | bytes 524320 | tf_op jit(solution)/shard_map/ppermute | solution.py:432
  63.3 0.7 collective-permute-done.18.refs_6_
  64.1 0.1 copy-done.14
  64.2 0.8 copy-done.15
  65.0 0.0 collective-permute-done.19.refs_7_
  65.1 16.8 %apply.1 = (f32[8,16,256]{2,1,0:T(8,128)}, f32[8,16,256]{2,1,0:T(8,128)}, f32[32,8,128]{2,1,0:T(8,128)}) custom-call(s32[6,8,256]{2,1,0:T(8,128)} %copy-done.8, bf16[152,2,256,256]{3,2,1,0:T(8,128)(2,1)} %get-tuple-element.38.tile_ref, f32[4,16,8,256]{3,2,1,0:T(8,128)} %copy-done.9, f32[4,16,8,256]{3,2,1,0:T(8,128)} %copy-done.12, ...), custom_call_target="tpu_custom_call" | custom-call | tf_op jit(solution)/shard_map/apply/pallas_call | solution.py:487
  81.9 32.7 %all_to_all.5.moment_ref = f32[32,8,128]{2,1,0:T(8,128)} all-to-all(f32[32,8,128]{2,1,0:T(8,128)} %get-tuple-element.43), channel_id=1, replica_groups=mesh['row'=4,'col'=8] {'row','col'}, dimensions={0} | all-to-all | bytes 262144 | tf_op jit(solution)/shard_map/all_to_all | solution.py:506
  114.6 2.7 %finish.1 = (f32[16,2048]{1,0:T(8,128)}, f32[16,2048]{1,0:T(8,128)}) custom-call(f32[32,8,128]{2,1,0:T(8,128)} %all_to_all.5.moment_ref, f32[16,2048]{1,0:T(8,128)} %values_ref.3, f32[8,16,256]{2,1,0:T(8,128)} %get-tuple-element.44.w_ref, f32[8,16,256]{2,1,0:T(8,128)} %get-tuple-element.45.x_ref), custom_call_target="tpu_custom_call" | custom-call | tf_op jit(solution)/shard_map/finish/pallas_call | solution.py:507
  (32 shorter events, 0.1 us)
Async XLA Ops:
  2.8 9.4 %collective-permute-start.5 = (f32[4,8,256]{2,1,0:T(8,128)}, f32[4,8,256]{2,1,0:T(8,128)S(1)}, u32[]{:S(2)}, u32[]{:S(2)}) collective-permute-start(f32[4,8,256]{2,1,0:T(8,128)} %get-tuple-element.25), channel_id=1, source_target_pairs={{0,6},{1,7},{2,4},{3,5},{4,2},{5,3},{6,0},{7,1},{8,14},{9,15},{10,... | collective-permute-start | bytes 98312 | tf_op jit(solution)/shard_map/ppermute | solution.py:430
  7.9 11.0 %collective-permute-start.4 = (f32[4,8,256]{2,1,0:T(8,128)}, f32[4,8,256]{2,1,0:T(8,128)S(1)}, u32[]{:S(2)}, u32[]{:S(2)}) collective-permute-start(f32[4,8,256]{2,1,0:T(8,128)} %get-tuple-element.25), channel_id=1, source_target_pairs={{0,4},{1,5},{2,6},{3,7},{4,0},{5,1},{6,2},{7,3},{8,12},{9,13},{10,... | collective-permute-start | bytes 98312 | tf_op jit(solution)/shard_map/ppermute | solution.py:430
  7.9 11.0 %collective-permute-start.3 = (f32[4,8,256]{2,1,0:T(8,128)}, f32[4,8,256]{2,1,0:T(8,128)S(1)}, u32[]{:S(2)}, u32[]{:S(2)}) collective-permute-start(f32[4,8,256]{2,1,0:T(8,128)} %get-tuple-element.25), channel_id=1, source_target_pairs={{0,2},{1,3},{2,0},{3,1},{4,6},{5,7},{6,4},{7,5},{8,10},{9,11},{10,... | collective-permute-start | bytes 98312 | tf_op jit(solution)/shard_map/ppermute | solution.py:430
  8.5 14.8 %collective-permute-start.2 = (f32[16,8,256]{2,1,0:T(8,128)}, f32[16,8,256]{2,1,0:T(8,128)S(1)}, u32[]{:S(2)}, u32[]{:S(2)}) collective-permute-start(f32[16,8,256]{2,1,0:T(8,128)} %get-tuple-element.24), channel_id=1, source_target_pairs={{0,6},{1,7},{2,4},{3,5},{4,2},{5,3},{6,0},{7,1},{8,14},{9,15},{10,... | collective-permute-start | bytes 393224 | tf_op jit(solution)/shard_map/ppermute | solution.py:430
  12.3 11.3 %collective-permute-start.1 = (f32[16,8,256]{2,1,0:T(8,128)}, f32[16,8,256]{2,1,0:T(8,128)S(1)}, u32[]{:S(2)}, u32[]{:S(2)}) collective-permute-start(f32[16,8,256]{2,1,0:T(8,128)} %get-tuple-element.24), channel_id=1, source_target_pairs={{0,4},{1,5},{2,6},{3,7},{4,0},{5,1},{6,2},{7,3},{8,12},{9,13},{10,... | collective-permute-start | bytes 393224 | tf_op jit(solution)/shard_map/ppermute | solution.py:430
  19.7 45.3 %copy-start = (f32[4,4,8,256]{3,2,1,0:T(8,128)}, f32[4,4,8,256]{3,2,1,0:T(8,128)S(1)}, u32[]{:S(2)}) copy-start(f32[4,4,8,256]{3,2,1,0:T(8,128)S(1)} %pad_maximum_fusion.1.refs_0_.refs_8_) | copy-start | bytes 393220
  19.7 5.9 %collective-permute-start.10 = (f32[4,4,8,256]{3,2,1,0:T(8,128)S(1)}, f32[4,4,8,256]{3,2,1,0:T(8,128)S(1)}, u32[]{:S(2)}, u32[]{:S(2)}) collective-permute-start(f32[4,4,8,256]{3,2,1,0:T(8,128)S(1)} %pad_maximum_fusion.1.refs_0_.refs_8_), channel_id=1, source_target_pairs={{0,17},{1,16},{2,19},{3,18},{4,21},{5,20},{6,23},{7,22},{8,25},{9,... | collective-permute-start | bytes 393224 | tf_op jit(solution)/shard_map/ppermute | solution.py:436
  22.2 5.0 %collective-permute-start.9 = (f32[4,4,8,256]{3,2,1,0:T(8,128)S(1)}, f32[4,4,8,256]{3,2,1,0:T(8,128)S(1)}, u32[]{:S(2)}, u32[]{:S(2)}) collective-permute-start(f32[4,4,8,256]{3,2,1,0:T(8,128)S(1)} %pad_maximum_fusion.1.refs_0_.refs_8_), channel_id=1, source_target_pairs={{0,16},{8,24},{16,0},{24,8},{1,17},{9,25},{17,1},{25,9},{2,18},{10... | collective-permute-start | bytes 393224 | tf_op jit(solution)/shard_map/ppermute | solution.py:432
  22.7 5.0 %collective-permute-start.6 = (f32[4,4,8,256]{3,2,1,0:T(8,128)S(1)}, f32[4,4,8,256]{3,2,1,0:T(8,128)S(1)}, u32[]{:S(2)}, u32[]{:S(2)}) collective-permute-start(f32[4,4,8,256]{3,2,1,0:T(8,128)S(1)} %pad_maximum_fusion.1.refs_0_.refs_8_), channel_id=1, source_target_pairs={{0,1},{1,0},{2,3},{3,2},{4,5},{5,4},{6,7},{7,6},{8,9},{9,8},{10,11... | collective-permute-start | bytes 393224 | tf_op jit(solution)/shard_map/ppermute | solution.py:430
  23.3 5.2 %collective-permute-start = (f32[16,8,256]{2,1,0:T(8,128)}, f32[16,8,256]{2,1,0:T(8,128)S(1)}, u32[]{:S(2)}, u32[]{:S(2)}) collective-permute-start(f32[16,8,256]{2,1,0:T(8,128)} %get-tuple-element.24), channel_id=1, source_target_pairs={{0,2},{1,3},{2,0},{3,1},{4,6},{5,7},{6,4},{7,5},{8,10},{9,11},{10,... | collective-permute-start | bytes 393224 | tf_op jit(solution)/shard_map/ppermute | solution.py:430
  23.5 5.9 %collective-permute-start.7 = (f32[4,4,8,256]{3,2,1,0:T(8,128)S(1)}, f32[4,4,8,256]{3,2,1,0:T(8,128)S(1)}, u32[]{:S(2)}, u32[]{:S(2)}) collective-permute-start(f32[4,4,8,256]{3,2,1,0:T(8,128)S(1)} %pad_maximum_fusion.1.refs_0_.refs_8_), channel_id=1, source_target_pairs={{0,8},{8,0},{16,24},{24,16},{1,9},{9,1},{17,25},{25,17},{2,10},{10... | collective-permute-start | bytes 393224 | tf_op jit(solution)/shard_map/ppermute | solution.py:432
  25.7 39.3 %copy-start.1 = (f32[4,4,8,256]{3,2,1,0:T(8,128)}, f32[4,4,8,256]{3,2,1,0:T(8,128)S(1)}, u32[]{:S(2)}) copy-start(f32[4,4,8,256]{3,2,1,0:T(8,128)S(1)} %collective-permute-done.10.refs_5_.refs_13_) | copy-start | bytes 393220
  25.7 3.8 %collective-permute-start.12 = (f32[4,4,8,256]{3,2,1,0:T(8,128)S(1)}, f32[4,4,8,256]{3,2,1,0:T(8,128)S(1)}, u32[]{:S(2)}, u32[]{:S(2)}) collective-permute-start(f32[4,4,8,256]{3,2,1,0:T(8,128)S(1)} %collective-permute-done.10.refs_5_.refs_13_), channel_id=1, source_target_pairs={{0,8},{8,0},{16,24},{24,16},{1,9},{9,1},{17,25},{25,17},{2,10},{10... | collective-permute-start | bytes 393224 | tf_op jit(solution)/shard_map/ppermute | solution.py:432
  27.2 37.8 %copy-start.2 = (f32[4,4,8,256]{3,2,1,0:T(8,128)}, f32[4,4,8,256]{3,2,1,0:T(8,128)S(1)}, u32[]{:S(2)}) copy-start(f32[4,4,8,256]{3,2,1,0:T(8,128)S(1)} %collective-permute-done.9.refs_4_.refs_12_) | copy-start | bytes 393220
  27.2 2.3 %collective-permute-start.11 = (f32[4,4,8,256]{3,2,1,0:T(8,128)S(1)}, f32[4,4,8,256]{3,2,1,0:T(8,128)S(1)}, u32[]{:S(2)}, u32[]{:S(2)}) collective-permute-start(f32[4,4,8,256]{3,2,1,0:T(8,128)S(1)} %collective-permute-done.9.refs_4_.refs_12_), channel_id=1, source_target_pairs={{0,8},{8,0},{16,24},{24,16},{1,9},{9,1},{17,25},{25,17},{2,10},{10... | collective-permute-start | bytes 393224 | tf_op jit(solution)/shard_map/ppermute | solution.py:432
  27.7 37.3 %copy-start.3 = (f32[4,4,8,256]{3,2,1,0:T(8,128)}, f32[4,4,8,256]{3,2,1,0:T(8,128)S(1)}, u32[]{:S(2)}) copy-start(f32[4,4,8,256]{3,2,1,0:T(8,128)S(1)} %collective-permute-done.6.refs_1_.refs_9_) | copy-start | bytes 393220
  27.7 1.8 %collective-permute-start.8 = (f32[4,4,8,256]{3,2,1,0:T(8,128)S(1)}, f32[4,4,8,256]{3,2,1,0:T(8,128)S(1)}, u32[]{:S(2)}, u32[]{:S(2)}) collective-permute-start(f32[4,4,8,256]{3,2,1,0:T(8,128)S(1)} %collective-permute-done.6.refs_1_.refs_9_), channel_id=1, source_target_pairs={{0,8},{8,0},{16,24},{24,16},{1,9},{9,1},{17,25},{25,17},{2,10},{10... | collective-permute-start | bytes 393224 | tf_op jit(solution)/shard_map/ppermute | solution.py:432
  29.4 35.6 %copy-start.9 = (f32[4,16,8,256]{3,2,1,0:T(8,128)}, f32[4,16,8,256]{3,2,1,0:T(8,128)S(1)}, u32[]{:S(2)}) copy-start(f32[4,16,8,256]{3,2,1,0:T(8,128)S(1)} %pad_maximum_fusion.refs_0_) | copy-start | bytes 1572868
  29.4 35.6 %copy-start.4 = (f32[4,4,8,256]{3,2,1,0:T(8,128)}, f32[4,4,8,256]{3,2,1,0:T(8,128)S(1)}, u32[]{:S(2)}) copy-start(f32[4,4,8,256]{3,2,1,0:T(8,128)S(1)} %collective-permute-done.7.refs_2_.refs_10_) | copy-start | bytes 393220
  29.4 35.6 %copy-start.5 = (f32[4,4,8,256]{3,2,1,0:T(8,128)}, f32[4,4,8,256]{3,2,1,0:T(8,128)S(1)}, u32[]{:S(2)}) copy-start(f32[4,4,8,256]{3,2,1,0:T(8,128)S(1)} %collective-permute-done.12.refs_7_.refs_15_) | copy-start | bytes 393220
  29.5 35.6 %copy-start.6 = (f32[4,4,8,256]{3,2,1,0:T(8,128)}, f32[4,4,8,256]{3,2,1,0:T(8,128)S(1)}, u32[]{:S(2)}) copy-start(f32[4,4,8,256]{3,2,1,0:T(8,128)S(1)} %collective-permute-done.11.refs_6_.refs_14_) | copy-start | bytes 393220
  29.5 35.6 %copy-start.7 = (f32[4,4,8,256]{3,2,1,0:T(8,128)}, f32[4,4,8,256]{3,2,1,0:T(8,128)S(1)}, u32[]{:S(2)}) copy-start(f32[4,4,8,256]{3,2,1,0:T(8,128)S(1)} %collective-permute-done.8.refs_3_.refs_11_) | copy-start | bytes 393220
  29.5 26.8 %collective-permute-start.15 = (f32[4,16,8,256]{3,2,1,0:T(8,128)S(1)}, f32[4,16,8,256]{3,2,1,0:T(8,128)S(1)}, u32[]{:S(2)}, u32[]{:S(2)}) collective-permute-start(f32[4,16,8,256]{3,2,1,0:T(8,128)S(1)} %pad_maximum_fusion.refs_0_), channel_id=1, source_target_pairs={{0,17},{1,16},{2,19},{3,18},{4,21},{5,20},{6,23},{7,22},{8,25},{9,... | collective-permute-start | bytes 1572872 | tf_op jit(solution)/shard_map/ppermute | solution.py:436
  32.0 24.3 %collective-permute-start.14 = (f32[4,16,8,256]{3,2,1,0:T(8,128)S(1)}, f32[4,16,8,256]{3,2,1,0:T(8,128)S(1)}, u32[]{:S(2)}, u32[]{:S(2)}) collective-permute-start(f32[4,16,8,256]{3,2,1,0:T(8,128)S(1)} %pad_maximum_fusion.refs_0_), channel_id=1, source_target_pairs={{0,16},{8,24},{16,0},{24,8},{1,17},{9,25},{17,1},{25,9},{2,18},{10... | collective-permute-start | bytes 1572872 | tf_op jit(solution)/shard_map/ppermute | solution.py:432
  32.5 23.8 %collective-permute-start.13 = (f32[4,16,8,256]{3,2,1,0:T(8,128)S(1)}, f32[4,16,8,256]{3,2,1,0:T(8,128)S(1)}, u32[]{:S(2)}, u32[]{:S(2)}) collective-permute-start(f32[4,16,8,256]{3,2,1,0:T(8,128)S(1)} %pad_maximum_fusion.refs_0_), channel_id=1, source_target_pairs={{0,1},{1,0},{2,3},{3,2},{4,5},{5,4},{6,7},{7,6},{8,9},{9,8},{10,11... | collective-permute-start | bytes 1572872 | tf_op jit(solution)/shard_map/ppermute | solution.py:430
  55.7 0.6 copy-start.8
  56.3 8.7 %copy-start.10 = (f32[4,16,8,256]{3,2,1,0:T(8,128)}, f32[4,16,8,256]{3,2,1,0:T(8,128)S(1)}, u32[]{:S(2)}) copy-start(f32[4,16,8,256]{3,2,1,0:T(8,128)S(1)} %collective-permute-done.15.refs_5_) | copy-start | bytes 1572868
  56.3 8.7 %copy-start.11 = (f32[4,16,8,256]{3,2,1,0:T(8,128)}, f32[4,16,8,256]{3,2,1,0:T(8,128)S(1)}, u32[]{:S(2)}) copy-start(f32[4,16,8,256]{3,2,1,0:T(8,128)S(1)} %collective-permute-done.14.refs_4_) | copy-start | bytes 1572868
  56.4 8.7 %copy-start.12 = (f32[4,16,8,256]{3,2,1,0:T(8,128)}, f32[4,16,8,256]{3,2,1,0:T(8,128)S(1)}, u32[]{:S(2)}) copy-start(f32[4,16,8,256]{3,2,1,0:T(8,128)S(1)} %collective-permute-done.13.refs_1_) | copy-start | bytes 1572868
  56.4 5.5 %collective-permute-start.16 = (f32[4,16,8,256]{3,2,1,0:T(8,128)S(1)}, f32[4,16,8,256]{3,2,1,0:T(8,128)S(1)}, u32[]{:S(2)}, u32[]{:S(2)}) collective-permute-start(f32[4,16,8,256]{3,2,1,0:T(8,128)S(1)} %pad_maximum_fusion.refs_0_), channel_id=1, source_target_pairs={{0,8},{8,0},{16,24},{24,16},{1,9},{9,1},{17,25},{25,17},{2,10},{10... | collective-permute-start | bytes 1572872 | tf_op jit(solution)/shard_map/ppermute | solution.py:432
  60.3 3.0 %collective-permute-start.17 = (f32[4,16,8,256]{3,2,1,0:T(8,128)S(1)}, f32[4,16,8,256]{3,2,1,0:T(8,128)S(1)}, u32[]{:S(2)}, u32[]{:S(2)}) collective-permute-start(f32[4,16,8,256]{3,2,1,0:T(8,128)S(1)} %collective-permute-done.13.refs_1_), channel_id=1, source_target_pairs={{0,8},{8,0},{16,24},{24,16},{1,9},{9,1},{17,25},{25,17},{2,10},{10... | collective-permute-start | bytes 1572872 | tf_op jit(solution)/shard_map/ppermute | solution.py:432
  60.4 3.7 %collective-permute-start.18 = (f32[4,16,8,256]{3,2,1,0:T(8,128)S(1)}, f32[4,16,8,256]{3,2,1,0:T(8,128)S(1)}, u32[]{:S(2)}, u32[]{:S(2)}) collective-permute-start(f32[4,16,8,256]{3,2,1,0:T(8,128)S(1)} %collective-permute-done.14.refs_4_), channel_id=1, source_target_pairs={{0,8},{8,0},{16,24},{24,16},{1,9},{9,1},{17,25},{25,17},{2,10},{10... | collective-permute-start | bytes 1572872 | tf_op jit(solution)/shard_map/ppermute | solution.py:432
  60.8 4.2 %collective-permute-start.19 = (f32[4,16,8,256]{3,2,1,0:T(8,128)S(1)}, f32[4,16,8,256]{3,2,1,0:T(8,128)}, u32[]{:S(2)}, u32[]{:S(2)}) collective-permute-start(f32[4,16,8,256]{3,2,1,0:T(8,128)S(1)} %collective-permute-done.15.refs_5_), channel_id=1, source_target_pairs={{0,8},{8,0},{16,24},{24,16},{1,9},{9,1},{17,25},{25,17},{2,10},{10... | collective-permute-start | bytes 1572872 | tf_op jit(solution)/shard_map/ppermute | solution.py:432
  61.8 3.3 %copy-start.13 = (f32[4,16,8,256]{3,2,1,0:T(8,128)}, f32[4,16,8,256]{3,2,1,0:T(8,128)S(1)}, u32[]{:S(2)}) copy-start(f32[4,16,8,256]{3,2,1,0:T(8,128)S(1)} %collective-permute-done.16.refs_2_) | copy-start | bytes 1572868
  63.3 0.8 copy-start.14
  64.2 0.8 copy-start.15
where the time goes:
time: 115 us; the launch traced here: 117 us
  Pallas kernels  43.8 us (38%)
  blocking collectives  32.7 us (28%)
  starting transfers between devices  21.1 us (18%)
  waiting for transfers between devices  15 us (13%)
  other arithmetic  2.29 us (2%)
  local copies, waits for them, and re-layouts  1.56 us (1%)
    all_to_all x1, blocking collectives, local(): moments = lax.all_to_all(moments, ('row', 'col'), 0, 0, tiled=False)  32.7 us
    pallas_call x1, Pallas kernels, local(): pl.pallas_call(functools.partial(tiles_kernel, len(point_parts), per_devi...  22.7 us
    pallas_call x1, Pallas kernels, local(): pl.pallas_call(functools.partial(apply_kernel, len(value_parts), len(poin...  16.8 us
    ppermute x8, starting transfers between devices, swap(): return lax.ppermute(array, 'col', [(i, i ^ col_mask) for i in range(cols)])  10.5 us
    ppermute x8, waiting for transfers between devices, swap(): return lax.ppermute(array, 'col', [(i, i ^ col_mask) for i in range(cols)])  8.16 us
    ppermute x10, starting transfers between devices, swap(): return lax.ppermute(array, 'row', [(i, i ^ row_mask) for i in range(rows)])  5.54 us
    ppermute x2, starting transfers between devices, swap(): return lax.ppermute(array, ('row', 'col'), pairs)  5.02 us
    ppermute x10, waiting for transfers between devices, swap(): return lax.ppermute(array, 'row', [(i, i ^ row_mask) for i in range(rows)])  4.75 us
  transfers between devices with their start and end apart: 20, of which 9 were waited for; matrix products, arithmetic and copies ran while one was open for 1% of the time, Pallas kernels for 19%

commit v1 on v0

--- a/solution.py
+++ b/solution.py
@@ -52,6 +52,13 @@
     out_ref[3, 0:1, HALF : HALF + tiles] = col_code
     out_ref[3, 1:2, 0:tiles] = col_code
     out_ref[3, 1:2, HALF : HALF + tiles] = row_code
+    lane = lax.broadcasted_iota(jnp.int32, (per_device, LANES), 1)
+    boxes = jnp.zeros((per_device, LANES), jnp.float32)
+    for axis in range(3):
+        line = out_ref[axis]
+        boxes = jnp.where(lane == axis, jnp.min(line, axis=1, keepdims=True), boxes)
+        boxes = jnp.where(lane == 3 + axis, jnp.max(line, axis=1, keepdims=True), boxes)
+    out_ref[3, :, LANES : 2 * LANES] = boxes
 
 
 def split(x):
@@ -60,19 +67,53 @@
     return high, low
 
 
-def evaluate(across, down, high_ref, low_ref):
+def shape_function(square):
+    square = jnp.maximum(square, 1e-30)
+    scaled = square * lax.rsqrt(square)
+    remain = jnp.maximum(1.0 - scaled, 0.0)
+    remain = remain * remain
+    return remain * remain * (scaled + 0.25)
+
+
+def evaluate(across, down, out_ref):
     down = jnp.transpose(jnp.concatenate(down + [jnp.zeros((5, BLK), jnp.float32)], axis=0))
     for s in range(0, BLK, 32):
         square = None
         for axis in range(3):
             gap = down[s : s + 32, axis : axis + 1] - across[axis]
             square = gap * gap if square is None else square + gap * gap
-        scaled = square * lax.rsqrt(jnp.maximum(square, 1e-30))
-        remain = jnp.maximum(1.0 - scaled, 0.0)
-        remain = remain * remain
-        high, low = split(remain * remain * (4.0 * scaled + 1.0))
-        high_ref[s : s + 32, :] = high
-        low_ref[s : s + 32, :] = low
+        high, low = split(shape_function(square))
+        out_ref[0, s : s + 32, :] = high
+        out_ref[1, s : s + 32, :] = low
+
+
+def thirds(x):
+    first = x.astype(jnp.bfloat16).astype(jnp.float32)
+    rest = x - first
+    second = rest.astype(jnp.bfloat16).astype(jnp.float32)
+    return first, second, rest - second
+
+
+def evaluate_flat(across, down, out_ref):
+    blank = [jnp.zeros((5, BLK), jnp.float32)]
+    q = jnp.concatenate(down + blank, axis=0)
+    origin = q[:, 0:1]
+    q = q - origin
+    p = jnp.concatenate(across + blank, axis=0) - origin
+    line = lax.broadcasted_iota(jnp.int32, (8, BLK), 0)
+    qq = jnp.sum(q * q, axis=0, keepdims=True)
+    pp = jnp.sum(p * p, axis=0, keepdims=True)
+    q = jnp.where(line == 3, qq, jnp.where(line == 4, 1.0, q))
+    p = jnp.where(line == 3, 1.0, jnp.where(line == 4, pp, -2.0 * p))
+    q1, q2, q3 = thirds(q)
+    p1, p2, p3 = thirds(p)
+    left = jnp.concatenate([q1, q1, q2, q1, q3, q2], axis=0).astype(jnp.bfloat16)
+    right = jnp.concatenate([p1, p2, p1, p3, p1, p2], axis=0).astype(jnp.bfloat16)
+    square = lax.dot_general(left, right, (((0,), (0,)), ((), ())), preferred_element_type=jnp.float32)
+    for s in range(0, BLK, 32):
+        high, low = split(shape_function(square[s : s + 32]))
+        out_ref[0, s : s + 32, :] = high
+        out_ref[1, s : s + 32, :] = low
 
 
 def point_rows(cloud, b, per_device):
@@ -94,7 +135,7 @@
 
 def tiles_kernel(pieces, per_device, cap, me_ref, *refs):
     list_ref, tile_ref = refs[pieces : pieces + 2]
-    cloud, stage, plan, lists, ring, sems, list_sem, tile_sem = refs[pieces + 2 :]
+    cloud, stage, plan, lists, sems, list_sem = refs[pieces + 2 :]
     devices = cloud.shape[0]
     blocks = devices * per_device
     copies = gather(refs[:pieces], cloud, sems)
@@ -104,33 +145,31 @@
         copy.wait()
 
     mine = me_ref[0] * per_device
-    ids = lax.broadcasted_iota(jnp.int32, (blocks, 2 * LANES), 0)
-
-    def one_hot(pair, line):
-        codes = []
-        for k in range(2):
-            row = cloud[2 * pair + k, 3, line : line + 1, 0:LANES].astype(jnp.int32)
-            codes.append(jnp.where(row >= 0, row ^ mine, -1))
-        codes = jnp.concatenate(codes, axis=1)
-        return jnp.where(ids == codes, 1.0, 0.0).astype(jnp.bfloat16)
-
-    stage[...] = jnp.zeros_like(stage)
-
-    def add_pairs(pair, carry):
-        stage[...] += lax.dot_general(
-            one_hot(pair, 0), one_hot(pair, 1), (((1,), (1,)), ((), ())), preferred_element_type=jnp.float32
-        )
+    ids = lax.broadcasted_iota(jnp.int32, (blocks, LANES), 0)
+    batch = 8
+
+    def one_hot(device, line):
+        row = cloud[device, 3, line : line + 1, 0:LANES].astype(jnp.int32)
+        row = jnp.where(row >= 0, row ^ mine, -1)
+        return jnp.where(ids == row, 1.0, 0.0).astype(jnp.bfloat16)
+
+    def pairs_of(group):
+        sides = [
+            jnp.concatenate([one_hot(group * batch + k, line) for k in range(batch)], axis=1) for line in range(2)
+        ]
+        return lax.dot_general(*sides, (((1,), (1,)), ((), ())), preferred_element_type=jnp.float32)
+
+    stage[...] = pairs_of(0)
+
+    def add_pairs(group, carry):
+        stage[...] += pairs_of(group)
         return carry
 
-    lax.fori_loop(0, devices // 2, add_pairs, 0)
-
-    lane = lax.broadcasted_iota(jnp.int32, (blocks, LANES), 1)
-    boxes = jnp.zeros((blocks, LANES), jnp.float32)
-    for axis in range(3):
-        coordinates = cloud[:, axis].reshape(blocks, BLK)
-        boxes = jnp.where(lane == axis, jnp.min(coordinates, axis=1, keepdims=True), boxes)
-        boxes = jnp.where(lane == 3 + axis, jnp.max(coordinates, axis=1, keepdims=True), boxes)
+    lax.fori_loop(1, devices // batch, add_pairs, 0)
+
+    boxes = cloud[:, 3, :, LANES : 2 * LANES].reshape(blocks, LANES)
     flat = jnp.transpose(boxes)
+    extent = jnp.max(flat[3:6, :] - flat[0:3, :])
     apart = None
     for axis in range(3):
         gap = jnp.maximum(
@@ -150,10 +189,14 @@
     near_col = near_col | (lax.broadcasted_iota(jnp.int32, (blocks, 1), 0) < per_device)
     near = jnp.where(near_row, 1.0, 0.0) + jnp.where(near_col, 1.0, 0.0)
     used = jnp.where(listed & (rows >= cols) & (near > 0.0), 1.0, 0.0)
-    exact = dict(precision=lax.Precision.HIGHEST, preferred_element_type=jnp.float32)
-    rank = jnp.dot(jnp.where(rows >= cols, 1.0, 0.0), used, **exact)
+
+    def counted(left, right):
+        return jnp.dot(left.astype(jnp.bfloat16), right.astype(jnp.bfloat16), preferred_element_type=jnp.float32)
+
+    rank = counted(jnp.where(rows >= cols, 1.0, 0.0), used)
     count = jnp.broadcast_to(rank[blocks - 1 : blocks, :], (8, blocks))
-    start = jnp.dot(count, jnp.where(rows < cols, 1.0, 0.0), **exact)
+    start = jnp.sum(counted(used, jnp.where(rows < cols, 1.0, 0.0)), axis=0, keepdims=True)
+    start = jnp.broadcast_to(start, (8, blocks))
     n = jnp.sum(count[0:1, :]).astype(jnp.int32)
     own = lax.broadcasted_iota(jnp.int32, (1, blocks), 1) < per_device
     n_own = jnp.sum(jnp.where(own, count[0:1, :], 0.0)).astype(jnp.int32)
@@ -167,7 +210,8 @@
         pick = jnp.where((start_col <= place) & (place < stop_col), 1.0, 0.0)
         low_index = jnp.sum(pick * index_col, axis=0, keepdims=True)
         begin = jnp.sum(pick * start_col, axis=0, keepdims=True)
-        ranks = jnp.dot(stage[...], pick, **exact)
+        high, low = split(stage[...])
+        ranks = counted(high, pick) + counted(low, pick)
         match = jnp.where(ranks == place - begin + 1.0, 1.0, 0.0)
         high_index = jnp.sum(match * index_col, axis=0, keepdims=True)
         both = jnp.concatenate([low_index, high_index], axis=0).astype(jnp.int32)
@@ -183,42 +227,33 @@
 
     lax.fori_loop(0, jnp.maximum((n + CHUNK - 1) // CHUNK, 1), write_list, 0)
 
-    def send(step):
-        slot = step & 1
-        return pltpu.make_async_copy(ring.at[slot], tile_ref.at[pl.ds(2 * step, 2)], tile_sem.at[slot])
-
-    def write_tiles(step, carry):
-        slot = step & 1
-
-        @pl.when(step >= 2)
-        def _():
-            send(step - 2).wait()
-
-        for part in range(2):
-            i, j = entry(lists, 2 * step + part)
-            evaluate(
-                point_rows(cloud, i, per_device),
-                point_rows(cloud, j, per_device),
-                ring.at[slot, part, 0],
-                ring.at[slot, part, 1],
-            )
-        send(step).start()
-        return carry
-
-    steps = (jnp.minimum(n, cap) + 1) // 2
-    lax.fori_loop(0, steps, write_tiles, 0)
-    for back in (2, 1):
-
-        @pl.when(steps >= back)
-        def _():
-            send(steps - back).wait()
+    held = jnp.minimum(n, cap)
+
+    def write_tiles(form, step):
+        def body(k, carry):
+            for part in range(step):
+                i, j = entry(lists, k * step + part)
+                form(
+                    point_rows(cloud, i, per_device), point_rows(cloud, j, per_device), tile_ref.at[k * step + part]
+                )
+            return carry
+
+        lax.fori_loop(0, (held + step - 1) // step, body, 0)
+
+    @pl.when(extent <= 1.5 / support)
+    def _():
+        write_tiles(evaluate_flat, UNROLL)
+
+    @pl.when(extent > 1.5 / support)
+    def _():
+        write_tiles(evaluate, 2)
 
 
 def apply_kernel(pieces, point_pieces, per_device, cap, lists, tile_ref, *refs):
     value_refs = refs[:pieces]
     point_refs = refs[pieces : pieces + point_pieces]
     w_ref, x_ref, moment_ref = refs[pieces + point_pieces : pieces + point_pieces + 3]
-    field, total, second, cache, cloud, sems, total_sems, point_sems, tile_sems = refs[pieces + point_pieces + 3 :]
+    field, total, second, late, cloud, sems, point_sems = refs[pieces + point_pieces + 3 :]
     devices = field.shape[0]
     blocks = devices * per_device
     block_shift = per_device.bit_length() - 1
@@ -226,33 +261,22 @@
     n = lists[0, 2, 0]
     n_own = lists[0, 3, 0]
     held = jnp.minimum(n, cap)
-    groups = (held + GROUP - 1) // GROUP
-
-    def fetch(group):
-        span = pl.ds(group * GROUP, GROUP)
-        return pltpu.make_async_copy(tile_ref.at[span], cache.at[span], tile_sems.at[group])
-
-    fills = gather(value_refs, field, sems) + gather(value_refs, total.at[pl.ds(0, devices)], total_sems)
+    fills = gather(value_refs, field, sems)
     for copy in fills:
         copy.start()
-
-    def start_fetch(group, carry):
-        fetch(group).start()
-        return carry
-
-    lax.fori_loop(0, groups, start_fetch, 0)
+    total[...] = jnp.zeros_like(total)
     for copy in fills:
         copy.wait()
 
     def at(b):
         return lax.shift_right_logical(b, block_shift), pl.ds(2 * (b & low_mask), 2)
 
-    def product(vector, slot, contract):
-        high, low = split(vector)
+    def product(vector, tile, contract):
+        high, low = split(4.0 * vector)
         both = jnp.concatenate([high, low], axis=0)
         dims = (((1,), (contract,)), ((), ()))
-        first = lax.dot_general(both, cache[slot, 0], dims, preferred_element_type=jnp.float32)
-        later = lax.dot_general(high, cache[slot, 1], dims, preferred_element_type=jnp.float32)
+        first = lax.dot_general(both, tile[0], dims, preferred_element_type=jnp.float32)
+        later = lax.dot_general(high, tile[1], dims, preferred_element_type=jnp.float32)
         return (first[0:16] + first[16:32] + later).reshape(2, 8, BLK)
 
     def load(ref, b):
@@ -265,26 +289,25 @@
 
     def evaluate_late(k):
         i, j = entry(lists, k)
-        evaluate(
-            point_rows(cloud, i, per_device), point_rows(cloud, j, per_device), cache.at[cap, 0], cache.at[cap, 1]
-        )
+        evaluate(point_rows(cloud, i, per_device), point_rows(cloud, j, per_device), late)
         return i, j
 
+    def image(b):
+        return load(total, b) + load(field, b)
+
     def first_group(group, carry):
-        fetch(group).wait()
-        for quad in range(0, GROUP, UNROLL):
-            pending = []
-            for u in range(UNROLL):
-                k = group * GROUP + quad + u
-                i, j = entry(lists, k)
-                live = k < held
-                pending.append((jnp.where(live, i, blocks), product(load(field, j), k, 0)))
-                pending.append((jnp.where(live & (i != j), j, blocks), product(load(field, i), k, 1)))
-            for b, value in pending:
-                add(total, b, value)
+        pending = []
+        for u in range(GROUP):
+            k = group * GROUP + u
+            i, j = entry(lists, k)
+            live = k < held
+            pending.append((jnp.where(live, i, blocks), product(load(field, j), tile_ref.at[k], 0)))
+            pending.append((jnp.where(live & (i != j), j, blocks), product(load(field, i), tile_ref.at[k], 1)))
+        for b, value in pending:
+            add(total, b, value)
         return carry
 
-    lax.fori_loop(0, groups, first_group, 0)
+    lax.fori_loop(0, (held + GROUP - 1) // GROUP, first_group, 0)
 
     @pl.when(n > cap)
     def _():
@@ -296,54 +319,54 @@
 
         def first_late(k, carry):
             i, j = evaluate_late(k)
-            add(total, i, product(load(field, j), cap, 0))
+            add(total, i, product(load(field, j), late, 0))
 
             @pl.when(i != j)
             def _():
-                add(total, j, product(load(field, i), cap, 1))
+                add(total, j, product(load(field, i), late, 1))
 
             return carry
 
         lax.fori_loop(cap, n, first_late, 0)
 
-    second[0] = total[0]
+    second[0] = total[0] + field[0]
     held_own = jnp.minimum(n_own, cap)
 
     def second_group(group, carry):
         pending = []
-        for u in range(UNROLL):
-            k = group * UNROLL + u
+        for u in range(GROUP):
+            k = group * GROUP + u
             i, j = entry(lists, k)
             live = k < held_own
-            pending.append((jnp.where(live, i, per_device), product(load(total, j), k, 0)))
+            pending.append((jnp.where(live, i, per_device), product(image(j), tile_ref.at[k], 0)))
         for b, value in pending:
             add(second, b, value)
-        for u in range(UNROLL):
-            k = group * UNROLL + u
+        for u in range(GROUP):
+            k = group * GROUP + u
             i, j = entry(lists, k)
 
             @pl.when((k < held_own) & (i != j) & (j < per_device))
             def _():
-                add(second, j, product(load(total, i), k, 1))
+                add(second, j, product(image(i), tile_ref.at[k], 1))
 
         return carry
 
-    lax.fori_loop(0, (held_own + UNROLL - 1) // UNROLL, second_group, 0)
+    lax.fori_loop(0, (held_own + GROUP - 1) // GROUP, second_group, 0)
 
     def second_late(k, carry):
         i, j = evaluate_late(k)
-        add(second, i, product(load(total, j), cap, 0))
+        add(second, i, product(image(j), late, 0))
 
         @pl.when((i != j) & (j < per_device))
         def _():
-            add(second, j, product(load(total, i), cap, 1))
+            add(second, j, product(image(i), late, 1))
 
         return carry
 
     lax.fori_loop(cap, n_own, second_late, 0)
 
     v = field[0].reshape(per_device, 16, BLK)
-    w = total[0].reshape(per_device, 16, BLK)
+    w = (total[0] + field[0]).reshape(per_device, 16, BLK)
     x = second[0].reshape(per_device, 16, BLK)
     w_ref[...] = w
     x_ref[...] = x
@@ -450,34 +473,35 @@
             plane[row_mask + 1, x] = swap(part, 1, 0)
         return [plane[row_mask, x] for row_mask in range(rows) for x in range(2)]
 
-    point_parts = pairs(across(along(own_points)))
-    value_line = along(own_values)
-    value_line, point_parts = lax.optimization_barrier((value_line, point_parts))
+    point_plane = across(along(own_points))
+    value_line, point_plane = lax.optimization_barrier((along(own_values), point_plane))
+    point_parts = pairs(point_plane)
     value_plane = across(value_line)
 
     me = row_id * cols + (col_id & 1) * depth + lax.shift_right_logical(col_id, 1)
     chunks = (devices * tile_lists.shape[1] + CHUNK - 1) // CHUNK
-    used = 2 * blocks * fields * BLK * 4
-    cap = max(GROUP, min(152, (54 * 2**20 - used) // (BLK * BLK * 4) // GROUP * GROUP))
+    tile_bytes = 4 * BLK * BLK
+    cloud_bytes = devices * 4 * per_device * BLK * 4
+    tiles_limit = cloud_bytes + 6 * 4 * blocks * blocks + 12 * 2**20
+    apply_limit = cloud_bytes + 2 * blocks * fields * BLK * 4 + 10 * 2**20
+    cap = max(GROUP, min(152, (60 * 2**20 - max(tiles_limit, apply_limit)) // tile_bytes // GROUP * GROUP))
     lists, tiles = pl.pallas_call(
         functools.partial(tiles_kernel, len(point_parts), per_device, cap),
         out_shape=(
             jax.ShapeDtypeStruct((chunks, 8, CHUNK), jnp.int32),
-            jax.ShapeDtypeStruct((cap, 2, BLK, BLK), jnp.bfloat16),
+            pltpu.VMEM((cap, 2, BLK, BLK), jnp.bfloat16),
         ),
         in_specs=[smem] + [anywhere] * len(point_parts),
-        out_specs=(vmem, anywhere),
+        out_specs=(vmem, vmem),
         scratch_shapes=[
             pltpu.VMEM((devices, 4, per_device, BLK), jnp.float32),
             pltpu.VMEM((blocks, blocks), jnp.float32),
             pltpu.VMEM((8, CHUNK), jnp.int32),
             pltpu.SMEM((chunks, 8, CHUNK), jnp.int32),
-            pltpu.VMEM((2, 2, 2, BLK, BLK), jnp.bfloat16),
             pltpu.SemaphoreType.DMA((len(point_parts),)),
             pltpu.SemaphoreType.DMA,
-            pltpu.SemaphoreType.DMA((2,)),
         ],
-        compiler_params=pltpu.CompilerParams(vmem_limit_bytes=40 * 2**20),
+        compiler_params=pltpu.CompilerParams(vmem_limit_bytes=tiles_limit),
         cost_estimate=pl.CostEstimate(flops=10**9, bytes_accessed=30 * 2**20, transcendentals=10**7),
         name="tiles",
     )(me.reshape(1).astype(jnp.int32), *point_parts)
@@ -487,22 +511,20 @@
     w, x, moments = pl.pallas_call(
         functools.partial(apply_kernel, len(value_parts), len(point_parts), per_device, cap),
         out_shape=(block_shape, block_shape, jax.ShapeDtypeStruct((devices, 8, LANES), jnp.float32)),
-        in_specs=[smem, anywhere] + [anywhere] * (len(value_parts) + len(point_parts)),
+        in_specs=[smem, vmem] + [anywhere] * (len(value_parts) + len(point_parts)),
         out_specs=(vmem, vmem, vmem),
         scratch_shapes=[
             pltpu.VMEM((devices, height, 8, BLK), jnp.float32),
             pltpu.VMEM((devices + 1, height, 8, BLK), jnp.float32),
             pltpu.VMEM((2, height, 8, BLK), jnp.float32),
-            pltpu.VMEM((cap + 1, 2, BLK, BLK), jnp.bfloat16),
+            pltpu.VMEM((2, BLK, BLK), jnp.bfloat16),
             pltpu.VMEM((devices, 4, per_device, BLK), jnp.float32),
             pltpu.SemaphoreType.DMA((len(value_parts),)),
-            pltpu.SemaphoreType.DMA((len(value_parts),)),
             pltpu.SemaphoreType.DMA((len(point_parts),)),
-            pltpu.SemaphoreType.DMA((cap // GROUP,)),
         ],
-        compiler_params=pltpu.CompilerParams(vmem_limit_bytes=60 * 2**20),
+        compiler_params=pltpu.CompilerParams(vmem_limit_bytes=apply_limit),
         name="apply",
-    )(lists, tiles, *value_parts, *point_parts)
+    )(lists, pltpu.with_memory_space_constraint(tiles, pltpu.VMEM), *value_parts, *point_parts)
     moments = lax.all_to_all(moments, ("row", "col"), 0, 0, tiled=False)
     return pl.pallas_call(
         functools.partial(finish_kernel, per_device),

time: 115 us -> 92.7 us (0.81); the launches traced: 117 us -> 92.5 us
  blocking collectives: 32.7 us -> 15.9 us
  Pallas kernels: 43.8 us -> 35.3 us
  starting transfers between devices: 21.1 us -> 22.6 us
    all_to_all x1, blocking collectives: 32.7 us -> 15.9 us  [local(): moments = lax.all_to_all(moments, ('row', 'col'), 0, 0, tiled=False)]
    pallas_call x1, Pallas kernels: 22.7 us -> 15.4 us  [local(): pl.pallas_call(functools.partial(tiles_kernel, len(point_parts), per_devi...]
    ppermute x10, waiting for transfers between devices: 4.75 us -> 7.4 us  [swap(): return lax.ppermute(array, 'row', [(i, i ^ row_mask) for i in range(rows)])]
    ppermute x2, waiting for transfers between devices: 2.11 us -> 0.01 us  [swap(): return lax.ppermute(array, ('row', 'col'), pairs)]
    ppermute x10, starting transfers between devices: 5.54 us -> 6.94 us  [swap(): return lax.ppermute(array, 'row', [(i, i ^ row_mask) for i in range(rows)])]
    ppermute x8, waiting for transfers between devices: 8.16 us -> 6.76 us  [swap(): return lax.ppermute(array, 'col', [(i, i ^ col_mask) for i in range(cols)])]
    pallas_call x1, Pallas kernels: 16.8 us -> 15.5 us  [local(): pl.pallas_call(functools.partial(apply_kernel, len(value_parts), len(poin...]
  transfers between devices with their start and end apart: 20 -> 20, of which waited for: 9 -> 12; matrix products, arithmetic and copies ran while one was open for 1% -> 2% of each run, Pallas kernels for 19% -> 17%
where the time goes in v1:
time: 92.7 us; the launch traced here: 92.5 us
  Pallas kernels  35.3 us (38%)
  starting transfers between devices  22.6 us (24%)
  blocking collectives  15.9 us (17%)
  waiting for transfers between devices  14.2 us (15%)
  other arithmetic  2.31 us (2%)
  local copies, waits for them, and re-layouts  1.46 us (2%)
    all_to_all x1, blocking collectives, local(): moments = lax.all_to_all(moments, ('row', 'col'), 0, 0, tiled=False)  15.9 us
    pallas_call x1, Pallas kernels, local(): pl.pallas_call(functools.partial(apply_kernel, len(value_parts), len(poin...  15.5 us
    pallas_call x1, Pallas kernels, local(): pl.pallas_call(functools.partial(tiles_kernel, len(point_parts), per_devi...  15.4 us
    ppermute x8, starting transfers between devices, swap(): return lax.ppermute(array, 'col', [(i, i ^ col_mask) for i in range(cols)])  11.6 us
    ppermute x10, waiting for transfers between devices, swap(): return lax.ppermute(array, 'row', [(i, i ^ row_mask) for i in range(rows)])  7.4 us
    ppermute x10, starting transfers between devices, swap(): return lax.ppermute(array, 'row', [(i, i ^ row_mask) for i in range(rows)])  6.94 us
    ppermute x8, waiting for transfers between devices, swap(): return lax.ppermute(array, 'col', [(i, i ^ col_mask) for i in range(cols)])  6.76 us
    ppermute x2, starting transfers between devices, swap(): return lax.ppermute(array, ('row', 'col'), pairs)  4 us
  transfers between devices with their start and end apart: 20, of which 12 were waited for; matrix products, arithmetic and copies ran while one was open for 2% of the time, Pallas kernels for 17%

profile of v1, /device:TPU:0, one launch (start us, length us, event | category | flops | bytes accessed | tf_op | source)
XLA Modules:
  0.0 92.5 jit_solution(5771322657048554787)
XLA Ops:
  0.6 0.6 pad_add_fusion.place_ref
  1.2 1.7 %pack.1 = (f32[16,8,256]{2,1,0:T(8,128)}, f32[4,8,256]{2,1,0:T(8,128)}) custom-call(s32[4]{0:T(128)} %pad_add_fusion.place_ref, f32[16,2048]{1,0:T(8,128)} %values_ref.3, f32[3,2048]{1,0:T(4,128)} %points_ref.1, s32[3,48]{1,0:T(4,128)} %lists_ref.1), custom_call_target="tpu_custom_call" | custom-call | tf_op jit(solution)/shard_map/pack/pallas_call | solution.py:440
  2.9 5.0 %collective-permute-start.5 = (f32[4,8,256]{2,1,0:T(8,128)}, f32[4,8,256]{2,1,0:T(8,128)S(1)}, u32[]{:S(2)}, u32[]{:S(2)}) collective-permute-start(f32[4,8,256]{2,1,0:T(8,128)} %get-tuple-element.21), channel_id=1, source_target_pairs={{0,6},{1,7},{2,4},{3,5},{4,2},{5,3},{6,0},{7,1},{8,14},{9,15},{10,... | collective-permute-start | bytes 98312 | tf_op jit(solution)/shard_map/ppermute | solution.py:453
  7.9 0.0 collective-permute-start.4
  7.9 0.6 collective-permute-start.3
  8.5 3.8 %collective-permute-start.2 = (f32[16,8,256]{2,1,0:T(8,128)}, f32[16,8,256]{2,1,0:T(8,128)S(1)}, u32[]{:S(2)}, u32[]{:S(2)}) collective-permute-start(f32[16,8,256]{2,1,0:T(8,128)} %get-tuple-element.20), channel_id=1, source_target_pairs={{0,6},{1,7},{2,4},{3,5},{4,2},{5,3},{6,0},{7,1},{8,14},{9,15},{10,... | collective-permute-start | bytes 393224 | tf_op jit(solution)/shard_map/ppermute | solution.py:453
  12.3 0.0 collective-permute-start.1
  12.3 0.0 collective-permute-done.5
  12.3 0.6 collective-permute-start
  12.9 4.6 %collective-permute-done.4 = f32[4,8,256]{2,1,0:T(8,128)S(1)} collective-permute-done((f32[4,8,256]{2,1,0:T(8,128)}, f32[4,8,256]{2,1,0:T(8,128)S(1)}, u32[]{:S(2)}, u32[]{:S(2)}) %collective-permute-start.4) | collective-permute-done | bytes 32800 | tf_op jit(solution)/shard_map/ppermute | solution.py:453
  17.5 0.0 collective-permute-done.3
  17.5 0.8 pad_maximum_fusion.1.refs_0_.refs_8_
  18.3 0.0 copy-start
  18.3 2.5 %collective-permute-start.8 = (f32[4,4,8,256]{3,2,1,0:T(8,128)S(1)}, f32[4,4,8,256]{3,2,1,0:T(8,128)S(1)}, u32[]{:S(2)}, u32[]{:S(2)}) collective-permute-start(f32[4,4,8,256]{3,2,1,0:T(8,128)S(1)} %pad_maximum_fusion.1.refs_0_.refs_8_), channel_id=1, source_target_pairs={{0,17},{1,16},{2,19},{3,18},{4,21},{5,20},{6,23},{7,22},{8,25},{9,... | collective-permute-start | bytes 393224 | tf_op jit(solution)/shard_map/ppermute | solution.py:459
  20.8 0.5 collective-permute-start.7
  21.3 0.5 collective-permute-start.6
  21.8 1.6 %collective-permute-done.1 = f32[16,8,256]{2,1,0:T(8,128)S(1)} collective-permute-done((f32[16,8,256]{2,1,0:T(8,128)}, f32[16,8,256]{2,1,0:T(8,128)S(1)}, u32[]{:S(2)}, u32[]{:S(2)}) %collective-permute-start.1) | collective-permute-done | bytes 131104 | tf_op jit(solution)/shard_map/ppermute | solution.py:453
  23.5 0.0 collective-permute-done
  23.5 0.9 %pad_maximum_fusion.refs_0_ = f32[4,16,8,256]{3,2,1,0:T(8,128)S(1)} fusion(f32[1,16,8,256]{3,2,1,0:T(8,128)S(1)} %bitcast.12, f32[1,16,8,256]{3,2,1,0:T(8,128)S(1)} %bitcast.13, f32[1,16,8,256]{3,2,1,0:T(8,128)S(1)} %bitcast.14, f32[1,16,8,256]{3,2,1,0:T(8,128)} %bitcast.11), kind=kLoop, calls=%fused_computation | loop fusion | flops 393216 | bytes 1048576 | tf_op jit(solution)/shard_map/stack | solution.py:462
  24.4 0.0 collective-permute-done.8.refs_5_.refs_13_
  24.5 1.3 %collective-permute-done.7.refs_4_.refs_12_ = f32[4,4,8,256]{3,2,1,0:T(8,128)S(1)} collective-permute-done((f32[4,4,8,256]{3,2,1,0:T(8,128)S(1)}, f32[4,4,8,256]{3,2,1,0:T(8,128)S(1)}, u32[]{:S(2)}, u32[]{:S(2)}) %collective-permute-start.7) | collective-permute-done | bytes 131104 | tf_op jit(solution)/shard_map/ppermute | solution.py:455
  25.8 0.5 collective-permute-done.6.refs_1_.refs_9_
  26.3 1.5 %collective-permute-start.11 = (f32[4,16,8,256]{3,2,1,0:T(8,128)S(1)}, f32[4,16,8,256]{3,2,1,0:T(8,128)S(1)}, u32[]{:S(2)}, u32[]{:S(2)}) collective-permute-start(f32[4,16,8,256]{3,2,1,0:T(8,128)S(1)} %pad_maximum_fusion.refs_0_), channel_id=1, source_target_pairs={{0,17},{1,16},{2,19},{3,18},{4,21},{5,20},{6,23},{7,22},{8,25},{9,... | collective-permute-start | bytes 1572872 | tf_op jit(solution)/shard_map/ppermute | solution.py:459
  27.8 0.9 collective-permute-start.10
  28.7 1.1 %collective-permute-start.9 = (f32[4,16,8,256]{3,2,1,0:T(8,128)S(1)}, f32[4,16,8,256]{3,2,1,0:T(8,128)S(1)}, u32[]{:S(2)}, u32[]{:S(2)}) collective-permute-start(f32[4,16,8,256]{3,2,1,0:T(8,128)S(1)} %pad_maximum_fusion.refs_0_), channel_id=1, source_target_pairs={{0,1},{1,0},{2,3},{3,2},{4,5},{5,4},{6,7},{7,6},{8,9},{9,8},{10,11... | collective-permute-start | bytes 1572872 | tf_op jit(solution)/shard_map/ppermute | solution.py:453
  29.8 0.0 collective-permute-start.12
  29.8 0.5 collective-permute-start.13
  30.3 0.8 collective-permute-done.12.refs_2_.refs_10_
  31.1 0.1 collective-permute-start.14
  31.3 0.0 collective-permute-done.13.refs_3_.refs_11_
  31.3 0.3 collective-permute-start.15
  31.6 0.8 collective-permute-done.14.refs_6_.refs_14_
  32.5 0.2 collective-permute-done.15.refs_7_.refs_15_
  32.7 15.4 %tiles.1 = (s32[6,8,256]{2,1,0:T(8,128)S(1)}, bf16[152,2,256,256]{3,2,1,0:T(8,128)(2,1)S(1)}) custom-call(s32[1]{0:T(128)} %bitcast.10.me_ref, f32[4,4,8,256]{3,2,1,0:T(8,128)S(1)} %pad_maximum_fusion.1.refs_0_.refs_8_, f32[4,4,8,256]{3,2,1,0:T(8,128)S(1)} %collective-permute-done.6.refs_1_.refs_9_, ...), custom_call_target="tpu_custom_call" | custom-call | flops 1000000000 | bytes 31457280 | tf_op jit(solution)/shard_map/tiles/pallas_call | solution.py:488
  48.1 0.6 copy-done.8
  48.7 1.0 %collective-permute-done.10.refs_4_ = f32[4,16,8,256]{3,2,1,0:T(8,128)S(1)} collective-permute-done((f32[4,16,8,256]{3,2,1,0:T(8,128)S(1)}, f32[4,16,8,256]{3,2,1,0:T(8,128)S(1)}, u32[]{:S(2)}, u32[]{:S(2)}) %collective-permute-start.10) | collective-permute-done | bytes 524320 | tf_op jit(solution)/shard_map/ppermute | solution.py:455
  49.7 4.0 %collective-permute-start.16 = (f32[4,16,8,256]{3,2,1,0:T(8,128)S(1)}, f32[4,16,8,256]{3,2,1,0:T(8,128)S(1)}, u32[]{:S(2)}, u32[]{:S(2)}) collective-permute-start(f32[4,16,8,256]{3,2,1,0:T(8,128)S(1)} %pad_maximum_fusion.refs_0_), channel_id=1, source_target_pairs={{0,8},{8,0},{16,24},{24,16},{1,9},{9,1},{17,25},{25,17},{2,10},{10... | collective-permute-start | bytes 1572872 | tf_op jit(solution)/shard_map/ppermute | solution.py:455
  53.7 0.1 collective-permute-start.17
  53.7 0.4 collective-permute-start.18
  54.2 0.1 collective-permute-start.19
  54.3 0.9 %collective-permute-done.16.refs_2_ = f32[4,16,8,256]{3,2,1,0:T(8,128)S(1)} collective-permute-done((f32[4,16,8,256]{3,2,1,0:T(8,128)S(1)}, f32[4,16,8,256]{3,2,1,0:T(8,128)S(1)}, u32[]{:S(2)}, u32[]{:S(2)}) %collective-permute-start.16) | collective-permute-done | bytes 524320 | tf_op jit(solution)/shard_map/ppermute | solution.py:455
  55.2 0.7 collective-permute-done.17.refs_3_
  56.0 0.7 collective-permute-done.18.refs_6_
  56.7 0.7 collective-permute-done.19.refs_7_
  57.6 0.8 copy-done.16
  58.4 15.5 %apply.1 = (f32[8,16,256]{2,1,0:T(8,128)}, f32[8,16,256]{2,1,0:T(8,128)}, f32[32,8,128]{2,1,0:T(8,128)}) custom-call(s32[6,8,256]{2,1,0:T(8,128)} %copy-done.8, bf16[152,2,256,256]{3,2,1,0:T(8,128)(2,1)S(1)} %get-tuple-element.30.tile_ref, f32[4,16,8,256]{3,2,1,0:T(8,128)} %copy-done.9, f32[4,16,8,256]{3,2,1,0:T(8,128)} %copy-done.12, ...), custom_call_target="tpu_custom_call" | custom-call | tf_op jit(solution)/shard_map/apply/pallas_call | solution.py:511
  73.9 15.9 %all_to_all.5.moment_ref = f32[32,8,128]{2,1,0:T(8,128)} all-to-all(f32[32,8,128]{2,1,0:T(8,128)} %get-tuple-element.35), channel_id=1, replica_groups=mesh['row'=4,'col'=8] {'row','col'}, dimensions={0} | all-to-all | bytes 262144 | tf_op jit(solution)/shard_map/all_to_all | solution.py:528
  89.8 2.7 %finish.1 = (f32[16,2048]{1,0:T(8,128)}, f32[16,2048]{1,0:T(8,128)}) custom-call(f32[32,8,128]{2,1,0:T(8,128)} %all_to_all.5.moment_ref, f32[16,2048]{1,0:T(8,128)} %values_ref.3, f32[8,16,256]{2,1,0:T(8,128)} %get-tuple-element.36.w_ref, f32[8,16,256]{2,1,0:T(8,128)} %get-tuple-element.37.x_ref), custom_call_target="tpu_custom_call" | custom-call | tf_op jit(solution)/shard_map/finish/pallas_call | solution.py:529
  (34 shorter events, 0.1 us)
Async XLA Ops:
  2.9 9.4 %collective-permute-start.5 = (f32[4,8,256]{2,1,0:T(8,128)}, f32[4,8,256]{2,1,0:T(8,128)S(1)}, u32[]{:S(2)}, u32[]{:S(2)}) collective-permute-start(f32[4,8,256]{2,1,0:T(8,128)} %get-tuple-element.21), channel_id=1, source_target_pairs={{0,6},{1,7},{2,4},{3,5},{4,2},{5,3},{6,0},{7,1},{8,14},{9,15},{10,... | collective-permute-start | bytes 98312 | tf_op jit(solution)/shard_map/ppermute | solution.py:453
  7.9 9.6 %collective-permute-start.4 = (f32[4,8,256]{2,1,0:T(8,128)}, f32[4,8,256]{2,1,0:T(8,128)S(1)}, u32[]{:S(2)}, u32[]{:S(2)}) collective-permute-start(f32[4,8,256]{2,1,0:T(8,128)} %get-tuple-element.21), channel_id=1, source_target_pairs={{0,4},{1,5},{2,6},{3,7},{4,0},{5,1},{6,2},{7,3},{8,12},{9,13},{10,... | collective-permute-start | bytes 98312 | tf_op jit(solution)/shard_map/ppermute | solution.py:453
  7.9 9.6 %collective-permute-start.3 = (f32[4,8,256]{2,1,0:T(8,128)}, f32[4,8,256]{2,1,0:T(8,128)S(1)}, u32[]{:S(2)}, u32[]{:S(2)}) collective-permute-start(f32[4,8,256]{2,1,0:T(8,128)} %get-tuple-element.21), channel_id=1, source_target_pairs={{0,2},{1,3},{2,0},{3,1},{4,6},{5,7},{6,4},{7,5},{8,10},{9,11},{10,... | collective-permute-start | bytes 98312 | tf_op jit(solution)/shard_map/ppermute | solution.py:453
  8.5 12.8 %collective-permute-start.2 = (f32[16,8,256]{2,1,0:T(8,128)}, f32[16,8,256]{2,1,0:T(8,128)S(1)}, u32[]{:S(2)}, u32[]{:S(2)}) collective-permute-start(f32[16,8,256]{2,1,0:T(8,128)} %get-tuple-element.20), channel_id=1, source_target_pairs={{0,6},{1,7},{2,4},{3,5},{4,2},{5,3},{6,0},{7,1},{8,14},{9,15},{10,... | collective-permute-start | bytes 393224 | tf_op jit(solution)/shard_map/ppermute | solution.py:453
  12.3 11.2 %collective-permute-start.1 = (f32[16,8,256]{2,1,0:T(8,128)}, f32[16,8,256]{2,1,0:T(8,128)S(1)}, u32[]{:S(2)}, u32[]{:S(2)}) collective-permute-start(f32[16,8,256]{2,1,0:T(8,128)} %get-tuple-element.20), channel_id=1, source_target_pairs={{0,4},{1,5},{2,6},{3,7},{4,0},{5,1},{6,2},{7,3},{8,12},{9,13},{10,... | collective-permute-start | bytes 393224 | tf_op jit(solution)/shard_map/ppermute | solution.py:453
  12.3 11.2 %collective-permute-start = (f32[16,8,256]{2,1,0:T(8,128)}, f32[16,8,256]{2,1,0:T(8,128)S(1)}, u32[]{:S(2)}, u32[]{:S(2)}) collective-permute-start(f32[16,8,256]{2,1,0:T(8,128)} %get-tuple-element.20), channel_id=1, source_target_pairs={{0,2},{1,3},{2,0},{3,1},{4,6},{5,7},{6,4},{7,5},{8,10},{9,11},{10,... | collective-permute-start | bytes 393224 | tf_op jit(solution)/shard_map/ppermute | solution.py:453
  18.3 39.2 %copy-start = (f32[4,4,8,256]{3,2,1,0:T(8,128)}, f32[4,4,8,256]{3,2,1,0:T(8,128)S(1)}, u32[]{:S(2)}) copy-start(f32[4,4,8,256]{3,2,1,0:T(8,128)S(1)} %pad_maximum_fusion.1.refs_0_.refs_8_) | copy-start | bytes 393220
  18.3 6.2 %collective-permute-start.8 = (f32[4,4,8,256]{3,2,1,0:T(8,128)S(1)}, f32[4,4,8,256]{3,2,1,0:T(8,128)S(1)}, u32[]{:S(2)}, u32[]{:S(2)}) collective-permute-start(f32[4,4,8,256]{3,2,1,0:T(8,128)S(1)} %pad_maximum_fusion.1.refs_0_.refs_8_), channel_id=1, source_target_pairs={{0,17},{1,16},{2,19},{3,18},{4,21},{5,20},{6,23},{7,22},{8,25},{9,... | collective-permute-start | bytes 393224 | tf_op jit(solution)/shard_map/ppermute | solution.py:459
  20.8 5.0 %collective-permute-start.7 = (f32[4,4,8,256]{3,2,1,0:T(8,128)S(1)}, f32[4,4,8,256]{3,2,1,0:T(8,128)S(1)}, u32[]{:S(2)}, u32[]{:S(2)}) collective-permute-start(f32[4,4,8,256]{3,2,1,0:T(8,128)S(1)} %pad_maximum_fusion.1.refs_0_.refs_8_), channel_id=1, source_target_pairs={{0,16},{8,24},{16,0},{24,8},{1,17},{9,25},{17,1},{25,9},{2,18},{10... | collective-permute-start | bytes 393224 | tf_op jit(solution)/shard_map/ppermute | solution.py:455
  21.3 5.0 %collective-permute-start.6 = (f32[4,4,8,256]{3,2,1,0:T(8,128)S(1)}, f32[4,4,8,256]{3,2,1,0:T(8,128)S(1)}, u32[]{:S(2)}, u32[]{:S(2)}) collective-permute-start(f32[4,4,8,256]{3,2,1,0:T(8,128)S(1)} %pad_maximum_fusion.1.refs_0_.refs_8_), channel_id=1, source_target_pairs={{0,1},{1,0},{2,3},{3,2},{4,5},{5,4},{6,7},{7,6},{8,9},{9,8},{10,11... | collective-permute-start | bytes 393224 | tf_op jit(solution)/shard_map/ppermute | solution.py:453
  24.4 33.0 %copy-start.9 = (f32[4,16,8,256]{3,2,1,0:T(8,128)}, f32[4,16,8,256]{3,2,1,0:T(8,128)S(1)}, u32[]{:S(2)}) copy-start(f32[4,16,8,256]{3,2,1,0:T(8,128)S(1)} %pad_maximum_fusion.refs_0_) | copy-start | bytes 1572868
  24.5 33.0 %copy-start.1 = (f32[4,4,8,256]{3,2,1,0:T(8,128)}, f32[4,4,8,256]{3,2,1,0:T(8,128)S(1)}, u32[]{:S(2)}) copy-start(f32[4,4,8,256]{3,2,1,0:T(8,128)S(1)} %collective-permute-done.8.refs_5_.refs_13_) | copy-start | bytes 393220
  25.8 31.7 %copy-start.2 = (f32[4,4,8,256]{3,2,1,0:T(8,128)}, f32[4,4,8,256]{3,2,1,0:T(8,128)S(1)}, u32[]{:S(2)}) copy-start(f32[4,4,8,256]{3,2,1,0:T(8,128)S(1)} %collective-permute-done.7.refs_4_.refs_12_) | copy-start | bytes 393220
  26.3 31.2 %copy-start.3 = (f32[4,4,8,256]{3,2,1,0:T(8,128)}, f32[4,4,8,256]{3,2,1,0:T(8,128)S(1)}, u32[]{:S(2)}) copy-start(f32[4,4,8,256]{3,2,1,0:T(8,128)S(1)} %collective-permute-done.6.refs_1_.refs_9_) | copy-start | bytes 393220
  26.3 22.4 %collective-permute-start.11 = (f32[4,16,8,256]{3,2,1,0:T(8,128)S(1)}, f32[4,16,8,256]{3,2,1,0:T(8,128)S(1)}, u32[]{:S(2)}, u32[]{:S(2)}) collective-permute-start(f32[4,16,8,256]{3,2,1,0:T(8,128)S(1)} %pad_maximum_fusion.refs_0_), channel_id=1, source_target_pairs={{0,17},{1,16},{2,19},{3,18},{4,21},{5,20},{6,23},{7,22},{8,25},{9,... | collective-permute-start | bytes 1572872 | tf_op jit(solution)/shard_map/ppermute | solution.py:459
  27.8 21.9 %collective-permute-start.10 = (f32[4,16,8,256]{3,2,1,0:T(8,128)S(1)}, f32[4,16,8,256]{3,2,1,0:T(8,128)S(1)}, u32[]{:S(2)}, u32[]{:S(2)}) collective-permute-start(f32[4,16,8,256]{3,2,1,0:T(8,128)S(1)} %pad_maximum_fusion.refs_0_), channel_id=1, source_target_pairs={{0,16},{8,24},{16,0},{24,8},{1,17},{9,25},{17,1},{25,9},{2,18},{10... | collective-permute-start | bytes 1572872 | tf_op jit(solution)/shard_map/ppermute | solution.py:455
  28.7 21.0 %collective-permute-start.9 = (f32[4,16,8,256]{3,2,1,0:T(8,128)S(1)}, f32[4,16,8,256]{3,2,1,0:T(8,128)S(1)}, u32[]{:S(2)}, u32[]{:S(2)}) collective-permute-start(f32[4,16,8,256]{3,2,1,0:T(8,128)S(1)} %pad_maximum_fusion.refs_0_), channel_id=1, source_target_pairs={{0,1},{1,0},{2,3},{3,2},{4,5},{5,4},{6,7},{7,6},{8,9},{9,8},{10,11... | collective-permute-start | bytes 1572872 | tf_op jit(solution)/shard_map/ppermute | solution.py:453
  29.8 1.3 %collective-permute-start.12 = (f32[4,4,8,256]{3,2,1,0:T(8,128)S(1)}, f32[4,4,8,256]{3,2,1,0:T(8,128)S(1)}, u32[]{:S(2)}, u32[]{:S(2)}) collective-permute-start(f32[4,4,8,256]{3,2,1,0:T(8,128)S(1)} %pad_maximum_fusion.1.refs_0_.refs_8_), channel_id=1, source_target_pairs={{0,8},{8,0},{16,24},{24,16},{1,9},{9,1},{17,25},{25,17},{2,10},{10... | collective-permute-start | bytes 393224 | tf_op jit(solution)/shard_map/ppermute | solution.py:455
  29.8 1.5 %collective-permute-start.13 = (f32[4,4,8,256]{3,2,1,0:T(8,128)S(1)}, f32[4,4,8,256]{3,2,1,0:T(8,128)S(1)}, u32[]{:S(2)}, u32[]{:S(2)}) collective-permute-start(f32[4,4,8,256]{3,2,1,0:T(8,128)S(1)} %collective-permute-done.6.refs_1_.refs_9_), channel_id=1, source_target_pairs={{0,8},{8,0},{16,24},{24,16},{1,9},{9,1},{17,25},{25,17},{2,10},{10... | collective-permute-start | bytes 393224 | tf_op jit(solution)/shard_map/ppermute | solution.py:455
  31.1 26.4 %copy-start.4 = (f32[4,4,8,256]{3,2,1,0:T(8,128)}, f32[4,4,8,256]{3,2,1,0:T(8,128)S(1)}, u32[]{:S(2)}) copy-start(f32[4,4,8,256]{3,2,1,0:T(8,128)S(1)} %collective-permute-done.12.refs_2_.refs_10_) | copy-start | bytes 393220
  31.1 1.3 %collective-permute-start.14 = (f32[4,4,8,256]{3,2,1,0:T(8,128)S(1)}, f32[4,4,8,256]{3,2,1,0:T(8,128)S(1)}, u32[]{:S(2)}, u32[]{:S(2)}) collective-permute-start(f32[4,4,8,256]{3,2,1,0:T(8,128)S(1)} %collective-permute-done.7.refs_4_.refs_12_), channel_id=1, source_target_pairs={{0,8},{8,0},{16,24},{24,16},{1,9},{9,1},{17,25},{25,17},{2,10},{10... | collective-permute-start | bytes 393224 | tf_op jit(solution)/shard_map/ppermute | solution.py:455
  31.3 26.2 %copy-start.5 = (f32[4,4,8,256]{3,2,1,0:T(8,128)}, f32[4,4,8,256]{3,2,1,0:T(8,128)S(1)}, u32[]{:S(2)}) copy-start(f32[4,4,8,256]{3,2,1,0:T(8,128)S(1)} %collective-permute-done.13.refs_3_.refs_11_) | copy-start | bytes 393220
  31.3 1.3 %collective-permute-start.15 = (f32[4,4,8,256]{3,2,1,0:T(8,128)S(1)}, f32[4,4,8,256]{3,2,1,0:T(8,128)S(1)}, u32[]{:S(2)}, u32[]{:S(2)}) collective-permute-start(f32[4,4,8,256]{3,2,1,0:T(8,128)S(1)} %collective-permute-done.8.refs_5_.refs_13_), channel_id=1, source_target_pairs={{0,8},{8,0},{16,24},{24,16},{1,9},{9,1},{17,25},{25,17},{2,10},{10... | collective-permute-start | bytes 393224 | tf_op jit(solution)/shard_map/ppermute | solution.py:455
  32.5 25.0 %copy-start.6 = (f32[4,4,8,256]{3,2,1,0:T(8,128)}, f32[4,4,8,256]{3,2,1,0:T(8,128)S(1)}, u32[]{:S(2)}) copy-start(f32[4,4,8,256]{3,2,1,0:T(8,128)S(1)} %collective-permute-done.14.refs_6_.refs_14_) | copy-start | bytes 393220
  32.7 24.8 %copy-start.7 = (f32[4,4,8,256]{3,2,1,0:T(8,128)}, f32[4,4,8,256]{3,2,1,0:T(8,128)S(1)}, u32[]{:S(2)}) copy-start(f32[4,4,8,256]{3,2,1,0:T(8,128)S(1)} %collective-permute-done.15.refs_7_.refs_15_) | copy-start | bytes 393220
  48.1 0.6 copy-start.8
  48.7 8.8 %copy-start.10 = (f32[4,16,8,256]{3,2,1,0:T(8,128)}, f32[4,16,8,256]{3,2,1,0:T(8,128)S(1)}, u32[]{:S(2)}) copy-start(f32[4,16,8,256]{3,2,1,0:T(8,128)S(1)} %collective-permute-done.11.refs_5_) | copy-start | bytes 1572868
  49.7 7.8 %copy-start.11 = (f32[4,16,8,256]{3,2,1,0:T(8,128)}, f32[4,16,8,256]{3,2,1,0:T(8,128)S(1)}, u32[]{:S(2)}) copy-start(f32[4,16,8,256]{3,2,1,0:T(8,128)S(1)} %collective-permute-done.10.refs_4_) | copy-start | bytes 1572868
  49.7 7.8 %copy-start.12 = (f32[4,16,8,256]{3,2,1,0:T(8,128)}, f32[4,16,8,256]{3,2,1,0:T(8,128)S(1)}, u32[]{:S(2)}) copy-start(f32[4,16,8,256]{3,2,1,0:T(8,128)S(1)} %collective-permute-done.9.refs_1_) | copy-start | bytes 1572868
  49.7 5.5 %collective-permute-start.16 = (f32[4,16,8,256]{3,2,1,0:T(8,128)S(1)}, f32[4,16,8,256]{3,2,1,0:T(8,128)S(1)}, u32[]{:S(2)}, u32[]{:S(2)}) collective-permute-start(f32[4,16,8,256]{3,2,1,0:T(8,128)S(1)} %pad_maximum_fusion.refs_0_), channel_id=1, source_target_pairs={{0,8},{8,0},{16,24},{24,16},{1,9},{9,1},{17,25},{25,17},{2,10},{10... | collective-permute-start | bytes 1572872 | tf_op jit(solution)/shard_map/ppermute | solution.py:455
  53.7 2.3 %collective-permute-start.17 = (f32[4,16,8,256]{3,2,1,0:T(8,128)S(1)}, f32[4,16,8,256]{3,2,1,0:T(8,128)S(1)}, u32[]{:S(2)}, u32[]{:S(2)}) collective-permute-start(f32[4,16,8,256]{3,2,1,0:T(8,128)S(1)} %collective-permute-done.9.refs_1_), channel_id=1, source_target_pairs={{0,8},{8,0},{16,24},{24,16},{1,9},{9,1},{17,25},{25,17},{2,10},{10... | collective-permute-start | bytes 1572872 | tf_op jit(solution)/shard_map/ppermute | solution.py:455
  53.7 3.0 %collective-permute-start.18 = (f32[4,16,8,256]{3,2,1,0:T(8,128)S(1)}, f32[4,16,8,256]{3,2,1,0:T(8,128)S(1)}, u32[]{:S(2)}, u32[]{:S(2)}) collective-permute-start(f32[4,16,8,256]{3,2,1,0:T(8,128)S(1)} %collective-permute-done.10.refs_4_), channel_id=1, source_target_pairs={{0,8},{8,0},{16,24},{24,16},{1,9},{9,1},{17,25},{25,17},{2,10},{10... | collective-permute-start | bytes 1572872 | tf_op jit(solution)/shard_map/ppermute | solution.py:455
  54.2 3.3 %collective-permute-start.19 = (f32[4,16,8,256]{3,2,1,0:T(8,128)S(1)}, f32[4,16,8,256]{3,2,1,0:T(8,128)S(1)}, u32[]{:S(2)}, u32[]{:S(2)}) collective-permute-start(f32[4,16,8,256]{3,2,1,0:T(8,128)S(1)} %collective-permute-done.11.refs_5_), channel_id=1, source_target_pairs={{0,8},{8,0},{16,24},{24,16},{1,9},{9,1},{17,25},{25,17},{2,10},{10... | collective-permute-start | bytes 1572872 | tf_op jit(solution)/shard_map/ppermute | solution.py:455
  55.2 2.3 %copy-start.13 = (f32[4,16,8,256]{3,2,1,0:T(8,128)}, f32[4,16,8,256]{3,2,1,0:T(8,128)S(1)}, u32[]{:S(2)}) copy-start(f32[4,16,8,256]{3,2,1,0:T(8,128)S(1)} %collective-permute-done.16.refs_2_) | copy-start | bytes 1572868
  56.0 1.6 %copy-start.14 = (f32[4,16,8,256]{3,2,1,0:T(8,128)}, f32[4,16,8,256]{3,2,1,0:T(8,128)S(1)}, u32[]{:S(2)}) copy-start(f32[4,16,8,256]{3,2,1,0:T(8,128)S(1)} %collective-permute-done.17.refs_3_) | copy-start | bytes 1572868
  56.7 0.9 copy-start.15
  57.6 0.8 copy-start.16

commit v2 on v1

--- a/solution.py
+++ b/solution.py
@@ -12,20 +12,19 @@
 LANES = 128
 CHUNK = 256
 GROUP = 8
-UNROLL = 4
 
 support = 0.5
 ridge_shift = 1.0
 
-SHIFT, VV, VW, QQ, QW, WW, QS, CROSS, WX = range(9)
+SHIFT, QQ, QW, WW, QS, CROSS, WX = range(7)
 HALF = 64
 
 
-def pack_kernel(per_device, place_ref, values_ref, points_ref, lists_ref, blocks_ref, out_ref):
-    row_base = place_ref[0]
-    col_id = place_ref[1]
-    col_count = place_ref[2]
-    x_step = place_ref[3]
+def pack_kernel(per_device, values_ref, points_ref, lists_ref, blocks_ref, out_ref):
+    row_base = lax.axis_index("row")
+    col_id = lax.axis_index("col")
+    col_count = lax.axis_size("col")
+    x_step = col_count // 2
     for b in range(per_device):
         for half in range(2):
             blocks_ref[2 * b + half] = values_ref[8 * half : 8 * half + 8, b * BLK : (b + 1) * BLK]
@@ -122,10 +121,22 @@
     return [cloud[device, axis, pl.ds(line, 1), :] for axis in range(3)]
 
 
-def entry(lists, k):
+def entry(lists, kind, k):
     chunk = lax.shift_right_logical(k, CHUNK.bit_length() - 1)
-    lane = k & (CHUNK - 1)
-    return lists[chunk, 0, lane], lists[chunk, 1, lane]
+    chunk = kind * (lists.shape[0] // 2) + jnp.minimum(chunk, lists.shape[0] // 2 - 1)
+    code = lists[chunk, 0, k & (CHUNK - 1)]
+    return code & 0xFFFF, lax.shift_right_logical(code, 16)
+
+
+def sizes(lists, cap):
+    found = []
+    base = 0
+    for kind in range(2):
+        n = lists[kind * (lists.shape[0] // 2), 1, 0]
+        held = jnp.minimum(n, jnp.maximum(cap - base, 0))
+        found.append((n, held, base))
+        base = base + held
+    return found, lists[0, 1, 1]
 
 
 def gather(refs, target, sems):
@@ -133,9 +144,9 @@
     return [pltpu.make_async_copy(ref, target.at[pl.ds(p * run, run)], sems.at[p]) for p, ref in enumerate(refs)]
 
 
-def tiles_kernel(pieces, per_device, cap, me_ref, *refs):
+def tiles_kernel(pieces, per_device, cap, *refs):
     list_ref, tile_ref = refs[pieces : pieces + 2]
-    cloud, stage, plan, lists, sems, list_sem = refs[pieces + 2 :]
+    cloud, stage, plan, lists, sems, list_sems = refs[pieces + 2 :]
     devices = cloud.shape[0]
     blocks = devices * per_device
     copies = gather(refs[:pieces], cloud, sems)
@@ -144,7 +155,10 @@
     for copy in copies:
         copy.wait()
 
-    mine = me_ref[0] * per_device
+    cols = lax.axis_size("col")
+    col_id = lax.axis_index("col")
+    mine = lax.axis_index("row") * cols + (col_id & 1) * (cols // 2) + lax.shift_right_logical(col_id, 1)
+    mine = mine * per_device
     ids = lax.broadcasted_iota(jnp.int32, (blocks, LANES), 0)
     batch = 8
 
@@ -182,71 +196,83 @@
 
     listed = stage[...] > 0.0
     rows = lax.broadcasted_iota(jnp.int32, (blocks, blocks), 0)
-    cols = lax.broadcasted_iota(jnp.int32, (blocks, blocks), 1)
+    columns = lax.broadcasted_iota(jnp.int32, (blocks, blocks), 1)
     near_row = jnp.max(stage[0:per_device, :], axis=0, keepdims=True) > 0.0
     near_row = near_row | (lax.broadcasted_iota(jnp.int32, (1, blocks), 1) < per_device)
     near_col = jnp.max(stage[:, 0:per_device], axis=1, keepdims=True) > 0.0
     near_col = near_col | (lax.broadcasted_iota(jnp.int32, (blocks, 1), 0) < per_device)
-    near = jnp.where(near_row, 1.0, 0.0) + jnp.where(near_col, 1.0, 0.0)
-    used = jnp.where(listed & (rows >= cols) & (near > 0.0), 1.0, 0.0)
 
     def counted(left, right):
         return jnp.dot(left.astype(jnp.bfloat16), right.astype(jnp.bfloat16), preferred_element_type=jnp.float32)
 
-    rank = counted(jnp.where(rows >= cols, 1.0, 0.0), used)
-    count = jnp.broadcast_to(rank[blocks - 1 : blocks, :], (8, blocks))
-    start = jnp.sum(counted(used, jnp.where(rows < cols, 1.0, 0.0)), axis=0, keepdims=True)
-    start = jnp.broadcast_to(start, (8, blocks))
-    n = jnp.sum(count[0:1, :]).astype(jnp.int32)
-    own = lax.broadcasted_iota(jnp.int32, (1, blocks), 1) < per_device
-    n_own = jnp.sum(jnp.where(own, count[0:1, :], 0.0)).astype(jnp.int32)
-    start_col = jnp.transpose(start)[:, 0:1]
-    stop_col = start_col + jnp.transpose(count)[:, 0:1]
-    stage[...] = rank * used
-    index_col = lax.broadcasted_iota(jnp.int32, (blocks, CHUNK), 0).astype(jnp.float32)
-
-    def write_list(chunk, carry):
-        place = lax.broadcasted_iota(jnp.int32, (1, CHUNK), 1).astype(jnp.float32) + (chunk * CHUNK).astype(jnp.float32)
-        pick = jnp.where((start_col <= place) & (place < stop_col), 1.0, 0.0)
-        low_index = jnp.sum(pick * index_col, axis=0, keepdims=True)
-        begin = jnp.sum(pick * start_col, axis=0, keepdims=True)
-        high, low = split(stage[...])
-        ranks = counted(high, pick) + counted(low, pick)
-        match = jnp.where(ranks == place - begin + 1.0, 1.0, 0.0)
-        high_index = jnp.sum(match * index_col, axis=0, keepdims=True)
-        both = jnp.concatenate([low_index, high_index], axis=0).astype(jnp.int32)
-        sizes = jnp.concatenate(
-            [jnp.full((1, CHUNK), n, jnp.int32), jnp.full((1, CHUNK), n_own, jnp.int32)], axis=0
-        )
-        plan[...] = jnp.concatenate([both, sizes, jnp.zeros((4, CHUNK), jnp.int32)], axis=0)
-        list_ref[chunk] = plan[...]
-        copy = pltpu.make_async_copy(plan, lists.at[chunk], list_sem)
-        copy.start()
-        copy.wait()
-        return carry
-
-    lax.fori_loop(0, jnp.maximum((n + CHUNK - 1) // CHUNK, 1), write_list, 0)
-
-    held = jnp.minimum(n, cap)
-
-    def write_tiles(form, step):
-        def body(k, carry):
-            for part in range(step):
-                i, j = entry(lists, k * step + part)
-                form(
-                    point_rows(cloud, i, per_device), point_rows(cloud, j, per_device), tile_ref.at[k * step + part]
-                )
+    low_ids = lax.broadcasted_iota(jnp.int32, (blocks, CHUNK), 0).astype(jnp.float32)
+    lower = jnp.where(rows >= columns, 1.0, 0.0)
+    upper = jnp.where(rows < columns, 1.0, 0.0)
+
+    def write_list(kind, used):
+        rank = counted(lower, used)
+        count = rank[blocks - 1 : blocks, :]
+        start = jnp.sum(counted(used, upper), axis=0, keepdims=True)
+        both = jnp.concatenate([start, start + count, jnp.zeros((6, blocks), jnp.float32)], axis=0)
+        both = jnp.transpose(both)
+        start_col = both[:, 0:1]
+        stop_col = both[:, 1:2]
+        n = jnp.sum(count).astype(jnp.int32)
+        own = lax.broadcasted_iota(jnp.int32, (1, blocks), 1) < per_device
+        n_own = jnp.sum(jnp.where(own, count, 0.0)).astype(jnp.int32)
+        stage[...] = rank * used
+        lane = lax.broadcasted_iota(jnp.int32, (1, CHUNK), 1)
+        totals = jnp.where(lane == 0, n, n_own)
+        first = kind * (list_ref.shape[0] // 2)
+
+        def write(chunk, carry):
+            place = lane.astype(jnp.float32) + (chunk * CHUNK).astype(jnp.float32)
+            pick = jnp.where((start_col <= place) & (place < stop_col), 1.0, 0.0)
+            column = jnp.sum(pick * low_ids, axis=0, keepdims=True)
+            begin = jnp.sum(pick * start_col, axis=0, keepdims=True)
+            high, low = split(stage[...])
+            ranks = counted(high, pick) + counted(low, pick)
+            match = jnp.where(ranks == place - begin + 1.0, 1.0, 0.0)
+            row = jnp.sum(match * low_ids, axis=0, keepdims=True)
+            code = row.astype(jnp.int32) * 65536 + column.astype(jnp.int32)
+            plan[...] = jnp.concatenate([code, totals], axis=0)
+            copies = [
+                pltpu.make_async_copy(plan, lists.at[first + chunk], list_sems.at[0]),
+                pltpu.make_async_copy(plan, list_ref.at[first + chunk], list_sems.at[1]),
+            ]
+            for copy in copies:
+                copy.start()
+            for copy in copies:
+                copy.wait()
             return carry
 
-        lax.fori_loop(0, (held + step - 1) // step, body, 0)
+        lax.fori_loop(0, jnp.maximum((n + CHUNK - 1) // CHUNK, 1), write, 0)
+
+    write_list(0, jnp.where(listed & (rows >= columns) & near_row & near_col, 1.0, 0.0))
+    write_list(1, jnp.where(listed & near_row & jnp.logical_not(near_col), 1.0, 0.0))
+    kinds, _ = sizes(lists, cap)
+
+    first_held = kinds[0][1]
+    held = first_held + kinds[1][1]
+
+    def write_tiles(form):
+        def body(group, carry):
+            for part in range(GROUP):
+                slot = group * GROUP + part
+                kind = (slot >= first_held).astype(jnp.int32)
+                i, j = entry(lists, kind, slot - kind * first_held)
+                form(point_rows(cloud, i, per_device), point_rows(cloud, j, per_device), tile_ref.at[slot])
+            return carry
+
+        lax.fori_loop(0, (held + GROUP - 1) // GROUP, body, 0)
 
     @pl.when(extent <= 1.5 / support)
     def _():
-        write_tiles(evaluate_flat, UNROLL)
+        write_tiles(evaluate_flat)
 
     @pl.when(extent > 1.5 / support)
     def _():
-        write_tiles(evaluate, 2)
+        write_tiles(evaluate)
 
 
 def apply_kernel(pieces, point_pieces, per_device, cap, lists, tile_ref, *refs):
@@ -258,9 +284,7 @@
     blocks = devices * per_device
     block_shift = per_device.bit_length() - 1
     low_mask = per_device - 1
-    n = lists[0, 2, 0]
-    n_own = lists[0, 3, 0]
-    held = jnp.minimum(n, cap)
+    kinds, n_own = sizes(lists, cap)
     fills = gather(value_refs, field, sems)
     for copy in fills:
         copy.start()
@@ -287,83 +311,78 @@
         device, span = at(b)
         ref[device, span] += value
 
-    def evaluate_late(k):
-        i, j = entry(lists, k)
-        evaluate(point_rows(cloud, i, per_device), point_rows(cloud, j, per_device), late)
-        return i, j
-
     def image(b):
         return load(total, b) + load(field, b)
 
-    def first_group(group, carry):
-        pending = []
-        for u in range(GROUP):
-            k = group * GROUP + u
-            i, j = entry(lists, k)
-            live = k < held
-            pending.append((jnp.where(live, i, blocks), product(load(field, j), tile_ref.at[k], 0)))
-            pending.append((jnp.where(live & (i != j), j, blocks), product(load(field, i), tile_ref.at[k], 1)))
-        for b, value in pending:
-            add(total, b, value)
-        return carry
-
-    lax.fori_loop(0, (held + GROUP - 1) // GROUP, first_group, 0)
-
-    @pl.when(n > cap)
+    def run(kind, held, source, target, spare, back):
+        base = kinds[kind][2]
+
+        def body(group, carry):
+            def forward(u):
+                k = group * GROUP + u
+                i, j = entry(lists, kind, k)
+                return jnp.where(k < held, i, spare), product(source(j), tile_ref.at[base + k], 0)
+
+            def reverse(u):
+                k = group * GROUP + u
+                i, j = entry(lists, kind, k)
+                wanted = (k < held) & (i != j) & (j < spare)
+                return jnp.where(wanted, j, spare), product(source(i), tile_ref.at[base + k], 1)
+
+            if back == "always":
+                pending = [form(u) for u in range(GROUP) for form in (forward, reverse)]
+            else:
+                pending = [forward(u) for u in range(GROUP)]
+            for b, value in pending:
+                add(target, b, value)
+            if back == "some":
+                for u in range(GROUP):
+                    k = group * GROUP + u
+                    i, j = entry(lists, kind, k)
+
+                    @pl.when((k < held) & (i != j) & (j < spare))
+                    def _():
+                        add(target, j, product(source(i), tile_ref.at[base + k], 1))
+
+            return carry
+
+        lax.fori_loop(0, (held + GROUP - 1) // GROUP, body, 0)
+
+    def run_late(kind, first, last, source, target, spare):
+        def body(k, carry):
+            i, j = entry(lists, kind, k)
+            evaluate(point_rows(cloud, i, per_device), point_rows(cloud, j, per_device), late)
+            add(target, i, product(source(j), late, 0))
+            if kind == 0:
+
+                @pl.when((i != j) & (j < spare))
+                def _():
+                    add(target, j, product(source(i), late, 1))
+
+            return carry
+
+        lax.fori_loop(first, last, body, 0)
+
+    def own_field(b):
+        return load(field, b)
+
+    run(0, kinds[0][1], own_field, total, blocks, "always")
+    run(1, kinds[1][1], own_field, total, blocks, "never")
+
+    @pl.when((kinds[0][0] > kinds[0][1]) | (kinds[1][0] > kinds[1][1]))
     def _():
         copies = gather(point_refs, cloud, point_sems)
         for copy in copies:
             copy.start()
         for copy in copies:
             copy.wait()
-
-        def first_late(k, carry):
-            i, j = evaluate_late(k)
-            add(total, i, product(load(field, j), late, 0))
-
-            @pl.when(i != j)
-            def _():
-                add(total, j, product(load(field, i), late, 1))
-
-            return carry
-
-        lax.fori_loop(cap, n, first_late, 0)
+        for kind, (n, held, _) in enumerate(kinds):
+            run_late(kind, held, n, own_field, total, blocks)
 
     second[0] = total[0] + field[0]
-    held_own = jnp.minimum(n_own, cap)
-
-    def second_group(group, carry):
-        pending = []
-        for u in range(GROUP):
-            k = group * GROUP + u
-            i, j = entry(lists, k)
-            live = k < held_own
-            pending.append((jnp.where(live, i, per_device), product(image(j), tile_ref.at[k], 0)))
-        for b, value in pending:
-            add(second, b, value)
-        for u in range(GROUP):
-            k = group * GROUP + u
-            i, j = entry(lists, k)
-
-            @pl.when((k < held_own) & (i != j) & (j < per_device))
-            def _():
-                add(second, j, product(image(i), tile_ref.at[k], 1))
-
-        return carry
-
-    lax.fori_loop(0, (held_own + GROUP - 1) // GROUP, second_group, 0)
-
-    def second_late(k, carry):
-        i, j = evaluate_late(k)
-        add(second, i, product(image(j), late, 0))
-
-        @pl.when((i != j) & (j < per_device))
-        def _():
-            add(second, j, product(image(i), late, 1))
-
-        return carry
-
-    lax.fori_loop(cap, n_own, second_late, 0)
+    held_own = jnp.minimum(n_own, kinds[0][1])
+    run(0, held_own, image, second, per_device, "some")
+    run_late(0, held_own, n_own, image, second, per_device)
 
     v = field[0].reshape(per_device, 16, BLK)
     w = (total[0] + field[0]).reshape(per_device, 16, BLK)
@@ -379,42 +398,44 @@
     shift = jnp.where(vw != 0.0, vv / jnp.where(vw != 0.0, vw, 1.0), 0.0)
     q = v - shift[None] * w
     s = w - shift[None] * x
-    sums = [shift, vv, vw, over(q * q), over(q * w), over(w * w), over(q * s), over(w * s + q * x), over(w * x)]
-    lane = lax.broadcasted_iota(jnp.int32, (8, LANES), 1)
-    sent = jnp.zeros((8, LANES), jnp.float32)
+    sums = [shift, over(q * q), over(q * w), over(w * w), over(q * s), over(w * s + q * x), over(w * x)]
+    lane = lax.broadcasted_iota(jnp.int32, (16, LANES), 1)
+    sent = jnp.zeros((16, LANES), jnp.float32)
     for m, value in enumerate(sums):
-        for half in range(2):
-            sent = jnp.where(lane == half * HALF + m, value[8 * half : 8 * half + 8], sent)
+        sent = jnp.where(lane == m, value, sent)
+    sent = jnp.concatenate([sent, jnp.zeros((LANES - 16, LANES), jnp.float32)], axis=0)
+    sent = jnp.transpose(sent)[0:8]
     for device in range(devices):
         moment_ref[device] = sent
 
 
 def finish_kernel(per_device, moment_ref, values_ref, w_ref, x_ref, solution_ref, residual_ref):
-    moments = moment_ref[...]
-
+    def take(m):
+        return moment_ref[:, m, :]
+
+    def whole(values):
+        return jnp.sum(values, axis=0, keepdims=True)
+
+    shift, qq, qw, ww = take(SHIFT), take(QQ), take(QW), take(WW)
+    rr = whole(qq + 2.0 * shift * qw + shift * shift * ww)
+    vw = whole(qw + shift * ww)
+    alpha = rr / vw
+    delta = alpha - shift
+    fresh = whole(qq - 2.0 * delta * qw + delta * delta * ww)
+    mixed = whole(qw - delta * ww)
+    curve = whole(take(QS) - delta * take(CROSS) + delta * delta * take(WX))
+    beta = fresh / rr
+    curve = curve + 2.0 * beta * mixed + beta * beta * vw
+    again = fresh / curve
+    steps = jnp.transpose(jnp.concatenate([alpha, beta, again, jnp.zeros((5, LANES), jnp.float32)], axis=0))
     for half in range(2):
-
-        def take(m):
-            return moments[:, :, half * HALF + m : half * HALF + m + 1]
-
-        def whole(values):
-            return jnp.sum(values, axis=0)
-
-        rr = whole(take(VV))
-        vw = whole(take(VW))
-        alpha = rr / vw
-        delta = alpha[None] - take(SHIFT)
-        fresh = whole(take(QQ) - 2.0 * delta * take(QW) + delta * delta * take(WW))
-        mixed = whole(take(QW) - delta * take(WW))
-        curve = whole(take(QS) - delta * take(CROSS) + delta * delta * take(WX))
-        beta = fresh / rr
-        curve = curve + 2.0 * beta * mixed + beta * beta * vw
-        again = fresh / curve
+        lines = slice(8 * half, 8 * half + 8)
+        alpha, beta, again = (steps[lines, m : m + 1] for m in range(3))
         for b in range(per_device):
-            at = (slice(8 * half, 8 * half + 8), slice(b * BLK, (b + 1) * BLK))
+            at = (lines, slice(b * BLK, (b + 1) * BLK))
             v = values_ref[at]
-            w = w_ref[b, 8 * half : 8 * half + 8, :]
-            x = x_ref[b, 8 * half : 8 * half + 8, :]
+            w = w_ref[b, lines, :]
+            x = x_ref[b, lines, :]
             r = v - alpha * w
             d = r + beta * v
             solution_ref[at] = alpha * v + again * d
@@ -427,8 +448,6 @@
     rows = lax.axis_size("row")
     cols = lax.axis_size("col")
     devices = rows * cols
-    row_id = lax.axis_index("row")
-    col_id = lax.axis_index("col")
     depth = cols // 2
     vmem = pl.BlockSpec(memory_space=pltpu.VMEM)
     smem = pl.BlockSpec(memory_space=pltpu.SMEM)
@@ -436,17 +455,16 @@
     height = 2 * per_device
     blocks = devices * per_device
 
-    place = jnp.stack([row_id, col_id, jnp.int32(cols), jnp.int32(depth)]).astype(jnp.int32)
     own_values, own_points = pl.pallas_call(
         functools.partial(pack_kernel, per_device),
         out_shape=(
             jax.ShapeDtypeStruct((height, 8, BLK), jnp.float32),
             jax.ShapeDtypeStruct((4, per_device, BLK), jnp.float32),
         ),
-        in_specs=[smem, vmem, vmem, vmem],
+        in_specs=[vmem, vmem, vmem],
         out_specs=(vmem, vmem),
         name="pack",
-    )(place, values, points, tile_lists)
+    )(values, points, tile_lists)
 
     def swap(array, row_mask, col_mask):
         if row_mask == 0:
@@ -478,33 +496,34 @@
     point_parts = pairs(point_plane)
     value_plane = across(value_line)
 
-    me = row_id * cols + (col_id & 1) * depth + lax.shift_right_logical(col_id, 1)
     chunks = (devices * tile_lists.shape[1] + CHUNK - 1) // CHUNK
     tile_bytes = 4 * BLK * BLK
     cloud_bytes = devices * 4 * per_device * BLK * 4
-    tiles_limit = cloud_bytes + 6 * 4 * blocks * blocks + 12 * 2**20
-    apply_limit = cloud_bytes + 2 * blocks * fields * BLK * 4 + 10 * 2**20
-    cap = max(GROUP, min(152, (60 * 2**20 - max(tiles_limit, apply_limit)) // tile_bytes // GROUP * GROUP))
+    field_bytes = blocks * fields * BLK * 4
+    tiles_limit = cloud_bytes + 6 * 4 * blocks * blocks + 10 * 2**20
+    apply_limit = cloud_bytes + 2 * field_bytes + 6 * 2**20
+    room = 60 * 2**20 - max(tiles_limit, apply_limit)
+    cap = max(GROUP, min(120, room // tile_bytes // GROUP * GROUP))
     lists, tiles = pl.pallas_call(
         functools.partial(tiles_kernel, len(point_parts), per_device, cap),
         out_shape=(
-            jax.ShapeDtypeStruct((chunks, 8, CHUNK), jnp.int32),
+            pltpu.HBM((2 * chunks, 2, CHUNK), jnp.int32),
             pltpu.VMEM((cap, 2, BLK, BLK), jnp.bfloat16),
         ),
-        in_specs=[smem] + [anywhere] * len(point_parts),
-        out_specs=(vmem, vmem),
+        in_specs=[anywhere] * len(point_parts),
+        out_specs=(anywhere, vmem),
         scratch_shapes=[
             pltpu.VMEM((devices, 4, per_device, BLK), jnp.float32),
             pltpu.VMEM((blocks, blocks), jnp.float32),
-            pltpu.VMEM((8, CHUNK), jnp.int32),
-            pltpu.SMEM((chunks, 8, CHUNK), jnp.int32),
+            pltpu.VMEM((2, CHUNK), jnp.int32),
+            pltpu.SMEM((2 * chunks, 2, CHUNK), jnp.int32),
             pltpu.SemaphoreType.DMA((len(point_parts),)),
-            pltpu.SemaphoreType.DMA,
+            pltpu.SemaphoreType.DMA((2,)),
         ],
         compiler_params=pltpu.CompilerParams(vmem_limit_bytes=tiles_limit),
         cost_estimate=pl.CostEstimate(flops=10**9, bytes_accessed=30 * 2**20, transcendentals=10**7),
         name="tiles",
-    )(me.reshape(1).astype(jnp.int32), *point_parts)
+    )(*point_parts)
     value_plane, lists, tiles = lax.optimization_barrier((value_plane, lists, tiles))
     value_parts = pairs(value_plane)
     block_shape = jax.ShapeDtypeStruct((per_device, fields, BLK), jnp.float32)

time: 92.7 us -> 87.6 us (0.945)
  Pallas kernels: 35.3 us -> 27.5 us
  blocking collectives: 15.9 us -> 20.1 us
  waiting for transfers between devices: 14.2 us -> 17.6 us
  starting transfers between devices: 22.6 us -> 20 us
    pallas_call x1, Pallas kernels: 15.5 us -> 11 us  [local(): pl.pallas_call(functools.partial(apply_kernel, len(value_parts), len(poin...]
    all_to_all x1, blocking collectives: 15.9 us -> 20.1 us  [local(): moments = lax.all_to_all(moments, ('row', 'col'), 0, 0, tiled=False)]
    ppermute x10, waiting for transfers between devices: 7.4 us -> 10.8 us  [swap(): return lax.ppermute(array, 'row', [(i, i ^ row_mask) for i in range(rows)])]
    pallas_call x1, Pallas kernels: 15.4 us -> 12.7 us  [local(): pl.pallas_call(functools.partial(tiles_kernel, len(point_parts), per_devi...]
    ppermute x10, starting transfers between devices: 6.94 us -> 4.35 us  [swap(): return lax.ppermute(array, 'row', [(i, i ^ row_mask) for i in range(rows)])]
  transfers between devices with their start and end apart: 20 -> 20, of which waited for: 12 -> 12; matrix products, arithmetic and copies ran while one was open for 2% -> 2% of each run, Pallas kernels for 17% -> 14%
where the time goes in v2:
time: 87.6 us; the launch traced here: 88.2 us
  Pallas kernels  27.5 us (31%)
  blocking collectives  20.1 us (23%)
  starting transfers between devices  20 us (23%)
  waiting for transfers between devices  17.6 us (20%)
  other arithmetic  1.71 us (2%)
    all_to_all x1, blocking collectives, local(): moments = lax.all_to_all(moments, ('row', 'col'), 0, 0, tiled=False)  20.1 us
    pallas_call x1, Pallas kernels, local(): pl.pallas_call(functools.partial(tiles_kernel, len(point_parts), per_devi...  12.7 us
    ppermute x8, starting transfers between devices, swap(): return lax.ppermute(array, 'col', [(i, i ^ col_mask) for i in range(cols)])  11.6 us
    pallas_call x1, Pallas kernels, local(): pl.pallas_call(functools.partial(apply_kernel, len(value_parts), len(poin...  11 us
    ppermute x10, waiting for transfers between devices, swap(): return lax.ppermute(array, 'row', [(i, i ^ row_mask) for i in range(rows)])  10.8 us
    ppermute x8, waiting for transfers between devices, swap(): return lax.ppermute(array, 'col', [(i, i ^ col_mask) for i in range(cols)])  6.78 us
    ppermute x10, starting transfers between devices, swap(): return lax.ppermute(array, 'row', [(i, i ^ row_mask) for i in range(rows)])  4.35 us
    ppermute x2, starting transfers between devices, swap(): return lax.ppermute(array, ('row', 'col'), pairs)  4 us
  transfers between devices with their start and end apart: 20, of which 12 were waited for; matrix products, arithmetic and copies ran while one was open for 2% of the time, Pallas kernels for 14%

profile of v2, /device:TPU:0, one launch (start us, length us, event | category | flops | bytes accessed | tf_op | source)
XLA Modules:
  0.0 88.2 jit_solution(10363064308498171850)
XLA Ops:
  0.6 1.6 %pack.1 = (f32[16,8,256]{2,1,0:T(8,128)}, f32[4,8,256]{2,1,0:T(8,128)}) custom-call(f32[16,2048]{1,0:T(8,128)} %values_ref.3, f32[3,2048]{1,0:T(4,128)} %points_ref.1, s32[3,48]{1,0:T(4,128)} %lists_ref.1), custom_call_target="tpu_custom_call" | custom-call | tf_op jit(solution)/shard_map/pack/pallas_call | solution.py:458
  2.3 5.0 %collective-permute-start.5 = (f32[4,8,256]{2,1,0:T(8,128)}, f32[4,8,256]{2,1,0:T(8,128)S(1)}, u32[]{:S(2)}, u32[]{:S(2)}) collective-permute-start(f32[4,8,256]{2,1,0:T(8,128)} %get-tuple-element.21), channel_id=1, source_target_pairs={{0,6},{1,7},{2,4},{3,5},{4,2},{5,3},{6,0},{7,1},{8,14},{9,15},{10,... | collective-permute-start | bytes 98312 | tf_op jit(solution)/shard_map/ppermute | solution.py:471
  7.3 0.0 collective-permute-start.4
  7.3 0.6 collective-permute-start.3
  7.9 3.8 %collective-permute-start.2 = (f32[16,8,256]{2,1,0:T(8,128)}, f32[16,8,256]{2,1,0:T(8,128)S(1)}, u32[]{:S(2)}, u32[]{:S(2)}) collective-permute-start(f32[16,8,256]{2,1,0:T(8,128)} %get-tuple-element.20), channel_id=1, source_target_pairs={{0,6},{1,7},{2,4},{3,5},{4,2},{5,3},{6,0},{7,1},{8,14},{9,15},{10,... | collective-permute-start | bytes 393224 | tf_op jit(solution)/shard_map/ppermute | solution.py:471
  11.7 0.0 collective-permute-start.1
  11.7 0.0 collective-permute-done.5
  11.7 0.6 collective-permute-start
  12.3 4.6 %collective-permute-done.4 = f32[4,8,256]{2,1,0:T(8,128)S(1)} collective-permute-done((f32[4,8,256]{2,1,0:T(8,128)}, f32[4,8,256]{2,1,0:T(8,128)S(1)}, u32[]{:S(2)}, u32[]{:S(2)}) %collective-permute-start.4) | collective-permute-done | bytes 32800 | tf_op jit(solution)/shard_map/ppermute | solution.py:471
  16.9 0.0 collective-permute-done.3
  16.9 0.8 pad_maximum_fusion.1.refs_0_.refs_8_
  17.7 2.5 %collective-permute-start.8 = (f32[4,4,8,256]{3,2,1,0:T(8,128)S(1)}, f32[4,4,8,256]{3,2,1,0:T(8,128)S(1)}, u32[]{:S(2)}, u32[]{:S(2)}) collective-permute-start(f32[4,4,8,256]{3,2,1,0:T(8,128)S(1)} %pad_maximum_fusion.1.refs_0_.refs_8_), channel_id=1, source_target_pairs={{0,17},{1,16},{2,19},{3,18},{4,21},{5,20},{6,23},{7,22},{8,25},{9,... | collective-permute-start | bytes 393224 | tf_op jit(solution)/shard_map/ppermute | solution.py:477
  20.2 0.5 collective-permute-start.7
  20.7 0.0 collective-permute-done.2
  20.7 0.5 collective-permute-start.6
  21.2 1.7 %collective-permute-done.1 = f32[16,8,256]{2,1,0:T(8,128)S(1)} collective-permute-done((f32[16,8,256]{2,1,0:T(8,128)}, f32[16,8,256]{2,1,0:T(8,128)S(1)}, u32[]{:S(2)}, u32[]{:S(2)}) %collective-permute-start.1) | collective-permute-done | bytes 131104 | tf_op jit(solution)/shard_map/ppermute | solution.py:471
  22.9 0.0 collective-permute-done
  22.9 0.9 %pad_maximum_fusion.refs_0_ = f32[4,16,8,256]{3,2,1,0:T(8,128)S(1)} fusion(f32[1,16,8,256]{3,2,1,0:T(8,128)S(1)} %bitcast.9, f32[1,16,8,256]{3,2,1,0:T(8,128)S(1)} %bitcast.10, f32[1,16,8,256]{3,2,1,0:T(8,128)S(1)} %bitcast.11, f32[1,16,8,256]{3,2,1,0:T(8,128)} %bitcast.8), kind=kLoop, calls=%fused_computation | loop fusion | flops 393216 | bytes 1048576 | tf_op jit(solution)/shard_map/stack | solution.py:480
  23.8 0.0 collective-permute-done.8.refs_5_.refs_13_
  23.8 1.3 %collective-permute-done.7.refs_4_.refs_12_ = f32[4,4,8,256]{3,2,1,0:T(8,128)S(1)} collective-permute-done((f32[4,4,8,256]{3,2,1,0:T(8,128)S(1)}, f32[4,4,8,256]{3,2,1,0:T(8,128)S(1)}, u32[]{:S(2)}, u32[]{:S(2)}) %collective-permute-start.7) | collective-permute-done | bytes 131104 | tf_op jit(solution)/shard_map/ppermute | solution.py:473
  25.1 0.5 collective-permute-done.6.refs_1_.refs_9_
  25.7 1.5 %collective-permute-start.11 = (f32[4,16,8,256]{3,2,1,0:T(8,128)S(1)}, f32[4,16,8,256]{3,2,1,0:T(8,128)S(1)}, u32[]{:S(2)}, u32[]{:S(2)}) collective-permute-start(f32[4,16,8,256]{3,2,1,0:T(8,128)S(1)} %pad_maximum_fusion.refs_0_), channel_id=1, source_target_pairs={{0,17},{1,16},{2,19},{3,18},{4,21},{5,20},{6,23},{7,22},{8,25},{9,... | collective-permute-start | bytes 1572872 | tf_op jit(solution)/shard_map/ppermute | solution.py:477
  27.1 0.9 %collective-permute-start.10 = (f32[4,16,8,256]{3,2,1,0:T(8,128)S(1)}, f32[4,16,8,256]{3,2,1,0:T(8,128)S(1)}, u32[]{:S(2)}, u32[]{:S(2)}) collective-permute-start(f32[4,16,8,256]{3,2,1,0:T(8,128)S(1)} %pad_maximum_fusion.refs_0_), channel_id=1, source_target_pairs={{0,16},{8,24},{16,0},{24,8},{1,17},{9,25},{17,1},{25,9},{2,18},{10... | collective-permute-start | bytes 1572872 | tf_op jit(solution)/shard_map/ppermute | solution.py:473
  28.1 1.1 %collective-permute-start.9 = (f32[4,16,8,256]{3,2,1,0:T(8,128)S(1)}, f32[4,16,8,256]{3,2,1,0:T(8,128)S(1)}, u32[]{:S(2)}, u32[]{:S(2)}) collective-permute-start(f32[4,16,8,256]{3,2,1,0:T(8,128)S(1)} %pad_maximum_fusion.refs_0_), channel_id=1, source_target_pairs={{0,1},{1,0},{2,3},{3,2},{4,5},{5,4},{6,7},{7,6},{8,9},{9,8},{10,11... | collective-permute-start | bytes 1572872 | tf_op jit(solution)/shard_map/ppermute | solution.py:471
  29.1 0.0 collective-permute-start.12
  29.1 0.5 collective-permute-start.13
  29.7 0.8 collective-permute-done.12.refs_2_.refs_10_
  30.5 0.1 collective-permute-start.14
  30.6 0.0 collective-permute-done.13.refs_3_.refs_11_
  30.7 0.3 collective-permute-start.15
  31.0 0.8 collective-permute-done.14.refs_6_.refs_14_
  31.8 0.2 collective-permute-done.15.refs_7_.refs_15_
  32.0 12.7 %tiles.1 = (s32[12,2,256]{2,1,0:T(2,128)}, bf16[120,2,256,256]{3,2,1,0:T(8,128)(2,1)S(1)}) custom-call(f32[4,4,8,256]{3,2,1,0:T(8,128)S(1)} %pad_maximum_fusion.1.refs_0_.refs_8_, f32[4,4,8,256]{3,2,1,0:T(8,128)S(1)} %collective-permute-done.6.refs_1_.refs_9_, f32[4,4,8,256]{3,2,1,0:T(8,128)S(1)} %collective-permute-done.12.refs_2_.refs_10_, ...), custom_call_target="tpu_custom_call" | custom-call | flops 1000000000 | bytes 31457280 | tf_op jit(solution)/shard_map/tiles/pallas_call | solution.py:507
  44.7 0.0 collective-permute-done.11.refs_5_
  44.7 4.4 %collective-permute-done.10.refs_4_ = f32[4,16,8,256]{3,2,1,0:T(8,128)S(1)} collective-permute-done((f32[4,16,8,256]{3,2,1,0:T(8,128)S(1)}, f32[4,16,8,256]{3,2,1,0:T(8,128)S(1)}, u32[]{:S(2)}, u32[]{:S(2)}) %collective-permute-start.10) | collective-permute-done | bytes 524320 | tf_op jit(solution)/shard_map/ppermute | solution.py:473
  49.1 0.0 collective-permute-done.9.refs_1_
  49.1 1.4 %collective-permute-start.16 = (f32[4,16,8,256]{3,2,1,0:T(8,128)S(1)}, f32[4,16,8,256]{3,2,1,0:T(8,128)S(1)}, u32[]{:S(2)}, u32[]{:S(2)}) collective-permute-start(f32[4,16,8,256]{3,2,1,0:T(8,128)S(1)} %pad_maximum_fusion.refs_0_), channel_id=1, source_target_pairs={{0,8},{8,0},{16,24},{24,16},{1,9},{9,1},{17,25},{25,17},{2,10},{10... | collective-permute-start | bytes 1572872 | tf_op jit(solution)/shard_map/ppermute | solution.py:473
  50.4 0.1 collective-permute-start.17
  50.5 0.4 collective-permute-start.18
  51.0 0.1 collective-permute-start.19
  51.0 0.9 %collective-permute-done.16.refs_2_ = f32[4,16,8,256]{3,2,1,0:T(8,128)S(1)} collective-permute-done((f32[4,16,8,256]{3,2,1,0:T(8,128)S(1)}, f32[4,16,8,256]{3,2,1,0:T(8,128)S(1)}, u32[]{:S(2)}, u32[]{:S(2)}) %collective-permute-start.16) | collective-permute-done | bytes 524320 | tf_op jit(solution)/shard_map/ppermute | solution.py:473
  52.0 0.7 collective-permute-done.17.refs_3_
  52.7 0.7 collective-permute-done.18.refs_6_
  53.5 0.7 collective-permute-done.19.refs_7_
  54.2 0.7 copy-done.2
  55.0 11.0 %apply.1 = (f32[8,16,256]{2,1,0:T(8,128)S(1)}, f32[8,16,256]{2,1,0:T(8,128)S(1)}, f32[32,8,128]{2,1,0:T(8,128)S(1)}) custom-call(s32[12,2,256]{2,1,0:T(2,128)S(1)} %copy-done.2, bf16[120,2,256,256]{3,2,1,0:T(8,128)(2,1)S(1)} %get-tuple-element.30.tile_ref, f32[4,16,8,256]{3,2,1,0:T(8,128)S(1)} %pad_maximum_fusion.refs_0_, ...), custom_call_target="tpu_custom_call" | custom-call | tf_op jit(solution)/shard_map/apply/pallas_call | solution.py:530
  66.0 20.1 %all_to_all.5.moment_ref = f32[32,8,128]{2,1,0:T(8,128)} all-to-all(f32[32,8,128]{2,1,0:T(8,128)S(1)} %get-tuple-element.35), channel_id=1, replica_groups=mesh['row'=4,'col'=8] {'row','col'}, dimensions={0} | all-to-all | bytes 262144 | tf_op jit(solution)/shard_map/all_to_all | solution.py:547
  86.1 2.1 %finish.1 = (f32[16,2048]{1,0:T(8,128)}, f32[16,2048]{1,0:T(8,128)}) custom-call(f32[32,8,128]{2,1,0:T(8,128)} %all_to_all.5.moment_ref, f32[16,2048]{1,0:T(8,128)} %values_ref.3, f32[8,16,256]{2,1,0:T(8,128)} %copy-done, f32[8,16,256]{2,1,0:T(8,128)} %copy-done.1), custom_call_target="tpu_custom_call" | custom-call | tf_op jit(solution)/shard_map/finish/pallas_call | solution.py:548
  (5 shorter events, 0.0 us)
Async XLA Ops:
  2.3 9.4 %collective-permute-start.5 = (f32[4,8,256]{2,1,0:T(8,128)}, f32[4,8,256]{2,1,0:T(8,128)S(1)}, u32[]{:S(2)}, u32[]{:S(2)}) collective-permute-start(f32[4,8,256]{2,1,0:T(8,128)} %get-tuple-element.21), channel_id=1, source_target_pairs={{0,6},{1,7},{2,4},{3,5},{4,2},{5,3},{6,0},{7,1},{8,14},{9,15},{10,... | collective-permute-start | bytes 98312 | tf_op jit(solution)/shard_map/ppermute | solution.py:471
  7.3 9.6 %collective-permute-start.4 = (f32[4,8,256]{2,1,0:T(8,128)}, f32[4,8,256]{2,1,0:T(8,128)S(1)}, u32[]{:S(2)}, u32[]{:S(2)}) collective-permute-start(f32[4,8,256]{2,1,0:T(8,128)} %get-tuple-element.21), channel_id=1, source_target_pairs={{0,4},{1,5},{2,6},{3,7},{4,0},{5,1},{6,2},{7,3},{8,12},{9,13},{10,... | collective-permute-start | bytes 98312 | tf_op jit(solution)/shard_map/ppermute | solution.py:471
  7.3 9.6 %collective-permute-start.3 = (f32[4,8,256]{2,1,0:T(8,128)}, f32[4,8,256]{2,1,0:T(8,128)S(1)}, u32[]{:S(2)}, u32[]{:S(2)}) collective-permute-start(f32[4,8,256]{2,1,0:T(8,128)} %get-tuple-element.21), channel_id=1, source_target_pairs={{0,2},{1,3},{2,0},{3,1},{4,6},{5,7},{6,4},{7,5},{8,10},{9,11},{10,... | collective-permute-start | bytes 98312 | tf_op jit(solution)/shard_map/ppermute | solution.py:471
  7.9 12.8 %collective-permute-start.2 = (f32[16,8,256]{2,1,0:T(8,128)}, f32[16,8,256]{2,1,0:T(8,128)S(1)}, u32[]{:S(2)}, u32[]{:S(2)}) collective-permute-start(f32[16,8,256]{2,1,0:T(8,128)} %get-tuple-element.20), channel_id=1, source_target_pairs={{0,6},{1,7},{2,4},{3,5},{4,2},{5,3},{6,0},{7,1},{8,14},{9,15},{10,... | collective-permute-start | bytes 393224 | tf_op jit(solution)/shard_map/ppermute | solution.py:471
  11.7 11.2 %collective-permute-start.1 = (f32[16,8,256]{2,1,0:T(8,128)}, f32[16,8,256]{2,1,0:T(8,128)S(1)}, u32[]{:S(2)}, u32[]{:S(2)}) collective-permute-start(f32[16,8,256]{2,1,0:T(8,128)} %get-tuple-element.20), channel_id=1, source_target_pairs={{0,4},{1,5},{2,6},{3,7},{4,0},{5,1},{6,2},{7,3},{8,12},{9,13},{10,... | collective-permute-start | bytes 393224 | tf_op jit(solution)/shard_map/ppermute | solution.py:471
  11.7 11.2 %collective-permute-start = (f32[16,8,256]{2,1,0:T(8,128)}, f32[16,8,256]{2,1,0:T(8,128)S(1)}, u32[]{:S(2)}, u32[]{:S(2)}) collective-permute-start(f32[16,8,256]{2,1,0:T(8,128)} %get-tuple-element.20), channel_id=1, source_target_pairs={{0,2},{1,3},{2,0},{3,1},{4,6},{5,7},{6,4},{7,5},{8,10},{9,11},{10,... | collective-permute-start | bytes 393224 | tf_op jit(solution)/shard_map/ppermute | solution.py:471
  17.7 6.2 %collective-permute-start.8 = (f32[4,4,8,256]{3,2,1,0:T(8,128)S(1)}, f32[4,4,8,256]{3,2,1,0:T(8,128)S(1)}, u32[]{:S(2)}, u32[]{:S(2)}) collective-permute-start(f32[4,4,8,256]{3,2,1,0:T(8,128)S(1)} %pad_maximum_fusion.1.refs_0_.refs_8_), channel_id=1, source_target_pairs={{0,17},{1,16},{2,19},{3,18},{4,21},{5,20},{6,23},{7,22},{8,25},{9,... | collective-permute-start | bytes 393224 | tf_op jit(solution)/shard_map/ppermute | solution.py:477
  20.2 5.0 %collective-permute-start.7 = (f32[4,4,8,256]{3,2,1,0:T(8,128)S(1)}, f32[4,4,8,256]{3,2,1,0:T(8,128)S(1)}, u32[]{:S(2)}, u32[]{:S(2)}) collective-permute-start(f32[4,4,8,256]{3,2,1,0:T(8,128)S(1)} %pad_maximum_fusion.1.refs_0_.refs_8_), channel_id=1, source_target_pairs={{0,16},{8,24},{16,0},{24,8},{1,17},{9,25},{17,1},{25,9},{2,18},{10... | collective-permute-start | bytes 393224 | tf_op jit(solution)/shard_map/ppermute | solution.py:473
  20.7 5.0 %collective-permute-start.6 = (f32[4,4,8,256]{3,2,1,0:T(8,128)S(1)}, f32[4,4,8,256]{3,2,1,0:T(8,128)S(1)}, u32[]{:S(2)}, u32[]{:S(2)}) collective-permute-start(f32[4,4,8,256]{3,2,1,0:T(8,128)S(1)} %pad_maximum_fusion.1.refs_0_.refs_8_), channel_id=1, source_target_pairs={{0,1},{1,0},{2,3},{3,2},{4,5},{5,4},{6,7},{7,6},{8,9},{9,8},{10,11... | collective-permute-start | bytes 393224 | tf_op jit(solution)/shard_map/ppermute | solution.py:471
  25.7 19.0 %collective-permute-start.11 = (f32[4,16,8,256]{3,2,1,0:T(8,128)S(1)}, f32[4,16,8,256]{3,2,1,0:T(8,128)S(1)}, u32[]{:S(2)}, u32[]{:S(2)}) collective-permute-start(f32[4,16,8,256]{3,2,1,0:T(8,128)S(1)} %pad_maximum_fusion.refs_0_), channel_id=1, source_target_pairs={{0,17},{1,16},{2,19},{3,18},{4,21},{5,20},{6,23},{7,22},{8,25},{9,... | collective-permute-start | bytes 1572872 | tf_op jit(solution)/shard_map/ppermute | solution.py:477
  27.1 21.9 %collective-permute-start.10 = (f32[4,16,8,256]{3,2,1,0:T(8,128)S(1)}, f32[4,16,8,256]{3,2,1,0:T(8,128)S(1)}, u32[]{:S(2)}, u32[]{:S(2)}) collective-permute-start(f32[4,16,8,256]{3,2,1,0:T(8,128)S(1)} %pad_maximum_fusion.refs_0_), channel_id=1, source_target_pairs={{0,16},{8,24},{16,0},{24,8},{1,17},{9,25},{17,1},{25,9},{2,18},{10... | collective-permute-start | bytes 1572872 | tf_op jit(solution)/shard_map/ppermute | solution.py:473
  28.1 21.0 %collective-permute-start.9 = (f32[4,16,8,256]{3,2,1,0:T(8,128)S(1)}, f32[4,16,8,256]{3,2,1,0:T(8,128)S(1)}, u32[]{:S(2)}, u32[]{:S(2)}) collective-permute-start(f32[4,16,8,256]{3,2,1,0:T(8,128)S(1)} %pad_maximum_fusion.refs_0_), channel_id=1, source_target_pairs={{0,1},{1,0},{2,3},{3,2},{4,5},{5,4},{6,7},{7,6},{8,9},{9,8},{10,11... | collective-permute-start | bytes 1572872 | tf_op jit(solution)/shard_map/ppermute | solution.py:471
  29.1 1.3 %collective-permute-start.12 = (f32[4,4,8,256]{3,2,1,0:T(8,128)S(1)}, f32[4,4,8,256]{3,2,1,0:T(8,128)S(1)}, u32[]{:S(2)}, u32[]{:S(2)}) collective-permute-start(f32[4,4,8,256]{3,2,1,0:T(8,128)S(1)} %pad_maximum_fusion.1.refs_0_.refs_8_), channel_id=1, source_target_pairs={{0,8},{8,0},{16,24},{24,16},{1,9},{9,1},{17,25},{25,17},{2,10},{10... | collective-permute-start | bytes 393224 | tf_op jit(solution)/shard_map/ppermute | solution.py:473
  29.1 1.5 %collective-permute-start.13 = (f32[4,4,8,256]{3,2,1,0:T(8,128)S(1)}, f32[4,4,8,256]{3,2,1,0:T(8,128)S(1)}, u32[]{:S(2)}, u32[]{:S(2)}) collective-permute-start(f32[4,4,8,256]{3,2,1,0:T(8,128)S(1)} %collective-permute-done.6.refs_1_.refs_9_), channel_id=1, source_target_pairs={{0,8},{8,0},{16,24},{24,16},{1,9},{9,1},{17,25},{25,17},{2,10},{10... | collective-permute-start | bytes 393224 | tf_op jit(solution)/shard_map/ppermute | solution.py:473
  30.5 1.3 %collective-permute-start.14 = (f32[4,4,8,256]{3,2,1,0:T(8,128)S(1)}, f32[4,4,8,256]{3,2,1,0:T(8,128)S(1)}, u32[]{:S(2)}, u32[]{:S(2)}) collective-permute-start(f32[4,4,8,256]{3,2,1,0:T(8,128)S(1)} %collective-permute-done.7.refs_4_.refs_12_), channel_id=1, source_target_pairs={{0,8},{8,0},{16,24},{24,16},{1,9},{9,1},{17,25},{25,17},{2,10},{10... | collective-permute-start | bytes 393224 | tf_op jit(solution)/shard_map/ppermute | solution.py:473
  30.7 1.3 %collective-permute-start.15 = (f32[4,4,8,256]{3,2,1,0:T(8,128)S(1)}, f32[4,4,8,256]{3,2,1,0:T(8,128)S(1)}, u32[]{:S(2)}, u32[]{:S(2)}) collective-permute-start(f32[4,4,8,256]{3,2,1,0:T(8,128)S(1)} %collective-permute-done.8.refs_5_.refs_13_), channel_id=1, source_target_pairs={{0,8},{8,0},{16,24},{24,16},{1,9},{9,1},{17,25},{25,17},{2,10},{10... | collective-permute-start | bytes 393224 | tf_op jit(solution)/shard_map/ppermute | solution.py:473
  49.1 2.9 %collective-permute-start.16 = (f32[4,16,8,256]{3,2,1,0:T(8,128)S(1)}, f32[4,16,8,256]{3,2,1,0:T(8,128)S(1)}, u32[]{:S(2)}, u32[]{:S(2)}) collective-permute-start(f32[4,16,8,256]{3,2,1,0:T(8,128)S(1)} %pad_maximum_fusion.refs_0_), channel_id=1, source_target_pairs={{0,8},{8,0},{16,24},{24,16},{1,9},{9,1},{17,25},{25,17},{2,10},{10... | collective-permute-start | bytes 1572872 | tf_op jit(solution)/shard_map/ppermute | solution.py:473
  50.4 2.3 %collective-permute-start.17 = (f32[4,16,8,256]{3,2,1,0:T(8,128)S(1)}, f32[4,16,8,256]{3,2,1,0:T(8,128)S(1)}, u32[]{:S(2)}, u32[]{:S(2)}) collective-permute-start(f32[4,16,8,256]{3,2,1,0:T(8,128)S(1)} %collective-permute-done.9.refs_1_), channel_id=1, source_target_pairs={{0,8},{8,0},{16,24},{24,16},{1,9},{9,1},{17,25},{25,17},{2,10},{10... | collective-permute-start | bytes 1572872 | tf_op jit(solution)/shard_map/ppermute | solution.py:473
  50.5 3.0 %collective-permute-start.18 = (f32[4,16,8,256]{3,2,1,0:T(8,128)S(1)}, f32[4,16,8,256]{3,2,1,0:T(8,128)S(1)}, u32[]{:S(2)}, u32[]{:S(2)}) collective-permute-start(f32[4,16,8,256]{3,2,1,0:T(8,128)S(1)} %collective-permute-done.10.refs_4_), channel_id=1, source_target_pairs={{0,8},{8,0},{16,24},{24,16},{1,9},{9,1},{17,25},{25,17},{2,10},{10... | collective-permute-start | bytes 1572872 | tf_op jit(solution)/shard_map/ppermute | solution.py:473
  51.0 3.3 %collective-permute-start.19 = (f32[4,16,8,256]{3,2,1,0:T(8,128)S(1)}, f32[4,16,8,256]{3,2,1,0:T(8,128)S(1)}, u32[]{:S(2)}, u32[]{:S(2)}) collective-permute-start(f32[4,16,8,256]{3,2,1,0:T(8,128)S(1)} %collective-permute-done.11.refs_5_), channel_id=1, source_target_pairs={{0,8},{8,0},{16,24},{24,16},{1,9},{9,1},{17,25},{25,17},{2,10},{10... | collective-permute-start | bytes 1572872 | tf_op jit(solution)/shard_map/ppermute | solution.py:473
  54.2 0.7 copy-start.2
  66.0 20.1 %copy-start = (f32[8,16,256]{2,1,0:T(8,128)}, f32[8,16,256]{2,1,0:T(8,128)S(1)}, u32[]{:S(2)}) copy-start(f32[8,16,256]{2,1,0:T(8,128)S(1)} %get-tuple-element.36.w_ref) | copy-start | bytes 393220
  66.0 20.1 %copy-start.1 = (f32[8,16,256]{2,1,0:T(8,128)}, f32[8,16,256]{2,1,0:T(8,128)S(1)}, u32[]{:S(2)}) copy-start(f32[8,16,256]{2,1,0:T(8,128)S(1)} %get-tuple-element.37.x_ref) | copy-start | bytes 393220

commit v3 on v2

--- a/solution.py
+++ b/solution.py
@@ -132,11 +132,12 @@
     found = []
     base = 0
     for kind in range(2):
-        n = lists[kind * (lists.shape[0] // 2), 1, 0]
+        chunk = kind * (lists.shape[0] // 2)
+        n = lists[chunk, 1, 0]
         held = jnp.minimum(n, jnp.maximum(cap - base, 0))
-        found.append((n, held, base))
+        found.append((n, lists[chunk, 1, 1], held, base))
         base = base + held
-    return found, lists[0, 1, 1]
+    return found
 
 
 def gather(refs, target, sems):
@@ -225,8 +226,8 @@
         totals = jnp.where(lane == 0, n, n_own)
         first = kind * (list_ref.shape[0] // 2)
 
-        def write(chunk, carry):
-            place = lane.astype(jnp.float32) + (chunk * CHUNK).astype(jnp.float32)
+        def write(chunk, place_in_plan):
+            place = lane.astype(jnp.float32) + chunk * float(CHUNK)
             pick = jnp.where((start_col <= place) & (place < stop_col), 1.0, 0.0)
             column = jnp.sum(pick * low_ids, axis=0, keepdims=True)
             begin = jnp.sum(pick * start_col, axis=0, keepdims=True)
@@ -235,25 +236,38 @@
             match = jnp.where(ranks == place - begin + 1.0, 1.0, 0.0)
             row = jnp.sum(match * low_ids, axis=0, keepdims=True)
             code = row.astype(jnp.int32) * 65536 + column.astype(jnp.int32)
-            plan[...] = jnp.concatenate([code, totals], axis=0)
-            copies = [
-                pltpu.make_async_copy(plan, lists.at[first + chunk], list_sems.at[0]),
-                pltpu.make_async_copy(plan, list_ref.at[first + chunk], list_sems.at[1]),
+            plan[place_in_plan] = jnp.concatenate([code, totals], axis=0)
+
+        def send(chunk, place_in_plan):
+            return [
+                pltpu.make_async_copy(plan.at[place_in_plan], target.at[first + chunk], list_sems.at[place_in_plan, k])
+                for k, target in enumerate((lists, list_ref))
             ]
-            for copy in copies:
+
+        def write_more(chunk, carry):
+            write(chunk.astype(jnp.float32), 2)
+            for copy in send(chunk, 2):
                 copy.start()
-            for copy in copies:
+            for copy in send(chunk, 2):
                 copy.wait()
             return carry
 
-        lax.fori_loop(0, jnp.maximum((n + CHUNK - 1) // CHUNK, 1), write, 0)
-
-    write_list(0, jnp.where(listed & (rows >= columns) & near_row & near_col, 1.0, 0.0))
-    write_list(1, jnp.where(listed & near_row & jnp.logical_not(near_col), 1.0, 0.0))
-    kinds, _ = sizes(lists, cap)
-
-    first_held = kinds[0][1]
-    held = first_held + kinds[1][1]
+        write(0.0, kind)
+        for copy in send(0, kind):
+            copy.start()
+        lax.fori_loop(1, (n + CHUNK - 1) // CHUNK, write_more, 0)
+        return send(0, kind)
+
+    sent = [
+        write_list(0, jnp.where(listed & (rows > columns) & near_row & near_col, 1.0, 0.0)),
+        write_list(1, jnp.where(listed & near_row & ((rows == columns) | jnp.logical_not(near_col)), 1.0, 0.0)),
+    ]
+    for to_lists, _ in sent:
+        to_lists.wait()
+    kinds = sizes(lists, cap)
+
+    first_held = kinds[0][2]
+    held = first_held + kinds[1][2]
 
     def write_tiles(form):
         def body(group, carry):
@@ -274,23 +288,26 @@
     def _():
         write_tiles(evaluate)
 
-
-def apply_kernel(pieces, point_pieces, per_device, cap, lists, tile_ref, *refs):
+    for _, to_result in sent:
+        to_result.wait()
+
+
+def apply_kernel(pieces, point_pieces, per_device, cap, list_ref, tile_ref, *refs):
     value_refs = refs[:pieces]
     point_refs = refs[pieces : pieces + point_pieces]
     w_ref, x_ref, moment_ref = refs[pieces + point_pieces : pieces + point_pieces + 3]
-    field, total, second, late, cloud, sems, point_sems = refs[pieces + point_pieces + 3 :]
+    field, total, second, late, cloud, lists, sems, point_sems, list_sem = refs[pieces + point_pieces + 3 :]
     devices = field.shape[0]
     blocks = devices * per_device
     block_shift = per_device.bit_length() - 1
     low_mask = per_device - 1
-    kinds, n_own = sizes(lists, cap)
-    fills = gather(value_refs, field, sems)
+    fills = [pltpu.make_async_copy(list_ref, lists, list_sem)] + gather(value_refs, field, sems)
     for copy in fills:
         copy.start()
     total[...] = jnp.zeros_like(total)
     for copy in fills:
         copy.wait()
+    kinds = sizes(lists, cap)
 
     def at(b):
         return lax.shift_right_logical(b, block_shift), pl.ds(2 * (b & low_mask), 2)
@@ -315,24 +332,17 @@
         return load(total, b) + load(field, b)
 
     def run(kind, held, source, target, spare, back):
-        base = kinds[kind][2]
+        base = kinds[kind][3]
 
         def body(group, carry):
-            def forward(u):
+            pending = []
+            for u in range(GROUP):
                 k = group * GROUP + u
                 i, j = entry(lists, kind, k)
-                return jnp.where(k < held, i, spare), product(source(j), tile_ref.at[base + k], 0)
-
-            def reverse(u):
-                k = group * GROUP + u
-                i, j = entry(lists, kind, k)
-                wanted = (k < held) & (i != j) & (j < spare)
-                return jnp.where(wanted, j, spare), product(source(i), tile_ref.at[base + k], 1)
-
-            if back == "always":
-                pending = [form(u) for u in range(GROUP) for form in (forward, reverse)]
-            else:
-                pending = [forward(u) for u in range(GROUP)]
+                live = k < held
+                pending.append((jnp.where(live, i, spare), product(source(j), tile_ref.at[base + k], 0)))
+                if back == "always":
+                    pending.append((jnp.where(live, j, spare), product(source(i), tile_ref.at[base + k], 1)))
             for b, value in pending:
                 add(target, b, value)
             if back == "some":
@@ -340,7 +350,7 @@
                     k = group * GROUP + u
                     i, j = entry(lists, kind, k)
 
-                    @pl.when((k < held) & (i != j) & (j < spare))
+                    @pl.when((k < held) & (j < spare))
                     def _():
                         add(target, j, product(source(i), tile_ref.at[base + k], 1))
 
@@ -355,7 +365,7 @@
             add(target, i, product(source(j), late, 0))
             if kind == 0:
 
-                @pl.when((i != j) & (j < spare))
+                @pl.when(j < spare)
                 def _():
                     add(target, j, product(source(i), late, 1))
 
@@ -366,23 +376,25 @@
     def own_field(b):
         return load(field, b)
 
-    run(0, kinds[0][1], own_field, total, blocks, "always")
-    run(1, kinds[1][1], own_field, total, blocks, "never")
-
-    @pl.when((kinds[0][0] > kinds[0][1]) | (kinds[1][0] > kinds[1][1]))
+    run(0, kinds[0][2], own_field, total, blocks, "always")
+    run(1, kinds[1][2], own_field, total, blocks, "never")
+
+    @pl.when((kinds[0][0] > kinds[0][2]) | (kinds[1][0] > kinds[1][2]))
     def _():
         copies = gather(point_refs, cloud, point_sems)
         for copy in copies:
             copy.start()
         for copy in copies:
             copy.wait()
-        for kind, (n, held, _) in enumerate(kinds):
+        for kind, (n, _, held, _) in enumerate(kinds):
             run_late(kind, held, n, own_field, total, blocks)
 
     second[0] = total[0] + field[0]
-    held_own = jnp.minimum(n_own, kinds[0][1])
-    run(0, held_own, image, second, per_device, "some")
-    run_late(0, held_own, n_own, image, second, per_device)
+    for kind, back in enumerate(("some", "never")):
+        _, n_own, held, _ = kinds[kind]
+        held_own = jnp.minimum(n_own, held)
+        run(kind, held_own, image, second, per_device, back)
+        run_late(kind, held_own, n_own, image, second, per_device)
 
     v = field[0].reshape(per_device, 16, BLK)
     w = (total[0] + field[0]).reshape(per_device, 16, BLK)
@@ -450,7 +462,6 @@
     devices = rows * cols
     depth = cols // 2
     vmem = pl.BlockSpec(memory_space=pltpu.VMEM)
-    smem = pl.BlockSpec(memory_space=pltpu.SMEM)
     anywhere = pl.BlockSpec(memory_space=pl.ANY)
     height = 2 * per_device
     blocks = devices * per_device
@@ -495,6 +506,7 @@
     value_line, point_plane = lax.optimization_barrier((along(own_values), point_plane))
     point_parts = pairs(point_plane)
     value_plane = across(value_line)
+    core_line = swap(value_line, 1, 0)
 
     chunks = (devices * tile_lists.shape[1] + CHUNK - 1) // CHUNK
     tile_bytes = 4 * BLK * BLK
@@ -515,22 +527,26 @@
         scratch_shapes=[
             pltpu.VMEM((devices, 4, per_device, BLK), jnp.float32),
             pltpu.VMEM((blocks, blocks), jnp.float32),
-            pltpu.VMEM((2, CHUNK), jnp.int32),
+            pltpu.VMEM((3, 2, CHUNK), jnp.int32),
             pltpu.SMEM((2 * chunks, 2, CHUNK), jnp.int32),
             pltpu.SemaphoreType.DMA((len(point_parts),)),
-            pltpu.SemaphoreType.DMA((2,)),
+            pltpu.SemaphoreType.DMA((3, 2)),
         ],
         compiler_params=pltpu.CompilerParams(vmem_limit_bytes=tiles_limit),
         cost_estimate=pl.CostEstimate(flops=10**9, bytes_accessed=30 * 2**20, transcendentals=10**7),
         name="tiles",
     )(*point_parts)
+    value_plane.pop((0, 0))
     value_plane, lists, tiles = lax.optimization_barrier((value_plane, lists, tiles))
-    value_parts = pairs(value_plane)
+    value_parts = [value_line, None, core_line, None] + [None] * (2 * rows - 4)
+    for (row_mask, x), part in value_plane.items():
+        value_parts[2 * row_mask + x] = part
+        value_parts[2 * row_mask + 2 + x] = swap(part, 1, 0)
     block_shape = jax.ShapeDtypeStruct((per_device, fields, BLK), jnp.float32)
     w, x, moments = pl.pallas_call(
         functools.partial(apply_kernel, len(value_parts), len(point_parts), per_device, cap),
         out_shape=(block_shape, block_shape, jax.ShapeDtypeStruct((devices, 8, LANES), jnp.float32)),
-        in_specs=[smem, vmem] + [anywhere] * (len(value_parts) + len(point_parts)),
+        in_specs=[anywhere, vmem] + [anywhere] * (len(value_parts) + len(point_parts)),
         out_specs=(vmem, vmem, vmem),
         scratch_shapes=[
             pltpu.VMEM((devices, height, 8, BLK), jnp.float32),
@@ -538,12 +554,19 @@
             pltpu.VMEM((2, height, 8, BLK), jnp.float32),
             pltpu.VMEM((2, BLK, BLK), jnp.bfloat16),
             pltpu.VMEM((devices, 4, per_device, BLK), jnp.float32),
+            pltpu.SMEM((2 * chunks, 2, CHUNK), jnp.int32),
             pltpu.SemaphoreType.DMA((len(value_parts),)),
             pltpu.SemaphoreType.DMA((len(point_parts),)),
+            pltpu.SemaphoreType.DMA,
         ],
         compiler_params=pltpu.CompilerParams(vmem_limit_bytes=apply_limit),
         name="apply",
-    )(lists, pltpu.with_memory_space_constraint(tiles, pltpu.VMEM), *value_parts, *point_parts)
+    )(
+        pltpu.with_memory_space_constraint(lists, pltpu.HBM),
+        pltpu.with_memory_space_constraint(tiles, pltpu.VMEM),
+        *value_parts,
+        *point_parts,
+    )
     moments = lax.all_to_all(moments, ("row", "col"), 0, 0, tiled=False)
     return pl.pallas_call(
         functools.partial(finish_kernel, per_device),

time: 87.6 us -> 84.2 us (0.961); the launches traced: 88.2 us -> 83 us
  Pallas kernels: 27.5 us -> 25.3 us
  starting transfers between devices: 20 us -> 18.7 us
  blocking collectives: 20.1 us -> 19.2 us
    pallas_call x1, Pallas kernels: 11 us -> 9.12 us  [local(): pl.pallas_call(functools.partial(apply_kernel, len(value_parts), len(poin...]
    ppermute x10, starting transfers between devices: 4.35 us -> 3.08 us  [swap(): return lax.ppermute(array, 'row', [(i, i ^ row_mask) for i in range(rows)])]
  transfers between devices with their start and end apart: 20 -> 20, of which waited for: 12 -> 10; matrix products, arithmetic and copies ran while one was open for 2% -> 2% of each run, Pallas kernels for 14% -> 15%
where the time goes in v3:
time: 84.2 us; the launch traced here: 83 us
  Pallas kernels  25.3 us (30%)
  blocking collectives  19.2 us (23%)
  starting transfers between devices  18.7 us (22%)
  waiting for transfers between devices  17.4 us (21%)
  other arithmetic  1.71 us (2%)
    all_to_all x1, blocking collectives, local(): moments = lax.all_to_all(moments, ('row', 'col'), 0, 0, tiled=False)  19.2 us
    pallas_call x1, Pallas kernels, local(): pl.pallas_call(functools.partial(tiles_kernel, len(point_parts), per_devi...  12.4 us
    ppermute x8, starting transfers between devices, swap(): return lax.ppermute(array, 'col', [(i, i ^ col_mask) for i in range(cols)])  11.6 us
    ppermute x10, waiting for transfers between devices, swap(): return lax.ppermute(array, 'row', [(i, i ^ row_mask) for i in range(rows)])  10.6 us
    pallas_call x1, Pallas kernels, local(): pl.pallas_call(functools.partial(apply_kernel, len(value_parts), len(poin...  9.12 us
    ppermute x8, waiting for transfers between devices, swap(): return lax.ppermute(array, 'col', [(i, i ^ col_mask) for i in range(cols)])  6.78 us
    ppermute x2, starting transfers between devices, swap(): return lax.ppermute(array, ('row', 'col'), pairs)  4 us
    ppermute x10, starting transfers between devices, swap(): return lax.ppermute(array, 'row', [(i, i ^ row_mask) for i in range(rows)])  3.08 us
  transfers between devices with their start and end apart: 20, of which 10 were waited for; matrix products, arithmetic and copies ran while one was open for 2% of the time, Pallas kernels for 15%

profile of v3, /device:TPU:0, one launch (start us, length us, event | category | flops | bytes accessed | tf_op | source)
XLA Modules:
  0.0 83.0 jit_solution(17631037728969695111)
XLA Ops:
  0.6 1.6 %pack.1 = (f32[16,8,256]{2,1,0:T(8,128)}, f32[4,8,256]{2,1,0:T(8,128)}) custom-call(f32[16,2048]{1,0:T(8,128)} %values_ref.3, f32[3,2048]{1,0:T(4,128)} %points_ref.1, s32[3,48]{1,0:T(4,128)} %lists_ref.1), custom_call_target="tpu_custom_call" | custom-call | tf_op jit(solution)/shard_map/pack/pallas_call | solution.py:469
  2.3 5.0 %collective-permute-start.5 = (f32[4,8,256]{2,1,0:T(8,128)}, f32[4,8,256]{2,1,0:T(8,128)S(1)}, u32[]{:S(2)}, u32[]{:S(2)}) collective-permute-start(f32[4,8,256]{2,1,0:T(8,128)} %get-tuple-element.20), channel_id=1, source_target_pairs={{0,6},{1,7},{2,4},{3,5},{4,2},{5,3},{6,0},{7,1},{8,14},{9,15},{10,... | collective-permute-start | bytes 98312 | tf_op jit(solution)/shard_map/ppermute | solution.py:482
  7.3 0.0 collective-permute-start.4
  7.3 0.6 collective-permute-start.3
  7.9 3.8 %collective-permute-start.2 = (f32[16,8,256]{2,1,0:T(8,128)}, f32[16,8,256]{2,1,0:T(8,128)S(1)}, u32[]{:S(2)}, u32[]{:S(2)}) collective-permute-start(f32[16,8,256]{2,1,0:T(8,128)} %get-tuple-element.19), channel_id=1, source_target_pairs={{0,6},{1,7},{2,4},{3,5},{4,2},{5,3},{6,0},{7,1},{8,14},{9,15},{10,... | collective-permute-start | bytes 393224 | tf_op jit(solution)/shard_map/ppermute | solution.py:482
  11.7 0.0 collective-permute-start.1
  11.7 0.0 collective-permute-done.5
  11.7 0.6 collective-permute-start
  12.3 4.6 %collective-permute-done.4 = f32[4,8,256]{2,1,0:T(8,128)S(1)} collective-permute-done((f32[4,8,256]{2,1,0:T(8,128)}, f32[4,8,256]{2,1,0:T(8,128)S(1)}, u32[]{:S(2)}, u32[]{:S(2)}) %collective-permute-start.4) | collective-permute-done | bytes 32800 | tf_op jit(solution)/shard_map/ppermute | solution.py:482
  16.9 0.0 collective-permute-done.3
  16.9 0.8 pad_maximum_fusion.1.refs_0_.refs_8_
  17.7 2.5 %collective-permute-start.8 = (f32[4,4,8,256]{3,2,1,0:T(8,128)S(1)}, f32[4,4,8,256]{3,2,1,0:T(8,128)S(1)}, u32[]{:S(2)}, u32[]{:S(2)}) collective-permute-start(f32[4,4,8,256]{3,2,1,0:T(8,128)S(1)} %pad_maximum_fusion.1.refs_0_.refs_8_), channel_id=1, source_target_pairs={{0,17},{1,16},{2,19},{3,18},{4,21},{5,20},{6,23},{7,22},{8,25},{9,... | collective-permute-start | bytes 393224 | tf_op jit(solution)/shard_map/ppermute | solution.py:488
  20.2 0.5 collective-permute-start.7
  20.7 0.0 collective-permute-done.2
  20.7 0.5 collective-permute-start.6
  21.2 1.7 %collective-permute-done.1 = f32[16,8,256]{2,1,0:T(8,128)S(1)} collective-permute-done((f32[16,8,256]{2,1,0:T(8,128)}, f32[16,8,256]{2,1,0:T(8,128)S(1)}, u32[]{:S(2)}, u32[]{:S(2)}) %collective-permute-start.1) | collective-permute-done | bytes 131104 | tf_op jit(solution)/shard_map/ppermute | solution.py:482
  22.9 0.0 collective-permute-done
  22.9 0.9 %pad_maximum_fusion.refs_0_ = f32[4,16,8,256]{3,2,1,0:T(8,128)S(1)} fusion(f32[1,16,8,256]{3,2,1,0:T(8,128)S(1)} %bitcast.9, f32[1,16,8,256]{3,2,1,0:T(8,128)S(1)} %bitcast.10, f32[1,16,8,256]{3,2,1,0:T(8,128)S(1)} %bitcast.11, f32[1,16,8,256]{3,2,1,0:T(8,128)} %bitcast.8), kind=kLoop, calls=%fused_computation | loop fusion | flops 393216 | bytes 1048576 | tf_op jit(solution)/shard_map/stack | solution.py:491
  23.8 0.0 collective-permute-done.8.refs_5_.refs_13_
  23.8 1.3 %collective-permute-done.7.refs_4_.refs_12_ = f32[4,4,8,256]{3,2,1,0:T(8,128)S(1)} collective-permute-done((f32[4,4,8,256]{3,2,1,0:T(8,128)S(1)}, f32[4,4,8,256]{3,2,1,0:T(8,128)S(1)}, u32[]{:S(2)}, u32[]{:S(2)}) %collective-permute-start.7) | collective-permute-done | bytes 131104 | tf_op jit(solution)/shard_map/ppermute | solution.py:484
  25.1 0.5 collective-permute-done.6.refs_1_.refs_9_
  25.7 1.5 %collective-permute-start.11 = (f32[4,16,8,256]{3,2,1,0:T(8,128)S(1)}, f32[4,16,8,256]{3,2,1,0:T(8,128)S(1)}, u32[]{:S(2)}, u32[]{:S(2)}) collective-permute-start(f32[4,16,8,256]{3,2,1,0:T(8,128)S(1)} %pad_maximum_fusion.refs_0_), channel_id=1, source_target_pairs={{0,17},{1,16},{2,19},{3,18},{4,21},{5,20},{6,23},{7,22},{8,25},{9,... | collective-permute-start | bytes 1572872 | tf_op jit(solution)/shard_map/ppermute | solution.py:488
  27.1 0.9 %collective-permute-start.10 = (f32[4,16,8,256]{3,2,1,0:T(8,128)S(1)}, f32[4,16,8,256]{3,2,1,0:T(8,128)S(1)}, u32[]{:S(2)}, u32[]{:S(2)}) collective-permute-start(f32[4,16,8,256]{3,2,1,0:T(8,128)S(1)} %pad_maximum_fusion.refs_0_), channel_id=1, source_target_pairs={{0,16},{8,24},{16,0},{24,8},{1,17},{9,25},{17,1},{25,9},{2,18},{10... | collective-permute-start | bytes 1572872 | tf_op jit(solution)/shard_map/ppermute | solution.py:484
  28.1 1.1 %collective-permute-start.9 = (f32[4,16,8,256]{3,2,1,0:T(8,128)S(1)}, f32[4,16,8,256]{3,2,1,0:T(8,128)S(1)}, u32[]{:S(2)}, u32[]{:S(2)}) collective-permute-start(f32[4,16,8,256]{3,2,1,0:T(8,128)S(1)} %pad_maximum_fusion.refs_0_), channel_id=1, source_target_pairs={{0,1},{1,0},{2,3},{3,2},{4,5},{5,4},{6,7},{7,6},{8,9},{9,8},{10,11... | collective-permute-start | bytes 1572872 | tf_op jit(solution)/shard_map/ppermute | solution.py:482
  29.1 0.0 collective-permute-start.12
  29.1 0.5 collective-permute-start.13
  29.7 0.8 %collective-permute-done.12.refs_2_.refs_10_ = f32[4,4,8,256]{3,2,1,0:T(8,128)S(1)} collective-permute-done((f32[4,4,8,256]{3,2,1,0:T(8,128)S(1)}, f32[4,4,8,256]{3,2,1,0:T(8,128)S(1)}, u32[]{:S(2)}, u32[]{:S(2)}) %collective-permute-start.12) | collective-permute-done | bytes 131104 | tf_op jit(solution)/shard_map/ppermute | solution.py:484
  30.5 0.1 collective-permute-start.14
  30.6 0.0 collective-permute-done.13.refs_3_.refs_11_
  30.7 0.3 collective-permute-start.15
  31.0 0.8 %collective-permute-done.14.refs_6_.refs_14_ = f32[4,4,8,256]{3,2,1,0:T(8,128)S(1)} collective-permute-done((f32[4,4,8,256]{3,2,1,0:T(8,128)S(1)}, f32[4,4,8,256]{3,2,1,0:T(8,128)S(1)}, u32[]{:S(2)}, u32[]{:S(2)}) %collective-permute-start.14) | collective-permute-done | bytes 131104 | tf_op jit(solution)/shard_map/ppermute | solution.py:484
  31.8 0.1 collective-permute-start.16
  32.0 0.0 collective-permute-done.15.refs_7_.refs_15_
  32.0 12.4 %tiles.1 = (s32[12,2,256]{2,1,0:T(2,128)}, bf16[120,2,256,256]{3,2,1,0:T(8,128)(2,1)S(1)}) custom-call(f32[4,4,8,256]{3,2,1,0:T(8,128)S(1)} %pad_maximum_fusion.1.refs_0_.refs_8_, f32[4,4,8,256]{3,2,1,0:T(8,128)S(1)} %collective-permute-done.6.refs_1_.refs_9_, f32[4,4,8,256]{3,2,1,0:T(8,128)S(1)} %collective-permute-done.12.refs_2_.refs_10_, ...), custom_call_target="tpu_custom_call" | custom-call | flops 1000000000 | bytes 31457280 | tf_op jit(solution)/shard_map/tiles/pallas_call | solution.py:519
  44.4 0.0 collective-permute-done.11.refs_5_
  44.4 4.7 %collective-permute-done.10.refs_4_ = f32[4,16,8,256]{3,2,1,0:T(8,128)S(1)} collective-permute-done((f32[4,16,8,256]{3,2,1,0:T(8,128)S(1)}, f32[4,16,8,256]{3,2,1,0:T(8,128)S(1)}, u32[]{:S(2)}, u32[]{:S(2)}) %collective-permute-start.10) | collective-permute-done | bytes 524320 | tf_op jit(solution)/shard_map/ppermute | solution.py:484
  49.1 0.0 collective-permute-done.9.refs_1_
  49.1 0.0 collective-permute-start.17
  49.1 0.5 collective-permute-start.18
  49.6 0.0 collective-permute-start.19
  49.6 0.0 collective-permute-done.16.refs_2_
  49.6 1.4 %collective-permute-done.17.refs_3_ = f32[4,16,8,256]{3,2,1,0:T(8,128)S(1)} collective-permute-done((f32[4,16,8,256]{3,2,1,0:T(8,128)S(1)}, f32[4,16,8,256]{3,2,1,0:T(8,128)S(1)}, u32[]{:S(2)}, u32[]{:S(2)}) %collective-permute-start.17) | collective-permute-done | bytes 524320 | tf_op jit(solution)/shard_map/ppermute | solution.py:484
  51.0 0.7 collective-permute-done.18.refs_6_
  51.7 0.7 collective-permute-done.19.refs_7_
  52.5 9.1 %apply.1 = (f32[8,16,256]{2,1,0:T(8,128)S(1)}, f32[8,16,256]{2,1,0:T(8,128)S(1)}, f32[32,8,128]{2,1,0:T(8,128)S(1)}) custom-call(s32[12,2,256]{2,1,0:T(2,128)} %get-tuple-element.28.list_ref, bf16[120,2,256,256]{3,2,1,0:T(8,128)(2,1)S(1)} %get-tuple-element.29.tile_ref, f32[4,16,8,256]{3,2,1,0:T(8,128)S(1)} %pad_maximum_fusion.refs_0_, ...), custom_call_target="tpu_custom_call" | custom-call | tf_op jit(solution)/shard_map/apply/pallas_call | solution.py:546
  61.6 0.0 copy-start
  61.6 19.2 %all_to_all.5.moment_ref = f32[32,8,128]{2,1,0:T(8,128)} all-to-all(f32[32,8,128]{2,1,0:T(8,128)S(1)} %get-tuple-element.33), channel_id=1, replica_groups=mesh['row'=4,'col'=8] {'row','col'}, dimensions={0} | all-to-all | bytes 262144 | tf_op jit(solution)/shard_map/all_to_all | solution.py:570
  80.8 2.1 %finish.1 = (f32[16,2048]{1,0:T(8,128)}, f32[16,2048]{1,0:T(8,128)}) custom-call(f32[32,8,128]{2,1,0:T(8,128)} %all_to_all.5.moment_ref, f32[16,2048]{1,0:T(8,128)} %values_ref.3, f32[8,16,256]{2,1,0:T(8,128)} %copy-done, f32[8,16,256]{2,1,0:T(8,128)} %copy-done.1), custom_call_target="tpu_custom_call" | custom-call | tf_op jit(solution)/shard_map/finish/pallas_call | solution.py:571
  (3 shorter events, 0.0 us)
Async XLA Ops:
  2.3 9.4 %collective-permute-start.5 = (f32[4,8,256]{2,1,0:T(8,128)}, f32[4,8,256]{2,1,0:T(8,128)S(1)}, u32[]{:S(2)}, u32[]{:S(2)}) collective-permute-start(f32[4,8,256]{2,1,0:T(8,128)} %get-tuple-element.20), channel_id=1, source_target_pairs={{0,6},{1,7},{2,4},{3,5},{4,2},{5,3},{6,0},{7,1},{8,14},{9,15},{10,... | collective-permute-start | bytes 98312 | tf_op jit(solution)/shard_map/ppermute | solution.py:482
  7.3 9.6 %collective-permute-start.4 = (f32[4,8,256]{2,1,0:T(8,128)}, f32[4,8,256]{2,1,0:T(8,128)S(1)}, u32[]{:S(2)}, u32[]{:S(2)}) collective-permute-start(f32[4,8,256]{2,1,0:T(8,128)} %get-tuple-element.20), channel_id=1, source_target_pairs={{0,4},{1,5},{2,6},{3,7},{4,0},{5,1},{6,2},{7,3},{8,12},{9,13},{10,... | collective-permute-start | bytes 98312 | tf_op jit(solution)/shard_map/ppermute | solution.py:482
  7.3 9.6 %collective-permute-start.3 = (f32[4,8,256]{2,1,0:T(8,128)}, f32[4,8,256]{2,1,0:T(8,128)S(1)}, u32[]{:S(2)}, u32[]{:S(2)}) collective-permute-start(f32[4,8,256]{2,1,0:T(8,128)} %get-tuple-element.20), channel_id=1, source_target_pairs={{0,2},{1,3},{2,0},{3,1},{4,6},{5,7},{6,4},{7,5},{8,10},{9,11},{10,... | collective-permute-start | bytes 98312 | tf_op jit(solution)/shard_map/ppermute | solution.py:482
  7.9 12.8 %collective-permute-start.2 = (f32[16,8,256]{2,1,0:T(8,128)}, f32[16,8,256]{2,1,0:T(8,128)S(1)}, u32[]{:S(2)}, u32[]{:S(2)}) collective-permute-start(f32[16,8,256]{2,1,0:T(8,128)} %get-tuple-element.19), channel_id=1, source_target_pairs={{0,6},{1,7},{2,4},{3,5},{4,2},{5,3},{6,0},{7,1},{8,14},{9,15},{10,... | collective-permute-start | bytes 393224 | tf_op jit(solution)/shard_map/ppermute | solution.py:482
  11.7 11.2 %collective-permute-start.1 = (f32[16,8,256]{2,1,0:T(8,128)}, f32[16,8,256]{2,1,0:T(8,128)S(1)}, u32[]{:S(2)}, u32[]{:S(2)}) collective-permute-start(f32[16,8,256]{2,1,0:T(8,128)} %get-tuple-element.19), channel_id=1, source_target_pairs={{0,4},{1,5},{2,6},{3,7},{4,0},{5,1},{6,2},{7,3},{8,12},{9,13},{10,... | collective-permute-start | bytes 393224 | tf_op jit(solution)/shard_map/ppermute | solution.py:482
  11.7 11.2 %collective-permute-start = (f32[16,8,256]{2,1,0:T(8,128)}, f32[16,8,256]{2,1,0:T(8,128)S(1)}, u32[]{:S(2)}, u32[]{:S(2)}) collective-permute-start(f32[16,8,256]{2,1,0:T(8,128)} %get-tuple-element.19), channel_id=1, source_target_pairs={{0,2},{1,3},{2,0},{3,1},{4,6},{5,7},{6,4},{7,5},{8,10},{9,11},{10,... | collective-permute-start | bytes 393224 | tf_op jit(solution)/shard_map/ppermute | solution.py:482
  17.7 6.2 %collective-permute-start.8 = (f32[4,4,8,256]{3,2,1,0:T(8,128)S(1)}, f32[4,4,8,256]{3,2,1,0:T(8,128)S(1)}, u32[]{:S(2)}, u32[]{:S(2)}) collective-permute-start(f32[4,4,8,256]{3,2,1,0:T(8,128)S(1)} %pad_maximum_fusion.1.refs_0_.refs_8_), channel_id=1, source_target_pairs={{0,17},{1,16},{2,19},{3,18},{4,21},{5,20},{6,23},{7,22},{8,25},{9,... | collective-permute-start | bytes 393224 | tf_op jit(solution)/shard_map/ppermute | solution.py:488
  20.2 5.0 %collective-permute-start.7 = (f32[4,4,8,256]{3,2,1,0:T(8,128)S(1)}, f32[4,4,8,256]{3,2,1,0:T(8,128)S(1)}, u32[]{:S(2)}, u32[]{:S(2)}) collective-permute-start(f32[4,4,8,256]{3,2,1,0:T(8,128)S(1)} %pad_maximum_fusion.1.refs_0_.refs_8_), channel_id=1, source_target_pairs={{0,16},{8,24},{16,0},{24,8},{1,17},{9,25},{17,1},{25,9},{2,18},{10... | collective-permute-start | bytes 393224 | tf_op jit(solution)/shard_map/ppermute | solution.py:484
  20.7 5.0 %collective-permute-start.6 = (f32[4,4,8,256]{3,2,1,0:T(8,128)S(1)}, f32[4,4,8,256]{3,2,1,0:T(8,128)S(1)}, u32[]{:S(2)}, u32[]{:S(2)}) collective-permute-start(f32[4,4,8,256]{3,2,1,0:T(8,128)S(1)} %pad_maximum_fusion.1.refs_0_.refs_8_), channel_id=1, source_target_pairs={{0,1},{1,0},{2,3},{3,2},{4,5},{5,4},{6,7},{7,6},{8,9},{9,8},{10,11... | collective-permute-start | bytes 393224 | tf_op jit(solution)/shard_map/ppermute | solution.py:482
  25.7 18.8 %collective-permute-start.11 = (f32[4,16,8,256]{3,2,1,0:T(8,128)S(1)}, f32[4,16,8,256]{3,2,1,0:T(8,128)S(1)}, u32[]{:S(2)}, u32[]{:S(2)}) collective-permute-start(f32[4,16,8,256]{3,2,1,0:T(8,128)S(1)} %pad_maximum_fusion.refs_0_), channel_id=1, source_target_pairs={{0,17},{1,16},{2,19},{3,18},{4,21},{5,20},{6,23},{7,22},{8,25},{9,... | collective-permute-start | bytes 1572872 | tf_op jit(solution)/shard_map/ppermute | solution.py:488
  27.1 21.9 %collective-permute-start.10 = (f32[4,16,8,256]{3,2,1,0:T(8,128)S(1)}, f32[4,16,8,256]{3,2,1,0:T(8,128)S(1)}, u32[]{:S(2)}, u32[]{:S(2)}) collective-permute-start(f32[4,16,8,256]{3,2,1,0:T(8,128)S(1)} %pad_maximum_fusion.refs_0_), channel_id=1, source_target_pairs={{0,16},{8,24},{16,0},{24,8},{1,17},{9,25},{17,1},{25,9},{2,18},{10... | collective-permute-start | bytes 1572872 | tf_op jit(solution)/shard_map/ppermute | solution.py:484
  28.1 21.0 %collective-permute-start.9 = (f32[4,16,8,256]{3,2,1,0:T(8,128)S(1)}, f32[4,16,8,256]{3,2,1,0:T(8,128)S(1)}, u32[]{:S(2)}, u32[]{:S(2)}) collective-permute-start(f32[4,16,8,256]{3,2,1,0:T(8,128)S(1)} %pad_maximum_fusion.refs_0_), channel_id=1, source_target_pairs={{0,1},{1,0},{2,3},{3,2},{4,5},{5,4},{6,7},{7,6},{8,9},{9,8},{10,11... | collective-permute-start | bytes 1572872 | tf_op jit(solution)/shard_map/ppermute | solution.py:482
  29.1 1.3 %collective-permute-start.12 = (f32[4,4,8,256]{3,2,1,0:T(8,128)S(1)}, f32[4,4,8,256]{3,2,1,0:T(8,128)S(1)}, u32[]{:S(2)}, u32[]{:S(2)}) collective-permute-start(f32[4,4,8,256]{3,2,1,0:T(8,128)S(1)} %pad_maximum_fusion.1.refs_0_.refs_8_), channel_id=1, source_target_pairs={{0,8},{8,0},{16,24},{24,16},{1,9},{9,1},{17,25},{25,17},{2,10},{10... | collective-permute-start | bytes 393224 | tf_op jit(solution)/shard_map/ppermute | solution.py:484
  29.1 1.5 %collective-permute-start.13 = (f32[4,4,8,256]{3,2,1,0:T(8,128)S(1)}, f32[4,4,8,256]{3,2,1,0:T(8,128)S(1)}, u32[]{:S(2)}, u32[]{:S(2)}) collective-permute-start(f32[4,4,8,256]{3,2,1,0:T(8,128)S(1)} %collective-permute-done.6.refs_1_.refs_9_), channel_id=1, source_target_pairs={{0,8},{8,0},{16,24},{24,16},{1,9},{9,1},{17,25},{25,17},{2,10},{10... | collective-permute-start | bytes 393224 | tf_op jit(solution)/shard_map/ppermute | solution.py:484
  30.5 1.3 %collective-permute-start.14 = (f32[4,4,8,256]{3,2,1,0:T(8,128)S(1)}, f32[4,4,8,256]{3,2,1,0:T(8,128)S(1)}, u32[]{:S(2)}, u32[]{:S(2)}) collective-permute-start(f32[4,4,8,256]{3,2,1,0:T(8,128)S(1)} %collective-permute-done.7.refs_4_.refs_12_), channel_id=1, source_target_pairs={{0,8},{8,0},{16,24},{24,16},{1,9},{9,1},{17,25},{25,17},{2,10},{10... | collective-permute-start | bytes 393224 | tf_op jit(solution)/shard_map/ppermute | solution.py:484
  30.7 1.3 %collective-permute-start.15 = (f32[4,4,8,256]{3,2,1,0:T(8,128)S(1)}, f32[4,4,8,256]{3,2,1,0:T(8,128)S(1)}, u32[]{:S(2)}, u32[]{:S(2)}) collective-permute-start(f32[4,4,8,256]{3,2,1,0:T(8,128)S(1)} %collective-permute-done.8.refs_5_.refs_13_), channel_id=1, source_target_pairs={{0,8},{8,0},{16,24},{24,16},{1,9},{9,1},{17,25},{25,17},{2,10},{10... | collective-permute-start | bytes 393224 | tf_op jit(solution)/shard_map/ppermute | solution.py:484
  31.8 17.8 %collective-permute-start.16 = (f32[4,16,8,256]{3,2,1,0:T(8,128)S(1)}, f32[4,16,8,256]{3,2,1,0:T(8,128)S(1)}, u32[]{:S(2)}, u32[]{:S(2)}) collective-permute-start(f32[4,16,8,256]{3,2,1,0:T(8,128)S(1)} %pad_maximum_fusion.refs_0_), channel_id=1, source_target_pairs={{0,8},{8,0},{16,24},{24,16},{1,9},{9,1},{17,25},{25,17},{2,10},{10... | collective-permute-start | bytes 1572872 | tf_op jit(solution)/shard_map/ppermute | solution.py:484
  49.1 1.9 %collective-permute-start.17 = (f32[4,16,8,256]{3,2,1,0:T(8,128)S(1)}, f32[4,16,8,256]{3,2,1,0:T(8,128)S(1)}, u32[]{:S(2)}, u32[]{:S(2)}) collective-permute-start(f32[4,16,8,256]{3,2,1,0:T(8,128)S(1)} %collective-permute-done.9.refs_1_), channel_id=1, source_target_pairs={{0,8},{8,0},{16,24},{24,16},{1,9},{9,1},{17,25},{25,17},{2,10},{10... | collective-permute-start | bytes 1572872 | tf_op jit(solution)/shard_map/ppermute | solution.py:484
  49.1 2.6 %collective-permute-start.18 = (f32[4,16,8,256]{3,2,1,0:T(8,128)S(1)}, f32[4,16,8,256]{3,2,1,0:T(8,128)S(1)}, u32[]{:S(2)}, u32[]{:S(2)}) collective-permute-start(f32[4,16,8,256]{3,2,1,0:T(8,128)S(1)} %collective-permute-done.10.refs_4_), channel_id=1, source_target_pairs={{0,8},{8,0},{16,24},{24,16},{1,9},{9,1},{17,25},{25,17},{2,10},{10... | collective-permute-start | bytes 1572872 | tf_op jit(solution)/shard_map/ppermute | solution.py:484
  49.6 2.9 %collective-permute-start.19 = (f32[4,16,8,256]{3,2,1,0:T(8,128)S(1)}, f32[4,16,8,256]{3,2,1,0:T(8,128)S(1)}, u32[]{:S(2)}, u32[]{:S(2)}) collective-permute-start(f32[4,16,8,256]{3,2,1,0:T(8,128)S(1)} %collective-permute-done.11.refs_5_), channel_id=1, source_target_pairs={{0,8},{8,0},{16,24},{24,16},{1,9},{9,1},{17,25},{25,17},{2,10},{10... | collective-permute-start | bytes 1572872 | tf_op jit(solution)/shard_map/ppermute | solution.py:484
  61.6 19.2 %copy-start = (f32[8,16,256]{2,1,0:T(8,128)}, f32[8,16,256]{2,1,0:T(8,128)S(1)}, u32[]{:S(2)}) copy-start(f32[8,16,256]{2,1,0:T(8,128)S(1)} %get-tuple-element.34.w_ref) | copy-start | bytes 393220
  61.6 19.2 %copy-start.1 = (f32[8,16,256]{2,1,0:T(8,128)}, f32[8,16,256]{2,1,0:T(8,128)S(1)}, u32[]{:S(2)}) copy-start(f32[8,16,256]{2,1,0:T(8,128)S(1)} %get-tuple-element.35.x_ref) | copy-start | bytes 393220

commit v4 on v3

--- a/solution.py
+++ b/solution.py
@@ -12,6 +12,7 @@
 LANES = 128
 CHUNK = 256
 GROUP = 8
+BATCH = 12
 
 support = 0.5
 ridge_shift = 1.0
@@ -271,14 +272,14 @@
 
     def write_tiles(form):
         def body(group, carry):
-            for part in range(GROUP):
-                slot = group * GROUP + part
+            for part in range(BATCH):
+                slot = group * BATCH + part
                 kind = (slot >= first_held).astype(jnp.int32)
                 i, j = entry(lists, kind, slot - kind * first_held)
                 form(point_rows(cloud, i, per_device), point_rows(cloud, j, per_device), tile_ref.at[slot])
             return carry
 
-        lax.fori_loop(0, (held + GROUP - 1) // GROUP, body, 0)
+        lax.fori_loop(0, (held + BATCH - 1) // BATCH, body, 0)
 
     @pl.when(extent <= 1.5 / support)
     def _():
@@ -514,13 +515,13 @@
     field_bytes = blocks * fields * BLK * 4
     tiles_limit = cloud_bytes + 6 * 4 * blocks * blocks + 10 * 2**20
     apply_limit = cloud_bytes + 2 * field_bytes + 6 * 2**20
-    room = 60 * 2**20 - max(tiles_limit, apply_limit)
-    cap = max(GROUP, min(120, room // tile_bytes // GROUP * GROUP))
+    room = 60 * 2**20 - max(GROUP, BATCH) * tile_bytes - max(tiles_limit, apply_limit)
+    cap = max(GROUP, min(112, room // tile_bytes // GROUP * GROUP))
     lists, tiles = pl.pallas_call(
         functools.partial(tiles_kernel, len(point_parts), per_device, cap),
         out_shape=(
             pltpu.HBM((2 * chunks, 2, CHUNK), jnp.int32),
-            pltpu.VMEM((cap, 2, BLK, BLK), jnp.bfloat16),
+            pltpu.VMEM((cap + max(GROUP, BATCH), 2, BLK, BLK), jnp.bfloat16),
         ),
         in_specs=[anywhere] * len(point_parts),
         out_specs=(anywhere, vmem),

time: 84.2 us -> 84.1 us (level)
  Pallas kernels: 25.3 us -> 18.3 us
  blocking collectives: 19.2 us -> 21.7 us
  waiting for transfers between devices: 17.4 us -> 19.9 us
  starting transfers between devices: 18.7 us -> 20.9 us
    pallas_call x1, Pallas kernels: 9.12 us -> 4.99 us  [local(): pl.pallas_call(functools.partial(apply_kernel, len(value_parts), len(poin...]
    pallas_call x1, Pallas kernels: 12.4 us -> 9.48 us  [local(): pl.pallas_call(functools.partial(tiles_kernel, len(point_parts), per_devi...]
    ppermute x10, waiting for transfers between devices: 10.6 us -> 13.1 us  [swap(): return lax.ppermute(array, 'row', [(i, i ^ row_mask) for i in range(rows)])]
    all_to_all x1, blocking collectives: 19.2 us -> 21.7 us  [local(): moments = lax.all_to_all(moments, ('row', 'col'), 0, 0, tiled=False)]
    ppermute x10, starting transfers between devices: 3.08 us -> 5.31 us  [swap(): return lax.ppermute(array, 'row', [(i, i ^ row_mask) for i in range(rows)])]
  transfers between devices with their start and end apart: 20 -> 20, of which waited for: 10 -> 10; matrix products, arithmetic and copies ran while one was open for 2% -> 2% of each run, Pallas kernels for 15% -> 11%
where the time goes in v4:
time: 84.1 us; the launch traced here: 83.2 us
  blocking collectives  21.7 us (26%)
  starting transfers between devices  20.9 us (25%)
  waiting for transfers between devices  19.9 us (24%)
  Pallas kernels  18.3 us (22%)
  other arithmetic  1.71 us (2%)
    all_to_all x1, blocking collectives, local(): moments = lax.all_to_all(moments, ('row', 'col'), 0, 0, tiled=False)  21.7 us
    ppermute x10, waiting for transfers between devices, swap(): return lax.ppermute(array, 'row', [(i, i ^ row_mask) for i in range(rows)])  13.1 us
    ppermute x8, starting transfers between devices, swap(): return lax.ppermute(array, 'col', [(i, i ^ col_mask) for i in range(cols)])  11.6 us
    pallas_call x1, Pallas kernels, local(): pl.pallas_call(functools.partial(tiles_kernel, len(point_parts), per_devi...  9.48 us
    ppermute x8, waiting for transfers between devices, swap(): return lax.ppermute(array, 'col', [(i, i ^ col_mask) for i in range(cols)])  6.78 us
    ppermute x10, starting transfers between devices, swap(): return lax.ppermute(array, 'row', [(i, i ^ row_mask) for i in range(rows)])  5.31 us
    pallas_call x1, Pallas kernels, local(): pl.pallas_call(functools.partial(apply_kernel, len(value_parts), len(poin...  4.99 us
    ppermute x2, starting transfers between devices, swap(): return lax.ppermute(array, ('row', 'col'), pairs)  4 us
  transfers between devices with their start and end apart: 20, of which 10 were waited for; matrix products, arithmetic and copies ran while one was open for 2% of the time, Pallas kernels for 11%

profile of v4, /device:TPU:0, one launch (start us, length us, event | category | flops | bytes accessed | tf_op | source)
XLA Modules:
  0.0 83.2 jit_solution(9312293899957840696)
XLA Ops:
  0.6 1.6 %pack.1 = (f32[16,8,256]{2,1,0:T(8,128)}, f32[4,8,256]{2,1,0:T(8,128)}) custom-call(f32[16,2048]{1,0:T(8,128)} %values_ref.3, f32[3,2048]{1,0:T(4,128)} %points_ref.1, s32[3,48]{1,0:T(4,128)} %lists_ref.1), custom_call_target="tpu_custom_call" | custom-call | tf_op jit(solution)/shard_map/pack/pallas_call | solution.py:470
  2.3 5.0 %collective-permute-start.5 = (f32[4,8,256]{2,1,0:T(8,128)}, f32[4,8,256]{2,1,0:T(8,128)S(1)}, u32[]{:S(2)}, u32[]{:S(2)}) collective-permute-start(f32[4,8,256]{2,1,0:T(8,128)} %get-tuple-element.20), channel_id=1, source_target_pairs={{0,6},{1,7},{2,4},{3,5},{4,2},{5,3},{6,0},{7,1},{8,14},{9,15},{10,... | collective-permute-start | bytes 98312 | tf_op jit(solution)/shard_map/ppermute | solution.py:483
  7.3 0.0 collective-permute-start.4
  7.3 0.6 collective-permute-start.3
  7.9 3.8 %collective-permute-start.2 = (f32[16,8,256]{2,1,0:T(8,128)}, f32[16,8,256]{2,1,0:T(8,128)S(1)}, u32[]{:S(2)}, u32[]{:S(2)}) collective-permute-start(f32[16,8,256]{2,1,0:T(8,128)} %get-tuple-element.19), channel_id=1, source_target_pairs={{0,6},{1,7},{2,4},{3,5},{4,2},{5,3},{6,0},{7,1},{8,14},{9,15},{10,... | collective-permute-start | bytes 393224 | tf_op jit(solution)/shard_map/ppermute | solution.py:483
  11.7 0.0 collective-permute-start.1
  11.7 0.0 collective-permute-done.5
  11.7 0.6 collective-permute-start
  12.3 4.6 %collective-permute-done.4 = f32[4,8,256]{2,1,0:T(8,128)S(1)} collective-permute-done((f32[4,8,256]{2,1,0:T(8,128)}, f32[4,8,256]{2,1,0:T(8,128)S(1)}, u32[]{:S(2)}, u32[]{:S(2)}) %collective-permute-start.4) | collective-permute-done | bytes 32800 | tf_op jit(solution)/shard_map/ppermute | solution.py:483
  16.9 0.0 collective-permute-done.3
  16.9 0.8 pad_maximum_fusion.1.refs_0_.refs_8_
  17.7 2.5 %collective-permute-start.8 = (f32[4,4,8,256]{3,2,1,0:T(8,128)S(1)}, f32[4,4,8,256]{3,2,1,0:T(8,128)S(1)}, u32[]{:S(2)}, u32[]{:S(2)}) collective-permute-start(f32[4,4,8,256]{3,2,1,0:T(8,128)S(1)} %pad_maximum_fusion.1.refs_0_.refs_8_), channel_id=1, source_target_pairs={{0,17},{1,16},{2,19},{3,18},{4,21},{5,20},{6,23},{7,22},{8,25},{9,... | collective-permute-start | bytes 393224 | tf_op jit(solution)/shard_map/ppermute | solution.py:489
  20.2 0.5 collective-permute-start.7
  20.7 0.0 collective-permute-done.2
  20.7 0.5 collective-permute-start.6
  21.2 1.7 %collective-permute-done.1 = f32[16,8,256]{2,1,0:T(8,128)S(1)} collective-permute-done((f32[16,8,256]{2,1,0:T(8,128)}, f32[16,8,256]{2,1,0:T(8,128)S(1)}, u32[]{:S(2)}, u32[]{:S(2)}) %collective-permute-start.1) | collective-permute-done | bytes 131104 | tf_op jit(solution)/shard_map/ppermute | solution.py:483
  22.9 0.0 collective-permute-done
  22.9 0.9 %pad_maximum_fusion.refs_0_ = f32[4,16,8,256]{3,2,1,0:T(8,128)S(1)} fusion(f32[1,16,8,256]{3,2,1,0:T(8,128)S(1)} %bitcast.9, f32[1,16,8,256]{3,2,1,0:T(8,128)S(1)} %bitcast.10, f32[1,16,8,256]{3,2,1,0:T(8,128)S(1)} %bitcast.11, f32[1,16,8,256]{3,2,1,0:T(8,128)} %bitcast.8), kind=kLoop, calls=%fused_computation | loop fusion | flops 393216 | bytes 1048576 | tf_op jit(solution)/shard_map/stack | solution.py:492
  23.8 0.0 collective-permute-done.8.refs_5_.refs_13_
  23.8 1.3 %collective-permute-done.7.refs_4_.refs_12_ = f32[4,4,8,256]{3,2,1,0:T(8,128)S(1)} collective-permute-done((f32[4,4,8,256]{3,2,1,0:T(8,128)S(1)}, f32[4,4,8,256]{3,2,1,0:T(8,128)S(1)}, u32[]{:S(2)}, u32[]{:S(2)}) %collective-permute-start.7) | collective-permute-done | bytes 131104 | tf_op jit(solution)/shard_map/ppermute | solution.py:485
  25.1 0.5 collective-permute-done.6.refs_1_.refs_9_
  25.7 1.5 %collective-permute-start.11 = (f32[4,16,8,256]{3,2,1,0:T(8,128)S(1)}, f32[4,16,8,256]{3,2,1,0:T(8,128)S(1)}, u32[]{:S(2)}, u32[]{:S(2)}) collective-permute-start(f32[4,16,8,256]{3,2,1,0:T(8,128)S(1)} %pad_maximum_fusion.refs_0_), channel_id=1, source_target_pairs={{0,17},{1,16},{2,19},{3,18},{4,21},{5,20},{6,23},{7,22},{8,25},{9,... | collective-permute-start | bytes 1572872 | tf_op jit(solution)/shard_map/ppermute | solution.py:489
  27.1 0.9 %collective-permute-start.10 = (f32[4,16,8,256]{3,2,1,0:T(8,128)S(1)}, f32[4,16,8,256]{3,2,1,0:T(8,128)S(1)}, u32[]{:S(2)}, u32[]{:S(2)}) collective-permute-start(f32[4,16,8,256]{3,2,1,0:T(8,128)S(1)} %pad_maximum_fusion.refs_0_), channel_id=1, source_target_pairs={{0,16},{8,24},{16,0},{24,8},{1,17},{9,25},{17,1},{25,9},{2,18},{10... | collective-permute-start | bytes 1572872 | tf_op jit(solution)/shard_map/ppermute | solution.py:485
  28.1 1.1 %collective-permute-start.9 = (f32[4,16,8,256]{3,2,1,0:T(8,128)S(1)}, f32[4,16,8,256]{3,2,1,0:T(8,128)S(1)}, u32[]{:S(2)}, u32[]{:S(2)}) collective-permute-start(f32[4,16,8,256]{3,2,1,0:T(8,128)S(1)} %pad_maximum_fusion.refs_0_), channel_id=1, source_target_pairs={{0,1},{1,0},{2,3},{3,2},{4,5},{5,4},{6,7},{7,6},{8,9},{9,8},{10,11... | collective-permute-start | bytes 1572872 | tf_op jit(solution)/shard_map/ppermute | solution.py:483
  29.1 0.0 collective-permute-start.12
  29.1 0.5 collective-permute-start.13
  29.7 0.8 %collective-permute-done.12.refs_2_.refs_10_ = f32[4,4,8,256]{3,2,1,0:T(8,128)S(1)} collective-permute-done((f32[4,4,8,256]{3,2,1,0:T(8,128)S(1)}, f32[4,4,8,256]{3,2,1,0:T(8,128)S(1)}, u32[]{:S(2)}, u32[]{:S(2)}) %collective-permute-start.12) | collective-permute-done | bytes 131104 | tf_op jit(solution)/shard_map/ppermute | solution.py:485
  30.5 0.1 collective-permute-start.14
  30.6 0.0 collective-permute-done.13.refs_3_.refs_11_
  30.7 0.3 collective-permute-start.15
  31.0 0.8 %collective-permute-done.14.refs_6_.refs_14_ = f32[4,4,8,256]{3,2,1,0:T(8,128)S(1)} collective-permute-done((f32[4,4,8,256]{3,2,1,0:T(8,128)S(1)}, f32[4,4,8,256]{3,2,1,0:T(8,128)S(1)}, u32[]{:S(2)}, u32[]{:S(2)}) %collective-permute-start.14) | collective-permute-done | bytes 131104 | tf_op jit(solution)/shard_map/ppermute | solution.py:485
  31.8 0.1 collective-permute-start.16
  32.0 0.0 collective-permute-done.15.refs_7_.refs_15_
  32.0 9.5 %tiles.1 = (s32[12,2,256]{2,1,0:T(2,128)}, bf16[124,2,256,256]{3,2,1,0:T(8,128)(2,1)S(1)}) custom-call(f32[4,4,8,256]{3,2,1,0:T(8,128)S(1)} %pad_maximum_fusion.1.refs_0_.refs_8_, f32[4,4,8,256]{3,2,1,0:T(8,128)S(1)} %collective-permute-done.6.refs_1_.refs_9_, f32[4,4,8,256]{3,2,1,0:T(8,128)S(1)} %collective-permute-done.12.refs_2_.refs_10_, ...), custom_call_target="tpu_custom_call" | custom-call | flops 1000000000 | bytes 31457280 | tf_op jit(solution)/shard_map/tiles/pallas_call | solution.py:520
  41.5 0.0 collective-permute-done.11.refs_5_
  41.5 7.6 %collective-permute-done.10.refs_4_ = f32[4,16,8,256]{3,2,1,0:T(8,128)S(1)} collective-permute-done((f32[4,16,8,256]{3,2,1,0:T(8,128)S(1)}, f32[4,16,8,256]{3,2,1,0:T(8,128)S(1)}, u32[]{:S(2)}, u32[]{:S(2)}) %collective-permute-start.10) | collective-permute-done | bytes 524320 | tf_op jit(solution)/shard_map/ppermute | solution.py:485
  49.1 0.0 collective-permute-done.9.refs_1_
  49.1 2.2 %collective-permute-start.17 = (f32[4,16,8,256]{3,2,1,0:T(8,128)S(1)}, f32[4,16,8,256]{3,2,1,0:T(8,128)S(1)}, u32[]{:S(2)}, u32[]{:S(2)}) collective-permute-start(f32[4,16,8,256]{3,2,1,0:T(8,128)S(1)} %collective-permute-done.9.refs_1_), channel_id=1, source_target_pairs={{0,8},{8,0},{16,24},{24,16},{1,9},{9,1},{17,25},{25,17},{2,10},{10... | collective-permute-start | bytes 1572872 | tf_op jit(solution)/shard_map/ppermute | solution.py:485
  51.3 0.1 collective-permute-start.18
  51.4 0.4 collective-permute-start.19
  51.8 0.0 collective-permute-done.16.refs_2_
  51.8 1.0 %collective-permute-done.17.refs_3_ = f32[4,16,8,256]{3,2,1,0:T(8,128)S(1)} collective-permute-done((f32[4,16,8,256]{3,2,1,0:T(8,128)S(1)}, f32[4,16,8,256]{3,2,1,0:T(8,128)S(1)}, u32[]{:S(2)}, u32[]{:S(2)}) %collective-permute-start.17) | collective-permute-done | bytes 524320 | tf_op jit(solution)/shard_map/ppermute | solution.py:485
  52.9 0.7 collective-permute-done.18.refs_6_
  53.6 0.7 collective-permute-done.19.refs_7_
  54.4 5.0 %apply.1 = (f32[8,16,256]{2,1,0:T(8,128)S(1)}, f32[8,16,256]{2,1,0:T(8,128)S(1)}, f32[32,8,128]{2,1,0:T(8,128)S(1)}) custom-call(s32[12,2,256]{2,1,0:T(2,128)} %get-tuple-element.28.list_ref, bf16[124,2,256,256]{3,2,1,0:T(8,128)(2,1)S(1)} %get-tuple-element.29.tile_ref, f32[4,16,8,256]{3,2,1,0:T(8,128)S(1)} %pad_maximum_fusion.refs_0_, ...), custom_call_target="tpu_custom_call" | custom-call | tf_op jit(solution)/shard_map/apply/pallas_call | solution.py:547
  59.4 0.0 copy-start
  59.4 21.7 %all_to_all.5.moment_ref = f32[32,8,128]{2,1,0:T(8,128)} all-to-all(f32[32,8,128]{2,1,0:T(8,128)S(1)} %get-tuple-element.33), channel_id=1, replica_groups=mesh['row'=4,'col'=8] {'row','col'}, dimensions={0} | all-to-all | bytes 262144 | tf_op jit(solution)/shard_map/all_to_all | solution.py:571
  81.1 2.1 %finish.1 = (f32[16,2048]{1,0:T(8,128)}, f32[16,2048]{1,0:T(8,128)}) custom-call(f32[32,8,128]{2,1,0:T(8,128)} %all_to_all.5.moment_ref, f32[16,2048]{1,0:T(8,128)} %values_ref.3, f32[8,16,256]{2,1,0:T(8,128)} %copy-done, f32[8,16,256]{2,1,0:T(8,128)} %copy-done.1), custom_call_target="tpu_custom_call" | custom-call | tf_op jit(solution)/shard_map/finish/pallas_call | solution.py:572
  (3 shorter events, 0.0 us)
Async XLA Ops:
  2.3 9.4 %collective-permute-start.5 = (f32[4,8,256]{2,1,0:T(8,128)}, f32[4,8,256]{2,1,0:T(8,128)S(1)}, u32[]{:S(2)}, u32[]{:S(2)}) collective-permute-start(f32[4,8,256]{2,1,0:T(8,128)} %get-tuple-element.20), channel_id=1, source_target_pairs={{0,6},{1,7},{2,4},{3,5},{4,2},{5,3},{6,0},{7,1},{8,14},{9,15},{10,... | collective-permute-start | bytes 98312 | tf_op jit(solution)/shard_map/ppermute | solution.py:483
  7.3 9.6 %collective-permute-start.4 = (f32[4,8,256]{2,1,0:T(8,128)}, f32[4,8,256]{2,1,0:T(8,128)S(1)}, u32[]{:S(2)}, u32[]{:S(2)}) collective-permute-start(f32[4,8,256]{2,1,0:T(8,128)} %get-tuple-element.20), channel_id=1, source_target_pairs={{0,4},{1,5},{2,6},{3,7},{4,0},{5,1},{6,2},{7,3},{8,12},{9,13},{10,... | collective-permute-start | bytes 98312 | tf_op jit(solution)/shard_map/ppermute | solution.py:483
  7.3 9.6 %collective-permute-start.3 = (f32[4,8,256]{2,1,0:T(8,128)}, f32[4,8,256]{2,1,0:T(8,128)S(1)}, u32[]{:S(2)}, u32[]{:S(2)}) collective-permute-start(f32[4,8,256]{2,1,0:T(8,128)} %get-tuple-element.20), channel_id=1, source_target_pairs={{0,2},{1,3},{2,0},{3,1},{4,6},{5,7},{6,4},{7,5},{8,10},{9,11},{10,... | collective-permute-start | bytes 98312 | tf_op jit(solution)/shard_map/ppermute | solution.py:483
  7.9 12.8 %collective-permute-start.2 = (f32[16,8,256]{2,1,0:T(8,128)}, f32[16,8,256]{2,1,0:T(8,128)S(1)}, u32[]{:S(2)}, u32[]{:S(2)}) collective-permute-start(f32[16,8,256]{2,1,0:T(8,128)} %get-tuple-element.19), channel_id=1, source_target_pairs={{0,6},{1,7},{2,4},{3,5},{4,2},{5,3},{6,0},{7,1},{8,14},{9,15},{10,... | collective-permute-start | bytes 393224 | tf_op jit(solution)/shard_map/ppermute | solution.py:483
  11.7 11.2 %collective-permute-start.1 = (f32[16,8,256]{2,1,0:T(8,128)}, f32[16,8,256]{2,1,0:T(8,128)S(1)}, u32[]{:S(2)}, u32[]{:S(2)}) collective-permute-start(f32[16,8,256]{2,1,0:T(8,128)} %get-tuple-element.19), channel_id=1, source_target_pairs={{0,4},{1,5},{2,6},{3,7},{4,0},{5,1},{6,2},{7,3},{8,12},{9,13},{10,... | collective-permute-start | bytes 393224 | tf_op jit(solution)/shard_map/ppermute | solution.py:483
  11.7 11.2 %collective-permute-start = (f32[16,8,256]{2,1,0:T(8,128)}, f32[16,8,256]{2,1,0:T(8,128)S(1)}, u32[]{:S(2)}, u32[]{:S(2)}) collective-permute-start(f32[16,8,256]{2,1,0:T(8,128)} %get-tuple-element.19), channel_id=1, source_target_pairs={{0,2},{1,3},{2,0},{3,1},{4,6},{5,7},{6,4},{7,5},{8,10},{9,11},{10,... | collective-permute-start | bytes 393224 | tf_op jit(solution)/shard_map/ppermute | solution.py:483
  17.7 6.2 %collective-permute-start.8 = (f32[4,4,8,256]{3,2,1,0:T(8,128)S(1)}, f32[4,4,8,256]{3,2,1,0:T(8,128)S(1)}, u32[]{:S(2)}, u32[]{:S(2)}) collective-permute-start(f32[4,4,8,256]{3,2,1,0:T(8,128)S(1)} %pad_maximum_fusion.1.refs_0_.refs_8_), channel_id=1, source_target_pairs={{0,17},{1,16},{2,19},{3,18},{4,21},{5,20},{6,23},{7,22},{8,25},{9,... | collective-permute-start | bytes 393224 | tf_op jit(solution)/shard_map/ppermute | solution.py:489
  20.2 5.0 %collective-permute-start.7 = (f32[4,4,8,256]{3,2,1,0:T(8,128)S(1)}, f32[4,4,8,256]{3,2,1,0:T(8,128)S(1)}, u32[]{:S(2)}, u32[]{:S(2)}) collective-permute-start(f32[4,4,8,256]{3,2,1,0:T(8,128)S(1)} %pad_maximum_fusion.1.refs_0_.refs_8_), channel_id=1, source_target_pairs={{0,16},{8,24},{16,0},{24,8},{1,17},{9,25},{17,1},{25,9},{2,18},{10... | collective-permute-start | bytes 393224 | tf_op jit(solution)/shard_map/ppermute | solution.py:485
  20.7 5.0 %collective-permute-start.6 = (f32[4,4,8,256]{3,2,1,0:T(8,128)S(1)}, f32[4,4,8,256]{3,2,1,0:T(8,128)S(1)}, u32[]{:S(2)}, u32[]{:S(2)}) collective-permute-start(f32[4,4,8,256]{3,2,1,0:T(8,128)S(1)} %pad_maximum_fusion.1.refs_0_.refs_8_), channel_id=1, source_target_pairs={{0,1},{1,0},{2,3},{3,2},{4,5},{5,4},{6,7},{7,6},{8,9},{9,8},{10,11... | collective-permute-start | bytes 393224 | tf_op jit(solution)/shard_map/ppermute | solution.py:483
  25.7 15.9 %collective-permute-start.11 = (f32[4,16,8,256]{3,2,1,0:T(8,128)S(1)}, f32[4,16,8,256]{3,2,1,0:T(8,128)S(1)}, u32[]{:S(2)}, u32[]{:S(2)}) collective-permute-start(f32[4,16,8,256]{3,2,1,0:T(8,128)S(1)} %pad_maximum_fusion.refs_0_), channel_id=1, source_target_pairs={{0,17},{1,16},{2,19},{3,18},{4,21},{5,20},{6,23},{7,22},{8,25},{9,... | collective-permute-start | bytes 1572872 | tf_op jit(solution)/shard_map/ppermute | solution.py:489
  27.1 21.9 %collective-permute-start.10 = (f32[4,16,8,256]{3,2,1,0:T(8,128)S(1)}, f32[4,16,8,256]{3,2,1,0:T(8,128)S(1)}, u32[]{:S(2)}, u32[]{:S(2)}) collective-permute-start(f32[4,16,8,256]{3,2,1,0:T(8,128)S(1)} %pad_maximum_fusion.refs_0_), channel_id=1, source_target_pairs={{0,16},{8,24},{16,0},{24,8},{1,17},{9,25},{17,1},{25,9},{2,18},{10... | collective-permute-start | bytes 1572872 | tf_op jit(solution)/shard_map/ppermute | solution.py:485
  28.1 21.0 %collective-permute-start.9 = (f32[4,16,8,256]{3,2,1,0:T(8,128)S(1)}, f32[4,16,8,256]{3,2,1,0:T(8,128)S(1)}, u32[]{:S(2)}, u32[]{:S(2)}) collective-permute-start(f32[4,16,8,256]{3,2,1,0:T(8,128)S(1)} %pad_maximum_fusion.refs_0_), channel_id=1, source_target_pairs={{0,1},{1,0},{2,3},{3,2},{4,5},{5,4},{6,7},{7,6},{8,9},{9,8},{10,11... | collective-permute-start | bytes 1572872 | tf_op jit(solution)/shard_map/ppermute | solution.py:483
  29.1 1.3 %collective-permute-start.12 = (f32[4,4,8,256]{3,2,1,0:T(8,128)S(1)}, f32[4,4,8,256]{3,2,1,0:T(8,128)S(1)}, u32[]{:S(2)}, u32[]{:S(2)}) collective-permute-start(f32[4,4,8,256]{3,2,1,0:T(8,128)S(1)} %pad_maximum_fusion.1.refs_0_.refs_8_), channel_id=1, source_target_pairs={{0,8},{8,0},{16,24},{24,16},{1,9},{9,1},{17,25},{25,17},{2,10},{10... | collective-permute-start | bytes 393224 | tf_op jit(solution)/shard_map/ppermute | solution.py:485
  29.1 1.5 %collective-permute-start.13 = (f32[4,4,8,256]{3,2,1,0:T(8,128)S(1)}, f32[4,4,8,256]{3,2,1,0:T(8,128)S(1)}, u32[]{:S(2)}, u32[]{:S(2)}) collective-permute-start(f32[4,4,8,256]{3,2,1,0:T(8,128)S(1)} %collective-permute-done.6.refs_1_.refs_9_), channel_id=1, source_target_pairs={{0,8},{8,0},{16,24},{24,16},{1,9},{9,1},{17,25},{25,17},{2,10},{10... | collective-permute-start | bytes 393224 | tf_op jit(solution)/shard_map/ppermute | solution.py:485
  30.5 1.3 %collective-permute-start.14 = (f32[4,4,8,256]{3,2,1,0:T(8,128)S(1)}, f32[4,4,8,256]{3,2,1,0:T(8,128)S(1)}, u32[]{:S(2)}, u32[]{:S(2)}) collective-permute-start(f32[4,4,8,256]{3,2,1,0:T(8,128)S(1)} %collective-permute-done.7.refs_4_.refs_12_), channel_id=1, source_target_pairs={{0,8},{8,0},{16,24},{24,16},{1,9},{9,1},{17,25},{25,17},{2,10},{10... | collective-permute-start | bytes 393224 | tf_op jit(solution)/shard_map/ppermute | solution.py:485
  30.7 1.3 %collective-permute-start.15 = (f32[4,4,8,256]{3,2,1,0:T(8,128)S(1)}, f32[4,4,8,256]{3,2,1,0:T(8,128)S(1)}, u32[]{:S(2)}, u32[]{:S(2)}) collective-permute-start(f32[4,4,8,256]{3,2,1,0:T(8,128)S(1)} %collective-permute-done.8.refs_5_.refs_13_), channel_id=1, source_target_pairs={{0,8},{8,0},{16,24},{24,16},{1,9},{9,1},{17,25},{25,17},{2,10},{10... | collective-permute-start | bytes 393224 | tf_op jit(solution)/shard_map/ppermute | solution.py:485
  31.8 20.0 %collective-permute-start.16 = (f32[4,16,8,256]{3,2,1,0:T(8,128)S(1)}, f32[4,16,8,256]{3,2,1,0:T(8,128)S(1)}, u32[]{:S(2)}, u32[]{:S(2)}) collective-permute-start(f32[4,16,8,256]{3,2,1,0:T(8,128)S(1)} %pad_maximum_fusion.refs_0_), channel_id=1, source_target_pairs={{0,8},{8,0},{16,24},{24,16},{1,9},{9,1},{17,25},{25,17},{2,10},{10... | collective-permute-start | bytes 1572872 | tf_op jit(solution)/shard_map/ppermute | solution.py:485
  49.1 3.8 %collective-permute-start.17 = (f32[4,16,8,256]{3,2,1,0:T(8,128)S(1)}, f32[4,16,8,256]{3,2,1,0:T(8,128)S(1)}, u32[]{:S(2)}, u32[]{:S(2)}) collective-permute-start(f32[4,16,8,256]{3,2,1,0:T(8,128)S(1)} %collective-permute-done.9.refs_1_), channel_id=1, source_target_pairs={{0,8},{8,0},{16,24},{24,16},{1,9},{9,1},{17,25},{25,17},{2,10},{10... | collective-permute-start | bytes 1572872 | tf_op jit(solution)/shard_map/ppermute | solution.py:485
  51.3 2.3 %collective-permute-start.18 = (f32[4,16,8,256]{3,2,1,0:T(8,128)S(1)}, f32[4,16,8,256]{3,2,1,0:T(8,128)S(1)}, u32[]{:S(2)}, u32[]{:S(2)}) collective-permute-start(f32[4,16,8,256]{3,2,1,0:T(8,128)S(1)} %collective-permute-done.10.refs_4_), channel_id=1, source_target_pairs={{0,8},{8,0},{16,24},{24,16},{1,9},{9,1},{17,25},{25,17},{2,10},{10... | collective-permute-start | bytes 1572872 | tf_op jit(solution)/shard_map/ppermute | solution.py:485
  51.4 3.0 %collective-permute-start.19 = (f32[4,16,8,256]{3,2,1,0:T(8,128)S(1)}, f32[4,16,8,256]{3,2,1,0:T(8,128)S(1)}, u32[]{:S(2)}, u32[]{:S(2)}) collective-permute-start(f32[4,16,8,256]{3,2,1,0:T(8,128)S(1)} %collective-permute-done.11.refs_5_), channel_id=1, source_target_pairs={{0,8},{8,0},{16,24},{24,16},{1,9},{9,1},{17,25},{25,17},{2,10},{10... | collective-permute-start | bytes 1572872 | tf_op jit(solution)/shard_map/ppermute | solution.py:485
  59.4 21.7 %copy-start = (f32[8,16,256]{2,1,0:T(8,128)}, f32[8,16,256]{2,1,0:T(8,128)S(1)}, u32[]{:S(2)}) copy-start(f32[8,16,256]{2,1,0:T(8,128)S(1)} %get-tuple-element.34.w_ref) | copy-start | bytes 393220
  59.4 21.7 %copy-start.1 = (f32[8,16,256]{2,1,0:T(8,128)}, f32[8,16,256]{2,1,0:T(8,128)S(1)}, u32[]{:S(2)}) copy-start(f32[8,16,256]{2,1,0:T(8,128)S(1)} %get-tuple-element.35.x_ref) | copy-start | bytes 393220
